TPU v7x, 32 devices: a whole 2x2x4 slice. The times are simulated.
32 devices in a mesh: groups: 2 (over x), expert: 4 (over y, core), sub: 4 (over z).
Axes of the slice: x: 2, y: 2, z: 4, core: 2. Of those that a mesh axis runs over, the one named last changes fastest.
Arguments:
- residual: bfloat16 [256, 2048], P(('groups', 'expert', 'sub')), parts along dimension 0, may hold values from -6 to 6
- query: bfloat16 [256, 2048], P(('groups', 'expert', 'sub')), parts along dimension 0, may hold values from -5 to 5
- new_key: bfloat16 [256, 512], P(('groups', 'expert', 'sub')), parts along dimension 0, may hold values from -5 to 5
- new_value: bfloat16 [256, 512], P(('groups', 'expert', 'sub')), parts along dimension 0, may hold values from -6 to 6
- key_cache: bfloat16 [256, 128, 512], P(('groups', 'expert', 'sub')), parts along dimension 0, may hold values from -5 to 5
- value_cache: bfloat16 [256, 128, 512], P(('groups', 'expert', 'sub')), parts along dimension 0, may hold values from -6 to 6
- cache_len: int32 [256], P(('groups', 'expert', 'sub')), parts along dimension 0, may hold values from 1 to 128, as said below
- out_weight: bfloat16 [2048, 2048], P('sub'), may hold values from -0.125 to 0.125
- norm_gain: bfloat16 [2048], replicated, may hold values from 0.099609375 to 1.8984375
- expert_ids: int32 [256, 8], P(('groups', 'expert', 'sub')), parts along dimension 0, may hold values from 0 to 15, as said below
- gate_scores: float32 [256, 8], P(('groups', 'expert', 'sub')), parts along dimension 0, may hold values from 0.05 to 1
- expert_gate: bfloat16 [16, 2048, 768], P(('expert', 'sub')), may hold values from -0.125 to 0.125
- expert_up: bfloat16 [16, 2048, 768], P(('expert', 'sub')), may hold values from -0.125 to 0.125
- expert_down: bfloat16 [16, 768, 2048], P(('expert', 'sub')), may hold values from -0.21875 to 0.21875
Outputs:
- layer_out: bfloat16 [256, 2048], P(('groups', 'expert', 'sub')), parts along dimension 0
There are 2 independent parts, one for each index of `groups`. A program takes and returns all parts, laid end to end along the dimension named above; an argument that names none is the same for every part. Nothing has to cross between parts.
Inputs may be any that keep to these rules, and one draw needn't show every extreme that they name: Stream t attends to cache positions below cache_len[t] and to its new frame; in every draw some stream holds all 128 frames. `expert_ids`: each row names 8 different experts. Among the 8 rows of one device no expert is named more than 8 times, and one expert is named exactly 8 times by the rows of every device.
All inputs are finite; a program needn't handle non-finite values.
Results may differ from a plain program's by a relative error of at most 0.0075.
Values may be sent and summed in bfloat16 or wider, within the bound.
No kernel may reach another device: no remote copies, remote signals or barrier semaphores. Data moves between devices by JAX's collectives and lax.ppermute only.
A program may use at most 64 MiB of HBM per device.

v0:
```python
import math

import jax
import jax.numpy as jnp
from jax import lax
from jax.sharding import PartitionSpec as P

KV_HEADS = 4
HEAD_DIM = 128


def attend(query, new_key, new_value, key_cache, value_cache, cache_len):
    streams = query.shape[0]
    frames = key_cache.shape[1]
    group_size = query.shape[1] // (KV_HEADS * HEAD_DIM)
    scale_factor = 1.0 / math.sqrt(HEAD_DIM)
    queries = query.reshape(streams, KV_HEADS, group_size, HEAD_DIM)
    keys_old = key_cache.reshape(streams, frames, KV_HEADS, HEAD_DIM)
    values_old = value_cache.reshape(streams, frames, KV_HEADS, HEAD_DIM)
    keys_new = new_key.reshape(streams, KV_HEADS, HEAD_DIM)
    values_new = new_value.reshape(streams, KV_HEADS, HEAD_DIM).astype(jnp.float32)
    scores_old = (
        jnp.einsum("skgd,slkd->skgl", queries, keys_old, preferred_element_type=jnp.float32)
        * scale_factor
    )
    scores_new = (
        jnp.einsum("skgd,skd->skg", queries, keys_new, preferred_element_type=jnp.float32)
        * scale_factor
    )
    is_valid = lax.broadcasted_iota(jnp.int32, (streams, frames), 1) < cache_len[:, None]
    scores_old = jnp.where(is_valid[:, None, None, :], scores_old, -1e30)
    highest = jnp.maximum(jnp.max(scores_old, axis=3), scores_new)
    exp_old = jnp.exp(scores_old - highest[..., None])
    exp_new = jnp.exp(scores_new - highest)
    total_mass = jnp.sum(exp_old, axis=3) + exp_new
    probs_old = (exp_old / total_mass[..., None]).astype(jnp.bfloat16)
    probs_new = (exp_new / total_mass).astype(jnp.bfloat16)
    context = jnp.einsum(
        "skgl,slkd->skgd", probs_old, values_old, preferred_element_type=jnp.float32
    )
    context = context + probs_new.astype(jnp.float32)[..., None] * values_new[:, :, None, :]
    return context.reshape(streams, query.shape[1]).astype(jnp.bfloat16)


def run_expert(inputs, gate_matrix, up_matrix, down_matrix):
    gate_part = jnp.dot(inputs, gate_matrix, preferred_element_type=jnp.float32)
    up_part = jnp.dot(inputs, up_matrix, preferred_element_type=jnp.float32)
    activated = (jax.nn.silu(gate_part) * up_part).astype(jnp.bfloat16)
    return jnp.dot(activated, down_matrix, preferred_element_type=jnp.float32).astype(jnp.bfloat16)


def layer_rows(members, capacity, out_weight, norm_gain, expert_gate, expert_up, expert_down):
    (
        residual,
        query,
        new_key,
        new_value,
        key_cache,
        value_cache,
        cache_len,
        expert_ids,
        gate_scores,
    ) = members
    streams = residual.shape[0]
    feature_width = residual.shape[1]
    top_count = expert_ids.shape[1]
    context = attend(query, new_key, new_value, key_cache, value_cache, cache_len)
    spread = lax.all_to_all(context, "sub", split_axis=1, concat_axis=0, tiled=True)
    hidden = residual.astype(jnp.float32) + lax.psum_scatter(
        jnp.dot(spread, out_weight, preferred_element_type=jnp.float32),
        "sub",
        scatter_dimension=0,
        tiled=True,
    )
    normed = hidden * lax.rsqrt(jnp.mean(hidden * hidden, axis=1, keepdims=True) + 1e-06)
    normed = (normed * norm_gain.astype(jnp.float32)).astype(jnp.bfloat16)
    owner_major = lax.axis_size("expert")
    owner_minor = lax.axis_size("sub")
    expert_total = owner_major * owner_minor
    slot_total = expert_total * capacity
    flat_ids = expert_ids.reshape(-1)
    one_hot = (flat_ids[:, None] == lax.broadcasted_iota(jnp.int32, (1, expert_total), 1)).astype(
        jnp.int32
    )
    before = jnp.cumsum(one_hot, axis=0) - one_hot
    position = jnp.sum(before * one_hot, axis=1)
    target = flat_ids * capacity + position
    slot_labels = lax.broadcasted_iota(jnp.int32, (slot_total, 1, 1), 0)
    placed = jnp.any(target.reshape(1, streams, top_count) == slot_labels, axis=2).astype(
        jnp.bfloat16
    )
    outgoing = jnp.dot(placed, normed, preferred_element_type=jnp.float32).astype(jnp.bfloat16)
    outgoing = outgoing.reshape(expert_total, capacity, feature_width)
    arrived = lax.all_to_all(outgoing, ("expert", "sub"), split_axis=0, concat_axis=0, tiled=True)
    result = run_expert(
        arrived.reshape(-1, feature_width), expert_gate[0], expert_up[0], expert_down[0]
    )
    returned = lax.all_to_all(
        result.reshape(arrived.shape), ("expert", "sub"), split_axis=0, concat_axis=0, tiled=True
    )
    fetched = returned.reshape(slot_total, feature_width)[target]
    fetched = fetched.astype(jnp.float32).reshape(streams, top_count, feature_width)
    weights = gate_scores / jnp.sum(gate_scores, axis=1, keepdims=True)
    mixture = jnp.sum(weights[:, :, None] * fetched, axis=1)
    return (hidden + mixture).astype(jnp.bfloat16)


def body(
    residual,
    query,
    new_key,
    new_value,
    key_cache,
    value_cache,
    cache_len,
    out_weight,
    norm_gain,
    expert_ids,
    gate_scores,
    expert_gate,
    expert_up,
    expert_down,
):
    streams = residual.shape[0]
    top_count = expert_ids.shape[1]
    expert_total = lax.axis_size("expert") * lax.axis_size("sub")
    capacity = max(2, 2 * (streams * top_count // expert_total))
    pieces = (
        residual,
        query,
        new_key,
        new_value,
        key_cache,
        value_cache,
        cache_len,
        expert_ids,
        gate_scores,
    )
    return layer_rows(pieces, capacity, out_weight, norm_gain, expert_gate, expert_up, expert_down)


def solution(mesh):
    placed = (
        P(("groups", "expert", "sub"), None),
        P(("groups", "expert", "sub"), None),
        P(("groups", "expert", "sub"), None),
        P(("groups", "expert", "sub"), None),
        P(("groups", "expert", "sub"), None, None),
        P(("groups", "expert", "sub"), None, None),
        P(("groups", "expert", "sub")),
        P("sub", None),
        P(),
        P(("groups", "expert", "sub"), None),
        P(("groups", "expert", "sub"), None),
        P(("expert", "sub"), None, None),
        P(("expert", "sub"), None, None),
        P(("expert", "sub"), None, None),
    )
    return jax.shard_map(
        body,
        mesh=mesh,
        in_specs=placed,
        out_specs=P(("groups", "expert", "sub"), None),
        check_vma=False,
    )
```

profile of v0, /device:TPU:0, one launch (start us, length us, event | category | flops | bytes accessed | tf_op | source)
XLA Modules:
  0.0 104.6 jit_solution(9305244903624549166)
XLA Ops:
  6.5 0.9 iota_compare_fusion.2
  7.4 1.0 fusion.46
  8.5 2.0 %fusion.55 = (f32[8,4,4]{2,1,0:T(4,128)S(1)}, f32[8,4,4,128]{3,2,1,0:T(4,128)S(1)}) fusion(bf16[8,4,4,128]{3,0,2,1:T(8,128)(2,1)} %bitcast.74, pred[8,128]{1,0:T(8,128)(4,1)S(1)} %iota_compare_fusion.2, bf16[8,128,512]{2,1,0:T(8,128)(2,1)} %param.18), kind=kOutput, calls=%fused_computation.69 | convolution fusion | flops 4243328 | bytes 1148416 | tf_op jit(solution)/shard_map/skgd,slkd->skgl/dot_general | solution.py:23
  10.5 0.2 fusion.37
  10.7 0.7 bitcast_convert_fusion
  11.4 1.7 %fusion.20 = bf16[8,4,4,128]{3,2,1,0:T(4,128)(2,1)S(1)} fusion(f32[8,4,4,128]{3,2,1,0:T(4,128)S(1)} %get-tuple-element.10, f32[8,4,128]{2,1,0:T(4,128)S(1)} %copy.27, f32[8,4,4]{2,1,0:T(4,128)S(1)} %get-tuple-element.6, f32[8,4,4]{2,1,0:T(4,128)S(1)} %get-tuple-element.5, f32[8,4,4]{2,1,0:T(4,128)S(1)} %multiply_maximum_fusion, bf16[8,128,512]{2,1,0:T(8,128)(2,1)} %param.19), kind=kOutput, calls=%fused_computation.16 | convolution fusion | flops 4292608 | bytes 1164800 | tf_op jit(solution)/shard_map/skgl,slkd->skgd/dot_general | solution.py:38
  13.1 0.6 copy.28
  13.7 6.3 %all-to-all-start = ((bf16[8,4,512]{2,0,1:T(8,128)(2,1)}), bf16[8,4,512]{2,0,1:T(8,128)(2,1)S(1)}, u32[]{:S(2)}, u32[]{:S(2)}) async-start(bf16[8,4,512]{2,0,1:T(8,128)(2,1)} %copy.28), calls=%async_computation | async-start | bytes 65536 | tf_op jit(solution)/shard_map/all_to_all | solution.py:68
  20.1 0.1 eq.28
  20.1 5.6 %all-to-all-done = bf16[8,4,512]{2,0,1:T(8,128)(2,1)S(1)} async-done(((bf16[8,4,512]{2,0,1:T(8,128)(2,1)}), bf16[8,4,512]{2,0,1:T(8,128)(2,1)S(1)}, u32[]{:S(2)}, u32[]{:S(2)}) %all-to-all-start) | async-done | bytes 32800 | tf_op jit(solution)/shard_map/all_to_all | solution.py:68
  25.7 2.8 %fusion.38 = f32[32,2048]{1,0:T(8,128)} fusion(bf16[512,2048]{1,0:T(8,128)(2,1)} %param.21, bf16[8,4,512]{2,0,1:T(8,128)(2,1)S(1)} %all-to-all-done), kind=kOutput, calls=%fused_computation.38 | convolution fusion | flops 67108864 | bytes 2392064 | tf_op jit(solution)/shard_map/dot_general | solution.py:70
  28.5 0.0 reduce-scatter.2.cloned.1.call-update
  28.5 0.1 fusion.42
  28.6 0.1 reduce_window_sum.11
  28.7 0.2 select_reduce_fusion
  28.8 0.1 reduce_sum.52
  29.0 0.1 fusion.45
  29.0 17.7 %reduce-scatter.2.cloned.1.call-done = f32[8,2048]{1,0:T(8,128)} async-done(((f32[32,2048]{1,0:T(8,128)}), f32[8,2048]{1,0:T(8,128)}) %reduce-scatter.2.cloned.1.call-update) | async-done | bytes 65552 | tf_op jit(solution)/shard_map/reduce_scatter | solution.py:69
  46.7 1.0 multiply_reduce_fusion
  47.7 1.2 %fusion.9 = bf16[16,8,2048]{2,1,0:T(8,128)(2,1)S(1)} fusion(pred[128,8]{0,1:T(8,128)(4,1)S(1)} %fusion.45, f32[2048]{0:T(1024)S(1)} %convert_element_type.67, f32[8]{0:T(128)S(1)} %add_rsqrt_fusion, f32[8,2048]{1,0:T(8,128)} %reduce-scatter.2.cloned.1.call-done, bf16[8,2048]{1,0:T(8,128)(2,1)S(1)} %copy-done.3), kind=kOutput, calls=%fused_computation.9 | convolution fusion | flops 4538368 | bytes 631840 | tf_op jit(solution)/shard_map/dot_general | solution.py:92
  48.9 18.4 %all_to_all.26 = bf16[16,8,2048]{2,1,0:T(8,128)(2,1)S(1)} all-to-all(bf16[16,8,2048]{2,1,0:T(8,128)(2,1)S(1)} %fusion.9), channel_id=1, replica_groups=mesh['groups'=2,'expert'=4,'sub'=4] {'expert','sub'}, dimensions={0} | all-to-all | bytes 1048576 | tf_op jit(solution)/shard_map/all_to_all | solution.py:94
  67.3 0.8 copy-done.1
  68.1 2.5 %fusion.4 = f32[128,768]{1,0:T(8,128)S(1)} fusion(bf16[1,2048,768]{2,1,0:T(8,128)(2,1)} %param.25, bf16[16,8,2048]{2,1,0:T(8,128)(2,1)S(1)} %all_to_all.26), kind=kOutput, calls=%fused_computation.5 | convolution fusion | flops 402653184 | bytes 4063232 | tf_op jit(solution)/shard_map/dot_general | solution.py:46
  70.6 4.1 %fusion.10 = bf16[16,8,2048]{2,1,0:T(8,128)(2,1)} fusion(bf16[1,768,2048]{2,1,0:T(8,128)(2,1)S(1)} %copy-done, bf16[1,2048,768]{2,1,0:T(8,128)(2,1)} %param.26, bf16[16,8,2048]{2,1,0:T(8,128)(2,1)} %copy-done.1, f32[128,768]{1,0:T(8,128)S(1)} %fusion.4), kind=kOutput, calls=%fused_computation.10 | convolution fusion | flops 806158336 | bytes 7733248 | tf_op jit(solution)/shard_map/dot_general | solution.py:49
  74.7 4.4 %all-to-all-start.2 = ((bf16[16,8,2048]{2,1,0:T(8,128)(2,1)}), bf16[16,8,2048]{2,1,0:T(8,128)(2,1)}, u32[]{:S(2)}, u32[]{:S(2)}) async-start(bf16[16,8,2048]{2,1,0:T(8,128)(2,1)} %fusion.10), calls=%async_computation.3 | async-start | bytes 1048576 | tf_op jit(solution)/shard_map/all_to_all | solution.py:98
  79.1 0.1 mul.98
  79.2 0.1 reduce_sum.50
  79.3 0.1 broadcast_divide_fusion
  79.4 15.4 %all-to-all-done.2 = bf16[16,8,2048]{2,1,0:T(8,128)(2,1)} async-done(((bf16[16,8,2048]{2,1,0:T(8,128)(2,1)}), bf16[16,8,2048]{2,1,0:T(8,128)(2,1)}, u32[]{:S(2)}, u32[]{:S(2)}) %all-to-all-start.2) | async-done | bytes 524320 | tf_op jit(solution)/shard_map/all_to_all | solution.py:98
  94.8 2.1 %gather_fusion = bf16[64,2048]{1,0:T(8,128)(2,1)S(1)} fusion(bf16[128,2048]{1,0:T(8,128)(2,1)} %bitcast.14, s32[1024]{0:T(1024)S(1)} %pad_clamp_fusion), kind=kCustom, calls=%fused_computation | custom fusion | bytes 524544 | tf_op jit(solution)/shard_map/gather | solution.py:101
  96.9 0.3 fusion.27
  97.2 0.6 add_convert_fusion
  (25 shorter events, 0.1 us)
Async XLA Ops:
  6.5 64.1 %copy-start = (bf16[1,768,2048]{2,1,0:T(8,128)(2,1)S(1)}, bf16[1,768,2048]{2,1,0:T(8,128)(2,1)}, u32[]{:S(2)}) copy-start(bf16[1,768,2048]{2,1,0:T(8,128)(2,1)} %param.27) | copy-start | bytes 9437188
  6.5 13.5 %copy-start.6 = (s32[8,8]{1,0:T(8,128)S(1)}, s32[8,8]{1,0:T(8,128)}, u32[]{:S(2)}) copy-start(s32[8,8]{1,0:T(8,128)} %param.23) | copy-start | bytes 772
  8.4 20.5 %copy-start.7 = (bf16[2048]{0:T(1024)(128)(2,1)S(1)}, bf16[2048]{0:T(1024)(128)(2,1)}, u32[]{:S(2)}) copy-start(bf16[2048]{0:T(1024)(128)(2,1)} %param.22) | copy-start | bytes 12292
  8.4 38.3 %copy-start.3 = (bf16[8,2048]{1,0:T(8,128)(2,1)S(1)}, bf16[8,2048]{1,0:T(8,128)(2,1)}, u32[]{:S(2)}) copy-start(bf16[8,2048]{1,0:T(8,128)(2,1)} %param.14) | copy-start | bytes 98308
  13.7 12.0 %all-to-all-start = ((bf16[8,4,512]{2,0,1:T(8,128)(2,1)}), bf16[8,4,512]{2,0,1:T(8,128)(2,1)S(1)}, u32[]{:S(2)}, u32[]{:S(2)}) async-start(bf16[8,4,512]{2,0,1:T(8,128)(2,1)} %copy.28), calls=%async_computation | async-start | bytes 65536 | tf_op jit(solution)/shard_map/all_to_all | solution.py:68
  20.1 26.6 %reduce-scatter.2.cloned.1.call-start = ((), (), s32[]{:S(2)}) async-start(), calls=%async_computation.4 | async-start | bytes 327680 | tf_op jit(solution)/shard_map/reduce_scatter | solution.py:69
  67.3 0.8 copy-start.1
  70.6 8.6 %copy-start.5 = (f32[8,8]{1,0:T(8,128)S(1)}, f32[8,8]{1,0:T(8,128)}, u32[]{:S(2)}) copy-start(f32[8,8]{1,0:T(8,128)} %param.24) | copy-start | bytes 772
  74.7 22.4 %copy-start.2 = (f32[8,2048]{1,0:T(8,128)S(1)}, f32[8,2048]{1,0:T(8,128)}, u32[]{:S(2)}) copy-start(f32[8,2048]{1,0:T(8,128)} %reduce-scatter.2.cloned.1.call-done) | copy-start | bytes 196612
  74.7 22.4 %copy-start.4 = (bf16[8,2048]{1,0:T(8,128)(2,1)S(1)}, bf16[8,2048]{1,0:T(8,128)(2,1)}, u32[]{:S(2)}) copy-start(bf16[8,2048]{1,0:T(8,128)(2,1)} %param.14) | copy-start | bytes 98308
  74.7 20.1 %all-to-all-start.2 = ((bf16[16,8,2048]{2,1,0:T(8,128)(2,1)}), bf16[16,8,2048]{2,1,0:T(8,128)(2,1)}, u32[]{:S(2)}, u32[]{:S(2)}) async-start(bf16[16,8,2048]{2,1,0:T(8,128)(2,1)} %fusion.10), calls=%async_computation.3 | async-start | bytes 1048576 | tf_op jit(solution)/shard_map/all_to_all | solution.py:98
Sparse Core Ops, SparseCore 0:
  28.6 18.0 reduce-scatter.1
where the time goes:
time: 105 us
  waiting for transfers between devices  38.6 us (37%)
  blocking collectives  18.4 us (18%)
  matrix products  15.2 us (14%)
  between operations  13.5 us (13%)
  starting transfers between devices  10.7 us (10%)
  other arithmetic  4.37 us (4%)
  local copies, waits for them, and re-layouts  3.83 us (4%)
    all_to_all x1, blocking collectives, layer_rows(): lax.all_to_all(outgoing, ('expert', 'sub'), split_axis=0, concat_axis=0,...  18.4 us
    reduce_scatter x1, waiting for transfers between devices, layer_rows(): lax.psum_scatter(jnp.dot(spread, out_weight, preferred_element_type=jnp.f...  17.7 us
    all_to_all x1, waiting for transfers between devices, layer_rows(): lax.all_to_all(result.reshape(arrived.shape), ('expert', 'sub'), split_ax...  15.4 us
    all_to_all x1, starting transfers between devices, layer_rows(): lax.all_to_all(context, 'sub', split_axis=1, concat_axis=0, tiled=True)  6.32 us
    all_to_all x1, waiting for transfers between devices, layer_rows(): lax.all_to_all(context, 'sub', split_axis=1, concat_axis=0, tiled=True)  5.57 us
    all_to_all x1, starting transfers between devices, layer_rows(): lax.all_to_all(result.reshape(arrived.shape), ('expert', 'sub'), split_ax...  4.37 us
    dot_general x1, matrix products, run_expert(): jnp.dot(activated, down_matrix, preferred_element_type=jnp.float32)  4.11 us
    dot_general x1, matrix products, layer_rows(): jnp.dot(spread, out_weight, preferred_element_type=jnp.float32)  2.75 us
  transfers between devices with their start and end apart: 3, of which 3 were waited for; matrix products, arithmetic and copies ran while one was open for 1% of the time, Pallas kernels for 0%

commit v1 on v0

v1 whole, which is shorter than its diff:
```python
import functools
import math

import jax
import jax.numpy as jnp
from jax import lax
from jax.experimental import pallas as pl
from jax.experimental.pallas import tpu as pltpu
from jax.sharding import PartitionSpec as P

HEAD_DIM = 128
LANES = 128
BF16, F32 = jnp.bfloat16, jnp.float32
VMEM = pl.BlockSpec(memory_space=pltpu.VMEM)
SMEM = pl.BlockSpec(memory_space=pltpu.SMEM)
ANY = pl.BlockSpec(memory_space=pl.ANY)


def params(mib):
    return pltpu.CompilerParams(vmem_limit_bytes=mib * 2**20)


def attend_kernel(len_ref, q_ref, nk_ref, nv_ref, k_hbm, v_hbm, out_ref, k_buf, v_buf, sems):
    k_copy = pltpu.make_async_copy(k_hbm, k_buf, sems.at[0])
    v_copy = pltpu.make_async_copy(v_hbm, v_buf, sems.at[1])
    k_copy.start()
    v_copy.start()
    streams, frames, kv_width = k_buf.shape
    heads = q_ref.shape[1] // HEAD_DIM
    group = heads // (kv_width // HEAD_DIM)
    scale = 1.0 / math.sqrt(HEAD_DIM)
    query = q_ref[...].astype(F32)
    new_key = nk_ref[...].astype(F32)
    zero = jnp.zeros((streams, HEAD_DIM), F32)
    rows, new_scores = [], []
    for h in range(heads):
        g = h // group
        q = query[:, h * HEAD_DIM : (h + 1) * HEAD_DIM]
        rows.append(
            jnp.concatenate([q if b == g else zero for b in range(kv_width // HEAD_DIM)], axis=1)
        )
        k = new_key[:, g * HEAD_DIM : (g + 1) * HEAD_DIM]
        new_scores.append(jnp.sum(q * k, axis=1, keepdims=True) * scale)
    spread = jnp.concatenate(rows, axis=0).astype(BF16)
    row = lax.broadcasted_iota(jnp.int32, (streams, streams * frames), 0)
    col = lax.broadcasted_iota(jnp.int32, (streams, streams * frames), 1)
    end = jnp.zeros_like(row)
    for s in range(streams):
        end = jnp.where(row == s, len_ref[s] + s * frames, end)
    valid = (col >= row * frames) & (col < end)
    k_copy.wait()
    scores = lax.dot_general(
        spread,
        k_buf[...].reshape(streams * frames, kv_width),
        (((1,), (1,)), ((), ())),
        preferred_element_type=F32,
    )
    probs, new_probs = [], []
    for h in range(heads):
        old = jnp.where(valid, scores[h * streams : (h + 1) * streams] * scale, -1e30)
        new = new_scores[h]
        top = jnp.maximum(jnp.max(old, axis=1, keepdims=True), new)
        old = jnp.exp(old - top)
        new = jnp.exp(new - top)
        total = jnp.sum(old, axis=1, keepdims=True) + new
        probs.append(old / total)
        new_probs.append((new / total).astype(BF16).astype(F32))
    probs = jnp.concatenate(probs, axis=0).astype(BF16)
    v_copy.wait()
    context = jnp.dot(
        probs, v_buf[...].reshape(streams * frames, kv_width), preferred_element_type=F32
    )
    new_value = nv_ref[...].astype(F32)
    width = out_ref.shape[2]
    for h in range(heads):
        c = (h // group) * HEAD_DIM
        part = context[h * streams : (h + 1) * streams, c : c + HEAD_DIM]
        part = part + new_probs[h] * new_value[:, c : c + HEAD_DIM]
        at = h * HEAD_DIM
        out_ref[at // width, :, at % width : at % width + HEAD_DIM] = part.astype(BF16)


def project_kernel(x_ref, w_ref, out_ref):
    pieces, streams, depth = x_ref.shape
    x = x_ref[...].astype(F32).reshape(pieces * streams, depth).astype(BF16)
    y = jnp.dot(x, w_ref[...], preferred_element_type=F32)
    out_ref[...] = y.reshape(pieces, streams, y.shape[1]).astype(BF16)


def norm_kernel(experts, part_ref, res_ref, gain_ref, ids_ref, gates_ref, hidden_ref, out_ref):
    hidden = res_ref[...].astype(F32)
    for i in range(part_ref.shape[0]):
        hidden = hidden + part_ref[i].astype(F32)
    hidden_ref[...] = hidden
    width = hidden.shape[1]
    normed = hidden * lax.rsqrt(jnp.mean(hidden * hidden, axis=1, keepdims=True) + 1e-06)
    normed = (normed * gain_ref[...].astype(F32)).astype(BF16)
    gates = gates_ref[...]
    weights = gates / jnp.sum(gates, axis=1, keepdims=True)
    ids = ids_ref[...]
    lane = lax.broadcasted_iota(jnp.int32, (ids.shape[0], out_ref.shape[2] - width), 1)
    label = jnp.where(lane >= experts, lane - experts, lane)
    table = jnp.zeros(lane.shape, F32)
    for k in range(ids.shape[1]):
        table = table + jnp.where(label == ids[:, k : k + 1], weights[:, k : k + 1], 0.0)
    high = table.astype(BF16)
    low = (table - high.astype(F32)).astype(BF16)
    table = jnp.where(lane < experts, high.astype(F32), low.astype(F32)).astype(BF16)
    for i in range(out_ref.shape[0]):
        out_ref[i, :, :width] = normed
        out_ref[i, :, width:] = table


def expert_kernel(experts, me_ref, own_ref, other_ref, gate_ref, up_ref, down_ref, keep_ref, send_ref):
    chips, streams, _ = own_ref.shape
    width = down_ref.shape[1]
    half = chips * streams

    def load(ref):
        return ref[...].astype(F32).reshape(half, ref.shape[2])

    full = jnp.concatenate([load(own_ref), load(other_ref)], axis=0)
    rows = full[:, :width].astype(BF16)
    table = full[:, width:]
    lane = lax.broadcasted_iota(jnp.int32, table.shape, 1)
    mine = me_ref[0]
    chosen = (lane == mine) | (lane == mine + experts)
    weight = jnp.sum(jnp.where(chosen, table, 0.0), axis=1, keepdims=True)
    gate = jnp.dot(rows, gate_ref[...], preferred_element_type=F32)
    up = jnp.dot(rows, up_ref[...], preferred_element_type=F32)
    act = (gate / (1.0 + jnp.exp(-gate)) * up).astype(BF16)
    y = jnp.dot(act, down_ref[...], preferred_element_type=F32) * weight
    keep_ref[...] = y[:half]
    send_ref[...] = y[half:].astype(BF16)


def body(
    residual,
    query,
    new_key,
    new_value,
    key_cache,
    value_cache,
    cache_len,
    out_weight,
    norm_gain,
    expert_ids,
    gate_scores,
    expert_gate,
    expert_up,
    expert_down,
):
    streams, width = residual.shape
    n_expert, n_sub = lax.axis_size("expert"), lax.axis_size("sub")
    experts = n_expert * n_sub
    chips = experts // 2
    both = ("expert", "sub")
    same_core = [
        [(2 * i + core) * n_sub + s for i in range(n_expert // 2) for s in range(n_sub)]
        for core in range(2)
    ]
    twins = [(i, i ^ 1) for i in range(n_expert)]
    shape = jax.ShapeDtypeStruct

    context = pl.pallas_call(
        attend_kernel,
        out_shape=shape((n_sub, streams, width // n_sub), BF16),
        in_specs=[SMEM, VMEM, VMEM, VMEM, ANY, ANY],
        out_specs=VMEM,
        scratch_shapes=[
            pltpu.VMEM(key_cache.shape, BF16),
            pltpu.VMEM(value_cache.shape, BF16),
            pltpu.SemaphoreType.DMA((2,)),
        ],
        compiler_params=params(16),
        name="attend",
    )(cache_len, query, new_key, new_value, key_cache, value_cache)
    context = lax.all_to_all(context, "sub", split_axis=0, concat_axis=0, tiled=True)

    partial = pl.pallas_call(
        project_kernel,
        out_shape=shape((n_sub, streams, width), BF16),
        in_specs=[VMEM, VMEM],
        out_specs=VMEM,
        compiler_params=params(16),
        name="project",
    )(context, out_weight)
    partial = lax.all_to_all(partial, "sub", split_axis=0, concat_axis=0, tiled=True)

    table = -(-2 * experts // LANES) * LANES
    hidden, rows = pl.pallas_call(
        functools.partial(norm_kernel, experts),
        out_shape=(shape((streams, width), F32), shape((chips, streams, width + table), BF16)),
        in_specs=[VMEM] * 5,
        out_specs=(VMEM, VMEM),
        compiler_params=params(16),
        name="norm",
    )(partial, residual, norm_gain.reshape(1, width), expert_ids, gate_scores)
    own = lax.all_to_all(
        rows, both, split_axis=0, concat_axis=0, tiled=True, axis_index_groups=same_core
    )
    other = lax.ppermute(own, "expert", twins)

    me = (lax.axis_index("expert") * n_sub + lax.axis_index("sub")).reshape(1)
    half = chips * streams
    keep, send = pl.pallas_call(
        functools.partial(expert_kernel, experts),
        out_shape=(shape((half, width), F32), shape((half, width), BF16)),
        in_specs=[SMEM] + [VMEM] * 5,
        out_specs=(VMEM, VMEM),
        compiler_params=params(48),
        name="expert",
    )(me, own, other, expert_gate[0], expert_up[0], expert_down[0])
    got = lax.ppermute(send, "expert", twins)
    summed = (keep + got.astype(F32)).astype(BF16).reshape(chips, streams, width)
    back = lax.all_to_all(
        summed, both, split_axis=0, concat_axis=0, tiled=True, axis_index_groups=same_core
    )
    return (hidden + jnp.sum(back.astype(F32), axis=0)).astype(BF16)


def solution(mesh):
    rows = P(("groups", "expert", "sub"), None)
    cache = P(("groups", "expert", "sub"), None, None)
    weights = P(("expert", "sub"), None, None)
    return jax.shard_map(
        body,
        mesh=mesh,
        in_specs=(
            rows,
            rows,
            rows,
            rows,
            cache,
            cache,
            P(("groups", "expert", "sub")),
            P("sub", None),
            P(),
            rows,
            rows,
            weights,
            weights,
            weights,
        ),
        out_specs=rows,
        check_vma=False,
    )
```

time: 105 us -> 65.6 us (0.62)
  waiting for transfers between devices: 38.6 us -> 8.28 us
  blocking collectives: 18.4 us -> 36.7 us
  matrix products: 15.2 us -> 0 us
  between operations: 13.5 us -> 0.05 us
  Pallas kernels: 0 us -> 7.5 us
  starting transfers between devices: 10.7 us -> 3.53 us
  local copies, waits for them, and re-layouts: 3.83 us -> 8.24 us
  other arithmetic: 4.37 us -> 0.71 us
    all_to_all x1 -> x3, blocking collectives: 18.4 us -> 36.7 us  [the longest x1 12.8 us: body(): lax.all_to_all(summed, both, split_axis=0, concat_axis=0, tiled=True, axi...]
    reduce_scatter x1 -> x0, waiting for transfers between devices: 17.7 us -> none  [layer_rows(): lax.psum_scatter(jnp.dot(spread, out_weight, preferred_element_type=jnp.f...]
    all_to_all x2 -> x1, waiting for transfers between devices: 21 us -> 5.19 us  [body(): lax.all_to_all(partial, 'sub', split_axis=0, concat_axis=0, tiled=True)]
    dot_general x7 -> x0, matrix products: 15.2 us -> none  [the longest x1 4.11 us: run_expert(): jnp.dot(activated, down_matrix, preferred_element_type=jnp.float32)]
    pallas_call x0 -> x4, Pallas kernels: none -> 7.5 us  [the longest x1 4.41 us: body(): pl.pallas_call(functools.partial(expert_kernel, experts), out_shape=(shap...]
    all_to_all x2 -> x1, starting transfers between devices: 10.7 us -> 3.32 us  [body(): lax.all_to_all(partial, 'sub', split_axis=0, concat_axis=0, tiled=True)]
    unnamed x16 -> x22, local copies, waits for them, and re-layouts: 0.84 us -> 7.54 us
    ppermute x0 -> x2, waiting for transfers between devices: none -> 3.09 us  [the longest x1 1.69 us: body(): other = lax.ppermute(own, 'expert', twins)]
where the time goes in v1:
time: 65.6 us; the launch traced here: 65 us
  blocking collectives  36.7 us (56%)
  waiting for transfers between devices  8.28 us (13%)
  local copies, waits for them, and re-layouts  8.24 us (13%)
  Pallas kernels  7.5 us (11%)
  starting transfers between devices  3.53 us (5%)
  other arithmetic  0.71 us (1%)
    all_to_all x1, blocking collectives, body(): lax.all_to_all(summed, both, split_axis=0, concat_axis=0, tiled=True, axi...  12.8 us
    all_to_all x1, blocking collectives, body(): lax.all_to_all(rows, both, split_axis=0, concat_axis=0, tiled=True, axis_...  12.1 us
    all_to_all x1, blocking collectives, body(): lax.all_to_all(context, 'sub', split_axis=0, concat_axis=0, tiled=True)  11.8 us
    unnamed x22, local copies, waits for them, and re-layouts  7.54 us
    all_to_all x1, waiting for transfers between devices, body(): lax.all_to_all(partial, 'sub', split_axis=0, concat_axis=0, tiled=True)  5.19 us
    pallas_call x1, Pallas kernels, body(): pl.pallas_call(functools.partial(expert_kernel, experts), out_shape=(shap...  4.41 us
    all_to_all x1, starting transfers between devices, body(): lax.all_to_all(partial, 'sub', split_axis=0, concat_axis=0, tiled=True)  3.32 us
    pallas_call x1, Pallas kernels, body(): pl.pallas_call(attend_kernel, out_shape=shape((n_sub, streams, width // n...  1.79 us
  transfers between devices with their start and end apart: 3, of which 3 were waited for; matrix products, arithmetic and copies ran while one was open for 1% of the time, Pallas kernels for 0%

profile of v1, /device:TPU:0, one launch (start us, length us, event | category | flops | bytes accessed | tf_op | source)
XLA Modules:
  0.0 65.0 jit_solution(17583050421883003257)
XLA Ops:
  0.0 0.0 copy-start.1
  0.0 0.0 copy-start.2
  0.0 1.4 %copy-done.2 = bf16[8,128,512]{2,1,0:T(8,128)(2,1)S(1)} copy-done((bf16[8,128,512]{2,1,0:T(8,128)(2,1)S(1)}, bf16[8,128,512]{2,1,0:T(8,128)(2,1)}, u32[]{:S(2)}) %copy-start.2) | copy-done | bytes 1048600
  1.4 0.0 copy-start.3
  1.4 1.2 %copy-done.3 = bf16[8,128,512]{2,1,0:T(8,128)(2,1)S(1)} copy-done((bf16[8,128,512]{2,1,0:T(8,128)(2,1)S(1)}, bf16[8,128,512]{2,1,0:T(8,128)(2,1)}, u32[]{:S(2)}) %copy-start.3) | copy-done | bytes 1048600
  2.6 0.0 copy-start.4
  2.6 0.8 %copy-done.4 = bf16[8,2048]{1,0:T(8,128)(2,1)S(1)} copy-done((bf16[8,2048]{1,0:T(8,128)(2,1)S(1)}, bf16[8,2048]{1,0:T(8,128)(2,1)}, u32[]{:S(2)}) %copy-start.4) | copy-done | bytes 32792
  3.4 0.7 %copy-done.6 = bf16[8,512]{1,0:T(8,128)(2,1)S(1)} copy-done((bf16[8,512]{1,0:T(8,128)(2,1)S(1)}, bf16[8,512]{1,0:T(8,128)(2,1)}, u32[]{:S(2)}) %copy-start.6) | copy-done | bytes 8216
  4.1 0.0 copy-start.7
  4.1 0.7 %copy-done.7 = bf16[8,512]{1,0:T(8,128)(2,1)S(1)} copy-done((bf16[8,512]{1,0:T(8,128)(2,1)S(1)}, bf16[8,512]{1,0:T(8,128)(2,1)}, u32[]{:S(2)}) %copy-start.7) | copy-done | bytes 8216
  4.8 0.0 copy-start.10
  4.8 0.7 %copy-done.10 = s32[8]{0:T(128)S(1)} copy-done((s32[8]{0:T(128)S(1)}, s32[8]{0:T(128)}, u32[]{:S(2)}) %copy-start.10) | copy-done | bytes 56
  5.4 1.8 %attend.1 = bf16[4,8,512]{2,1,0:T(8,128)(2,1)S(1)} custom-call(s32[8]{0:T(128)S(1)} %copy-done.10, bf16[8,2048]{1,0:T(8,128)(2,1)S(1)} %copy-done.4, bf16[8,512]{1,0:T(8,128)(2,1)S(1)} %copy-done.6, bf16[8,512]{1,0:T(8,128)(2,1)S(1)} %copy-done.7, bf16[8,128,512]{2,1,0:T(8,128)(2,1)S(1)} %copy-done.2, bf16[8,128,512]{2,1,0:T(8,128)(2,1)S(1)} %copy-done.3), custom_call_target="tpu_custom_call" | custom-call | tf_op jit(solution)/shard_map/attend/pallas_call | solution.py:165
  7.2 11.8 %all_to_all.20.x_ref = bf16[4,8,512]{2,1,0:T(8,128)(2,1)S(1)} all-to-all(bf16[4,8,512]{2,1,0:T(8,128)(2,1)S(1)} %attend.1), channel_id=1, replica_groups=mesh['groups'=2,'expert'=4,'sub'=4] {'sub'}, dimensions={0} | all-to-all | bytes 65536 | tf_op jit(solution)/shard_map/all_to_all | solution.py:178
  19.0 0.0 copy-done.1
  19.0 1.1 %project.1 = bf16[4,8,2048]{2,1,0:T(8,128)(2,1)} custom-call(bf16[4,8,512]{2,1,0:T(8,128)(2,1)S(1)} %all_to_all.20.x_ref, bf16[512,2048]{1,0:T(8,128)(2,1)S(1)} %copy-done.1), custom_call_target="tpu_custom_call" | custom-call | tf_op jit(solution)/shard_map/project/pallas_call | solution.py:180
  20.1 3.3 %all-to-all-start.1 = ((bf16[4,8,2048]{2,1,0:T(8,128)(2,1)}), bf16[4,8,2048]{2,1,0:T(8,128)(2,1)S(1)}, u32[]{:S(2)}, u32[]{:S(2)}) async-start(bf16[4,8,2048]{2,1,0:T(8,128)(2,1)} %project.1), calls=%async_computation.1 | async-start | bytes 262144 | tf_op jit(solution)/shard_map/all_to_all | solution.py:188
  23.4 0.7 %reshape.9.gain_ref = bf16[1,2048]{1,0:T(2,128)(2,1)S(1)} reshape(bf16[2048]{0:T(1024)(128)(2,1)} %param.22) | data formatting | bytes 8192 | tf_op jit(solution)/shard_map/reshape | solution.py:198
  24.1 5.2 %all-to-all-done.1.part_ref = bf16[4,8,2048]{2,1,0:T(8,128)(2,1)S(1)} async-done(((bf16[4,8,2048]{2,1,0:T(8,128)(2,1)}), bf16[4,8,2048]{2,1,0:T(8,128)(2,1)S(1)}, u32[]{:S(2)}, u32[]{:S(2)}) %all-to-all-start.1) | async-done | bytes 131104 | tf_op jit(solution)/shard_map/all_to_all | solution.py:188
  29.3 0.8 %copy-done.5 = bf16[8,2048]{1,0:T(8,128)(2,1)S(1)} copy-done((bf16[8,2048]{1,0:T(8,128)(2,1)S(1)}, bf16[8,2048]{1,0:T(8,128)(2,1)}, u32[]{:S(2)}) %copy-start.5) | copy-done | bytes 32792
  30.1 0.7 %copy-done.8 = s32[8,8]{1,0:T(8,128)S(1)} copy-done((s32[8,8]{1,0:T(8,128)S(1)}, s32[8,8]{1,0:T(8,128)}, u32[]{:S(2)}) %copy-start.8) | copy-done | bytes 280
  30.8 0.7 %copy-done.9 = f32[8,8]{1,0:T(8,128)S(1)} copy-done((f32[8,8]{1,0:T(8,128)S(1)}, f32[8,8]{1,0:T(8,128)}, u32[]{:S(2)}) %copy-start.9) | copy-done | bytes 280
  31.5 0.2 norm.1
  31.7 12.1 %all_to_all.21.own_ref = bf16[8,8,2176]{2,1,0:T(8,128)(2,1)S(1)} all-to-all(bf16[8,8,2176]{2,1,0:T(8,128)(2,1)S(1)} %get-tuple-element.10), channel_id=1, replica_groups={{0,1,2,3,8,9,10,11},{4,5,6,7,12,13,14,15},{16,17,18,19,24,25,26,27},{20..., dimensions={0} | all-to-all | bytes 557056 | tf_op jit(solution)/shard_map/all_to_all | solution.py:199
  43.8 0.0 collective-permute-start
  43.8 1.7 %collective-permute-done.other_ref = bf16[8,8,2176]{2,1,0:T(8,128)(2,1)} collective-permute-done((bf16[8,8,2176]{2,1,0:T(8,128)(2,1)S(1)}, bf16[8,8,2176]{2,1,0:T(8,128)(2,1)}, u32[]{:S(2)}, u32[]{:S(2)}) %collective-permute-start) | collective-permute-done | bytes 278560 | tf_op jit(solution)/shard_map/ppermute | solution.py:202
  45.5 0.0 copy-done
  45.5 4.4 %expert.1 = (f32[64,2048]{1,0:T(8,128)S(1)}, bf16[64,2048]{1,0:T(8,128)(2,1)S(1)}) custom-call(s32[1]{0:T(128)} %bitcast.me_ref, bf16[8,8,2176]{2,1,0:T(8,128)(2,1)S(1)} %all_to_all.21.own_ref, bf16[8,8,2176]{2,1,0:T(8,128)(2,1)} %collective-permute-done.other_ref, bf16[2048,768]{1,0:T(8,128)(2,1)S(1)} %bitcast.6, bf16[2048,768]{1,0:T(8,128)(2,1)} %bitcast.7, ...), custom_call_target="tpu_custom_call" | custom-call | tf_op jit(solution)/shard_map/expert/pallas_call | solution.py:206
  49.9 0.2 collective-permute-start.1
  50.1 1.4 %collective-permute-done.1 = bf16[64,2048]{1,0:T(8,128)(2,1)S(1)} collective-permute-done((bf16[64,2048]{1,0:T(8,128)(2,1)S(1)}, bf16[64,2048]{1,0:T(8,128)(2,1)S(1)}, u32[]{:S(2)}, u32[]{:S(2)}) %collective-permute-start.1) | collective-permute-done | bytes 262176 | tf_op jit(solution)/shard_map/ppermute | solution.py:214
  51.6 12.8 %all_to_all.22 = bf16[8,8,2048]{2,1,0:T(8,128)(2,1)S(1)} all-to-all(bf16[8,8,2048]{2,1,0:T(8,128)(2,1)S(1)} %fusion), channel_id=1, replica_groups={{0,1,2,3,8,9,10,11},{4,5,6,7,12,13,14,15},{16,17,18,19,24,25,26,27},{20..., dimensions={0} | all-to-all | bytes 524288 | tf_op jit(solution)/shard_map/all_to_all | solution.py:216
  64.4 0.6 add_convert_fusion.1
  (7 shorter events, 0.1 us)
Async XLA Ops:
  0.0 19.0 %copy-start.1 = (bf16[512,2048]{1,0:T(8,128)(2,1)S(1)}, bf16[512,2048]{1,0:T(8,128)(2,1)}, u32[]{:S(2)}) copy-start(bf16[512,2048]{1,0:T(8,128)(2,1)} %w_ref.1) | copy-start | bytes 6291460
  0.0 1.4 %copy-start.2 = (bf16[8,128,512]{2,1,0:T(8,128)(2,1)S(1)}, bf16[8,128,512]{2,1,0:T(8,128)(2,1)}, u32[]{:S(2)}) copy-start(bf16[8,128,512]{2,1,0:T(8,128)(2,1)} %k_hbm.1) | copy-start | bytes 3145732
  1.4 1.2 %copy-start.3 = (bf16[8,128,512]{2,1,0:T(8,128)(2,1)S(1)}, bf16[8,128,512]{2,1,0:T(8,128)(2,1)}, u32[]{:S(2)}) copy-start(bf16[8,128,512]{2,1,0:T(8,128)(2,1)} %v_hbm.1) | copy-start | bytes 3145732
  2.6 0.8 %copy-start.4 = (bf16[8,2048]{1,0:T(8,128)(2,1)S(1)}, bf16[8,2048]{1,0:T(8,128)(2,1)}, u32[]{:S(2)}) copy-start(bf16[8,2048]{1,0:T(8,128)(2,1)} %q_ref.1) | copy-start | bytes 98308
  3.4 0.7 %copy-start.6 = (bf16[8,512]{1,0:T(8,128)(2,1)S(1)}, bf16[8,512]{1,0:T(8,128)(2,1)}, u32[]{:S(2)}) copy-start(bf16[8,512]{1,0:T(8,128)(2,1)} %nk_ref.1) | copy-start | bytes 24580
  4.1 0.7 %copy-start.7 = (bf16[8,512]{1,0:T(8,128)(2,1)S(1)}, bf16[8,512]{1,0:T(8,128)(2,1)}, u32[]{:S(2)}) copy-start(bf16[8,512]{1,0:T(8,128)(2,1)} %nv_ref.1) | copy-start | bytes 24580
  4.8 0.7 %copy-start.10 = (s32[8]{0:T(128)S(1)}, s32[8]{0:T(128)}, u32[]{:S(2)}) copy-start(s32[8]{0:T(128)} %len_ref.1) | copy-start | bytes 100
  5.4 40.1 %copy-start = (bf16[1,2048,768]{2,1,0:T(8,128)(2,1)S(1)}, bf16[1,2048,768]{2,1,0:T(8,128)(2,1)}, u32[]{:S(2)}) copy-start(bf16[1,2048,768]{2,1,0:T(8,128)(2,1)} %param.25) | copy-start | bytes 9437188
  20.1 9.2 %all-to-all-start.1 = ((bf16[4,8,2048]{2,1,0:T(8,128)(2,1)}), bf16[4,8,2048]{2,1,0:T(8,128)(2,1)S(1)}, u32[]{:S(2)}, u32[]{:S(2)}) async-start(bf16[4,8,2048]{2,1,0:T(8,128)(2,1)} %project.1), calls=%async_computation.1 | async-start | bytes 262144 | tf_op jit(solution)/shard_map/all_to_all | solution.py:188
  29.3 0.8 %copy-start.5 = (bf16[8,2048]{1,0:T(8,128)(2,1)S(1)}, bf16[8,2048]{1,0:T(8,128)(2,1)}, u32[]{:S(2)}) copy-start(bf16[8,2048]{1,0:T(8,128)(2,1)} %res_ref.1) | copy-start | bytes 98308
  30.1 0.7 %copy-start.8 = (s32[8,8]{1,0:T(8,128)S(1)}, s32[8,8]{1,0:T(8,128)}, u32[]{:S(2)}) copy-start(s32[8,8]{1,0:T(8,128)} %ids_ref.1) | copy-start | bytes 772
  30.8 0.7 %copy-start.9 = (f32[8,8]{1,0:T(8,128)S(1)}, f32[8,8]{1,0:T(8,128)}, u32[]{:S(2)}) copy-start(f32[8,8]{1,0:T(8,128)} %gates_ref.1) | copy-start | bytes 772
  43.8 1.7 %collective-permute-start = (bf16[8,8,2176]{2,1,0:T(8,128)(2,1)S(1)}, bf16[8,8,2176]{2,1,0:T(8,128)(2,1)}, u32[]{:S(2)}, u32[]{:S(2)}) collective-permute-start(bf16[8,8,2176]{2,1,0:T(8,128)(2,1)S(1)} %all_to_all.21.own_ref), channel_id=1, source_target_pairs={{0,4},{4,0},{8,12},{12,8},{1,5},{5,1},{9,13},{13,9},{2,6},{6,2},{1... | collective-permute-start | bytes 835592 | tf_op jit(solution)/shard_map/ppermute | solution.py:202
  49.9 1.6 %collective-permute-start.1 = (bf16[64,2048]{1,0:T(8,128)(2,1)S(1)}, bf16[64,2048]{1,0:T(8,128)(2,1)S(1)}, u32[]{:S(2)}, u32[]{:S(2)}) collective-permute-start(bf16[64,2048]{1,0:T(8,128)(2,1)S(1)} %get-tuple-element.12), channel_id=1, source_target_pairs={{0,4},{4,0},{8,12},{12,8},{1,5},{5,1},{9,13},{13,9},{2,6},{6,2},{1... | collective-permute-start | bytes 786440 | tf_op jit(solution)/shard_map/ppermute | solution.py:214

commit v2 on v1

--- a/solution.py
+++ b/solution.py
@@ -13,18 +13,55 @@
 BF16, F32 = jnp.bfloat16, jnp.float32
 VMEM = pl.BlockSpec(memory_space=pltpu.VMEM)
 SMEM = pl.BlockSpec(memory_space=pltpu.SMEM)
-ANY = pl.BlockSpec(memory_space=pl.ANY)
-
-
+HBM = pl.BlockSpec(memory_space=pltpu.HBM)
 def params(mib):
     return pltpu.CompilerParams(vmem_limit_bytes=mib * 2**20)
 
 
-def attend_kernel(len_ref, q_ref, nk_ref, nv_ref, k_hbm, v_hbm, out_ref, k_buf, v_buf, sems):
-    k_copy = pltpu.make_async_copy(k_hbm, k_buf, sems.at[0])
-    v_copy = pltpu.make_async_copy(v_hbm, v_buf, sems.at[1])
-    k_copy.start()
-    v_copy.start()
+def in_hbm(x):
+    return pltpu.with_memory_space_constraint(x, pltpu.HBM)
+
+
+def attend_kernel(
+    experts,
+    len_hbm,
+    q_hbm,
+    nk_hbm,
+    nv_hbm,
+    k_hbm,
+    v_hbm,
+    res_hbm,
+    ids_hbm,
+    gates_hbm,
+    out_ref,
+    res_ref,
+    table_ref,
+    len_ref,
+    q_ref,
+    nk_ref,
+    nv_ref,
+    k_buf,
+    v_buf,
+    ids_ref,
+    gates_ref,
+    sems,
+):
+    pairs = (
+        (k_hbm, k_buf),
+        (q_hbm, q_ref),
+        (nk_hbm, nk_ref),
+        (len_hbm, len_ref),
+        (v_hbm, v_buf),
+        (nv_hbm, nv_ref),
+        (ids_hbm, ids_ref),
+        (gates_hbm, gates_ref),
+        (res_hbm, res_ref),
+    )
+    copies = [pltpu.make_async_copy(a, b, sems.at[i]) for i, (a, b) in enumerate(pairs)]
+    for copy in copies:
+        copy.start()
+    for copy in copies[1:4]:
+        copy.wait()
     streams, frames, kv_width = k_buf.shape
     heads = q_ref.shape[1] // HEAD_DIM
     group = heads // (kv_width // HEAD_DIM)
@@ -48,7 +85,7 @@
     for s in range(streams):
         end = jnp.where(row == s, len_ref[s] + s * frames, end)
     valid = (col >= row * frames) & (col < end)
-    k_copy.wait()
+    copies[0].wait()
     scores = lax.dot_general(
         spread,
         k_buf[...].reshape(streams * frames, kv_width),
@@ -66,7 +103,8 @@
         probs.append(old / total)
         new_probs.append((new / total).astype(BF16).astype(F32))
     probs = jnp.concatenate(probs, axis=0).astype(BF16)
-    v_copy.wait()
+    copies[4].wait()
+    copies[5].wait()
     context = jnp.dot(
         probs, v_buf[...].reshape(streams * frames, kv_width), preferred_element_type=F32
     )
@@ -78,6 +116,18 @@
         part = part + new_probs[h] * new_value[:, c : c + HEAD_DIM]
         at = h * HEAD_DIM
         out_ref[at // width, :, at % width : at % width + HEAD_DIM] = part.astype(BF16)
+    for copy in copies[6:]:
+        copy.wait()
+    gates = gates_ref[...]
+    weights = gates / jnp.sum(gates, axis=1, keepdims=True)
+    ids = ids_ref[...]
+    lane = lax.broadcasted_iota(jnp.int32, table_ref.shape, 1)
+    label = jnp.where(lane >= experts, lane - experts, lane)
+    table = jnp.zeros(lane.shape, F32)
+    for k in range(ids.shape[1]):
+        table = table + jnp.where(label == ids[:, k : k + 1], weights[:, k : k + 1], 0.0)
+    high = table.astype(BF16).astype(F32)
+    table_ref[...] = jnp.where(lane < experts, high, table - high).astype(BF16)
 
 
 def project_kernel(x_ref, w_ref, out_ref):
@@ -87,7 +137,7 @@
     out_ref[...] = y.reshape(pieces, streams, y.shape[1]).astype(BF16)
 
 
-def norm_kernel(experts, part_ref, res_ref, gain_ref, ids_ref, gates_ref, hidden_ref, out_ref):
+def norm_kernel(part_ref, res_ref, gain_ref, table_ref, hidden_ref, out_ref):
     hidden = res_ref[...].astype(F32)
     for i in range(part_ref.shape[0]):
         hidden = hidden + part_ref[i].astype(F32)
@@ -95,23 +145,30 @@
     width = hidden.shape[1]
     normed = hidden * lax.rsqrt(jnp.mean(hidden * hidden, axis=1, keepdims=True) + 1e-06)
     normed = (normed * gain_ref[...].astype(F32)).astype(BF16)
-    gates = gates_ref[...]
-    weights = gates / jnp.sum(gates, axis=1, keepdims=True)
-    ids = ids_ref[...]
-    lane = lax.broadcasted_iota(jnp.int32, (ids.shape[0], out_ref.shape[2] - width), 1)
-    label = jnp.where(lane >= experts, lane - experts, lane)
-    table = jnp.zeros(lane.shape, F32)
-    for k in range(ids.shape[1]):
-        table = table + jnp.where(label == ids[:, k : k + 1], weights[:, k : k + 1], 0.0)
-    high = table.astype(BF16)
-    low = (table - high.astype(F32)).astype(BF16)
-    table = jnp.where(lane < experts, high.astype(F32), low.astype(F32)).astype(BF16)
+    table = table_ref[...]
     for i in range(out_ref.shape[0]):
         out_ref[i, :, :width] = normed
         out_ref[i, :, width:] = table
 
 
-def expert_kernel(experts, me_ref, own_ref, other_ref, gate_ref, up_ref, down_ref, keep_ref, send_ref):
+def expert_kernel(
+    experts,
+    me_ref,
+    own_ref,
+    other_ref,
+    gate_ref,
+    up_hbm,
+    down_hbm,
+    keep_ref,
+    send_ref,
+    up_ref,
+    down_ref,
+    sems,
+):
+    up_copy = pltpu.make_async_copy(up_hbm, up_ref, sems.at[0])
+    down_copy = pltpu.make_async_copy(down_hbm, down_ref, sems.at[1])
+    up_copy.start()
+    down_copy.start()
     chips, streams, _ = own_ref.shape
     width = down_ref.shape[1]
     half = chips * streams
@@ -127,8 +184,11 @@
     chosen = (lane == mine) | (lane == mine + experts)
     weight = jnp.sum(jnp.where(chosen, table, 0.0), axis=1, keepdims=True)
     gate = jnp.dot(rows, gate_ref[...], preferred_element_type=F32)
+    act = gate / (1.0 + jnp.exp(-gate))
+    up_copy.wait()
     up = jnp.dot(rows, up_ref[...], preferred_element_type=F32)
-    act = (gate / (1.0 + jnp.exp(-gate)) * up).astype(BF16)
+    act = (act * up).astype(BF16)
+    down_copy.wait()
     y = jnp.dot(act, down_ref[...], preferred_element_type=F32) * weight
     keep_ref[...] = y[:half]
     send_ref[...] = y[half:].astype(BF16)
@@ -162,19 +222,46 @@
     twins = [(i, i ^ 1) for i in range(n_expert)]
     shape = jax.ShapeDtypeStruct
 
-    context = pl.pallas_call(
-        attend_kernel,
-        out_shape=shape((n_sub, streams, width // n_sub), BF16),
-        in_specs=[SMEM, VMEM, VMEM, VMEM, ANY, ANY],
-        out_specs=VMEM,
+    table_width = -(-2 * experts // LANES) * LANES
+    context, resident, table = pl.pallas_call(
+        functools.partial(attend_kernel, experts),
+        out_shape=(
+            shape((n_sub, streams, width // n_sub), BF16),
+            shape(residual.shape, BF16),
+            shape((streams, table_width), BF16),
+        ),
+        in_specs=[HBM] * 9,
+        out_specs=(VMEM, VMEM, VMEM),
         scratch_shapes=[
+            pltpu.SMEM(cache_len.shape, jnp.int32),
+            pltpu.VMEM(query.shape, BF16),
+            pltpu.VMEM(new_key.shape, BF16),
+            pltpu.VMEM(new_value.shape, BF16),
             pltpu.VMEM(key_cache.shape, BF16),
             pltpu.VMEM(value_cache.shape, BF16),
-            pltpu.SemaphoreType.DMA((2,)),
+            pltpu.VMEM(expert_ids.shape, jnp.int32),
+            pltpu.VMEM(gate_scores.shape, F32),
+            pltpu.SemaphoreType.DMA((9,)),
         ],
-        compiler_params=params(16),
+        compiler_params=params(12),
         name="attend",
-    )(cache_len, query, new_key, new_value, key_cache, value_cache)
+    )(
+        *(
+            in_hbm(a)
+            for a in (
+                cache_len,
+                query,
+                new_key,
+                new_value,
+                key_cache,
+                value_cache,
+                residual,
+                expert_ids,
+                gate_scores,
+            )
+        )
+    )
+    gate = expert_gate[0]
     context = lax.all_to_all(context, "sub", split_axis=0, concat_axis=0, tiled=True)
 
     partial = pl.pallas_call(
@@ -182,20 +269,19 @@
         out_shape=shape((n_sub, streams, width), BF16),
         in_specs=[VMEM, VMEM],
         out_specs=VMEM,
-        compiler_params=params(16),
+        compiler_params=params(8),
         name="project",
     )(context, out_weight)
     partial = lax.all_to_all(partial, "sub", split_axis=0, concat_axis=0, tiled=True)
 
-    table = -(-2 * experts // LANES) * LANES
     hidden, rows = pl.pallas_call(
-        functools.partial(norm_kernel, experts),
-        out_shape=(shape((streams, width), F32), shape((chips, streams, width + table), BF16)),
-        in_specs=[VMEM] * 5,
+        norm_kernel,
+        out_shape=(shape((streams, width), F32), shape((chips, streams, width + table_width), BF16)),
+        in_specs=[VMEM] * 4,
         out_specs=(VMEM, VMEM),
-        compiler_params=params(16),
+        compiler_params=params(8),
         name="norm",
-    )(partial, residual, norm_gain.reshape(1, width), expert_ids, gate_scores)
+    )(partial, resident, norm_gain.reshape(1, width), table)
     own = lax.all_to_all(
         rows, both, split_axis=0, concat_axis=0, tiled=True, axis_index_groups=same_core
     )
@@ -206,11 +292,16 @@
     keep, send = pl.pallas_call(
         functools.partial(expert_kernel, experts),
         out_shape=(shape((half, width), F32), shape((half, width), BF16)),
-        in_specs=[SMEM] + [VMEM] * 5,
+        in_specs=[SMEM, VMEM, VMEM, VMEM, HBM, HBM],
         out_specs=(VMEM, VMEM),
-        compiler_params=params(48),
+        scratch_shapes=[
+            pltpu.VMEM(expert_up.shape[1:], BF16),
+            pltpu.VMEM(expert_down.shape[1:], BF16),
+            pltpu.SemaphoreType.DMA((2,)),
+        ],
+        compiler_params=params(18 + half // 16),
         name="expert",
-    )(me, own, other, expert_gate[0], expert_up[0], expert_down[0])
+    )(me, own, other, gate, in_hbm(expert_up[0]), in_hbm(expert_down[0]))
     got = lax.ppermute(send, "expert", twins)
     summed = (keep + got.astype(F32)).astype(BF16).reshape(chips, streams, width)
     back = lax.all_to_all(

time: 65.6 us -> 59.2 us (0.902)
  local copies, waits for them, and re-layouts: 8.24 us -> 0.02 us
  Pallas kernels: 7.5 us -> 8.87 us
  waiting for transfers between devices: 8.28 us -> 8.96 us
    unnamed x22 -> x6, local copies, waits for them, and re-layouts: 7.54 us -> 0.01 us
    pallas_call x2, Pallas kernels: 1.97 us -> 2.78 us  [the longest x1 2.64 us: body(): pl.pallas_call(functools.partial(attend_kernel, experts), out_shape=(shap...]
    reshape x1, local copies, waits for them, and re-layouts: 0.7 us -> 0.01 us  [body(): norm_gain.reshape(1, width)]
    all_to_all x1, waiting for transfers between devices: 5.19 us -> 5.86 us  [body(): lax.all_to_all(partial, 'sub', split_axis=0, concat_axis=0, tiled=True)]
  transfers between devices with their start and end apart: 3 -> 3, of which waited for: 3 -> 3; matrix products, arithmetic and copies ran while one was open for 1% -> 0% of each run, Pallas kernels for 0% -> 0%
where the time goes in v2:
time: 59.2 us; the launch traced here: 58.8 us
  blocking collectives  36.7 us (62%)
  waiting for transfers between devices  8.96 us (15%)
  Pallas kernels  8.87 us (15%)
  starting transfers between devices  3.52 us (6%)
  other arithmetic  0.71 us (1%)
    all_to_all x1, blocking collectives, body(): lax.all_to_all(summed, both, split_axis=0, concat_axis=0, tiled=True, axi...  12.8 us
    all_to_all x1, blocking collectives, body(): lax.all_to_all(rows, both, split_axis=0, concat_axis=0, tiled=True, axis_...  12.2 us
    all_to_all x1, blocking collectives, body(): lax.all_to_all(context, 'sub', split_axis=0, concat_axis=0, tiled=True)  11.8 us
    all_to_all x1, waiting for transfers between devices, body(): lax.all_to_all(partial, 'sub', split_axis=0, concat_axis=0, tiled=True)  5.86 us
    pallas_call x1, Pallas kernels, body(): pl.pallas_call(functools.partial(expert_kernel, experts), out_shape=(shap...  4.96 us
    all_to_all x1, starting transfers between devices, body(): lax.all_to_all(partial, 'sub', split_axis=0, concat_axis=0, tiled=True)  3.32 us
    pallas_call x1, Pallas kernels, body(): pl.pallas_call(functools.partial(attend_kernel, experts), out_shape=(shap...  2.64 us
    ppermute x1, waiting for transfers between devices, body(): other = lax.ppermute(own, 'expert', twins)  1.69 us
  transfers between devices with their start and end apart: 3, of which 3 were waited for; matrix products, arithmetic and copies ran while one was open for 0% of the time, Pallas kernels for 0%

profile of v2, /device:TPU:0, one launch (start us, length us, event | category | flops | bytes accessed | tf_op | source)
XLA Modules:
  0.0 58.8 jit_solution(1119310761144265051)
XLA Ops:
  0.0 0.0 copy-start.1
  0.0 0.0 copy-start.2
  0.0 0.0 copy-start
  0.0 2.6 %attend.1 = (bf16[4,8,512]{2,1,0:T(8,128)(2,1)S(1)}, bf16[8,2048]{1,0:T(8,128)(2,1)S(1)}, bf16[8,128]{1,0:T(8,128)(2,1)S(1)}) custom-call(s32[8]{0:T(128)} %len_hbm.1, bf16[8,2048]{1,0:T(8,128)(2,1)} %q_hbm.1, bf16[8,512]{1,0:T(8,128)(2,1)} %nk_hbm.1, bf16[8,512]{1,0:T(8,128)(2,1)} %nv_hbm.1, bf16[8,128,512]{2,1,0:T(8,128)(2,1)} %k_hbm.1, ...), custom_call_target="tpu_custom_call" | custom-call | tf_op jit(solution)/shard_map/attend/pallas_call | solution.py:226
  2.7 11.8 %all_to_all.20.x_ref = bf16[4,8,512]{2,1,0:T(8,128)(2,1)S(1)} all-to-all(bf16[4,8,512]{2,1,0:T(8,128)(2,1)S(1)} %get-tuple-element.12), channel_id=1, replica_groups=mesh['groups'=2,'expert'=4,'sub'=4] {'sub'}, dimensions={0} | all-to-all | bytes 65536 | tf_op jit(solution)/shard_map/all_to_all | solution.py:265
  14.4 0.0 copy-done.1
  14.4 1.1 %project.1 = bf16[4,8,2048]{2,1,0:T(8,128)(2,1)} custom-call(bf16[4,8,512]{2,1,0:T(8,128)(2,1)S(1)} %all_to_all.20.x_ref, bf16[512,2048]{1,0:T(8,128)(2,1)S(1)} %copy-done.1), custom_call_target="tpu_custom_call" | custom-call | tf_op jit(solution)/shard_map/project/pallas_call | solution.py:267
  15.6 3.3 %all-to-all-start.1 = ((bf16[4,8,2048]{2,1,0:T(8,128)(2,1)}), bf16[4,8,2048]{2,1,0:T(8,128)(2,1)S(1)}, u32[]{:S(2)}, u32[]{:S(2)}) async-start(bf16[4,8,2048]{2,1,0:T(8,128)(2,1)} %project.1), calls=%async_computation.1 | async-start | bytes 262144 | tf_op jit(solution)/shard_map/all_to_all | solution.py:275
  18.9 0.0 copy-done.2
  18.9 5.9 %all-to-all-done.1.part_ref = bf16[4,8,2048]{2,1,0:T(8,128)(2,1)S(1)} async-done(((bf16[4,8,2048]{2,1,0:T(8,128)(2,1)}), bf16[4,8,2048]{2,1,0:T(8,128)(2,1)S(1)}, u32[]{:S(2)}, u32[]{:S(2)}) %all-to-all-start.1) | async-done | bytes 131104 | tf_op jit(solution)/shard_map/all_to_all | solution.py:275
  24.8 0.1 norm.1
  24.9 12.2 %all_to_all.21.own_ref = bf16[8,8,2176]{2,1,0:T(8,128)(2,1)S(1)} all-to-all(bf16[8,8,2176]{2,1,0:T(8,128)(2,1)S(1)} %get-tuple-element.16), channel_id=1, replica_groups={{0,1,2,3,8,9,10,11},{4,5,6,7,12,13,14,15},{16,17,18,19,24,25,26,27},{20..., dimensions={0} | all-to-all | bytes 557056 | tf_op jit(solution)/shard_map/all_to_all | solution.py:285
  37.1 0.0 collective-permute-start
  37.1 1.7 %collective-permute-done.other_ref = bf16[8,8,2176]{2,1,0:T(8,128)(2,1)} collective-permute-done((bf16[8,8,2176]{2,1,0:T(8,128)(2,1)S(1)}, bf16[8,8,2176]{2,1,0:T(8,128)(2,1)}, u32[]{:S(2)}, u32[]{:S(2)}) %collective-permute-start) | collective-permute-done | bytes 278560 | tf_op jit(solution)/shard_map/ppermute | solution.py:288
  38.8 0.0 copy-done
  38.8 5.0 %expert.1 = (f32[64,2048]{1,0:T(8,128)S(1)}, bf16[64,2048]{1,0:T(8,128)(2,1)S(1)}) custom-call(s32[1]{0:T(128)} %bitcast.me_ref, bf16[8,8,2176]{2,1,0:T(8,128)(2,1)S(1)} %all_to_all.21.own_ref, bf16[8,8,2176]{2,1,0:T(8,128)(2,1)} %collective-permute-done.other_ref, bf16[2048,768]{1,0:T(8,128)(2,1)S(1)} %bitcast.6, bf16[2048,768]{1,0:T(8,128)(2,1)} %bitcast.7, ...), custom_call_target="tpu_custom_call" | custom-call | tf_op jit(solution)/shard_map/expert/pallas_call | solution.py:292
  43.7 0.2 collective-permute-start.1
  43.9 1.4 %collective-permute-done.1 = bf16[64,2048]{1,0:T(8,128)(2,1)S(1)} collective-permute-done((bf16[64,2048]{1,0:T(8,128)(2,1)S(1)}, bf16[64,2048]{1,0:T(8,128)(2,1)S(1)}, u32[]{:S(2)}, u32[]{:S(2)}) %collective-permute-start.1) | collective-permute-done | bytes 262176 | tf_op jit(solution)/shard_map/ppermute | solution.py:305
  45.4 12.8 %all_to_all.22 = bf16[8,8,2048]{2,1,0:T(8,128)(2,1)S(1)} all-to-all(bf16[8,8,2048]{2,1,0:T(8,128)(2,1)S(1)} %fusion), channel_id=1, replica_groups={{0,1,2,3,8,9,10,11},{4,5,6,7,12,13,14,15},{16,17,18,19,24,25,26,27},{20..., dimensions={0} | all-to-all | bytes 524288 | tf_op jit(solution)/shard_map/all_to_all | solution.py:307
  58.2 0.6 %add_convert_fusion.1 = bf16[8,2048]{1,0:T(8,128)(2,1)} fusion(f32[8,2048]{1,0:T(8,128)S(1)} %get-tuple-element.15, f32[8,2048]{1,0:T(8,128)S(1)} %convert_reduce_fusion), kind=kLoop, calls=%fused_computation.3 | loop fusion | flops 32768 | bytes 163840 | tf_op jit(solution)/shard_map/convert_element_type | solution.py:310
  (3 shorter events, 0.1 us)
Async XLA Ops:
  0.0 14.4 %copy-start.1 = (bf16[512,2048]{1,0:T(8,128)(2,1)S(1)}, bf16[512,2048]{1,0:T(8,128)(2,1)}, u32[]{:S(2)}) copy-start(bf16[512,2048]{1,0:T(8,128)(2,1)} %w_ref.1) | copy-start | bytes 6291460
  0.0 18.9 %copy-start.2 = (bf16[2048]{0:T(1024)(128)(2,1)S(1)}, bf16[2048]{0:T(1024)(128)(2,1)}, u32[]{:S(2)}) copy-start(bf16[2048]{0:T(1024)(128)(2,1)} %param.22) | copy-start | bytes 12292
  0.0 38.8 %copy-start = (bf16[1,2048,768]{2,1,0:T(8,128)(2,1)S(1)}, bf16[1,2048,768]{2,1,0:T(8,128)(2,1)}, u32[]{:S(2)}) copy-start(bf16[1,2048,768]{2,1,0:T(8,128)(2,1)} %param.25) | copy-start | bytes 9437188
  15.6 9.2 %all-to-all-start.1 = ((bf16[4,8,2048]{2,1,0:T(8,128)(2,1)}), bf16[4,8,2048]{2,1,0:T(8,128)(2,1)S(1)}, u32[]{:S(2)}, u32[]{:S(2)}) async-start(bf16[4,8,2048]{2,1,0:T(8,128)(2,1)} %project.1), calls=%async_computation.1 | async-start | bytes 262144 | tf_op jit(solution)/shard_map/all_to_all | solution.py:275
  37.1 1.7 %collective-permute-start = (bf16[8,8,2176]{2,1,0:T(8,128)(2,1)S(1)}, bf16[8,8,2176]{2,1,0:T(8,128)(2,1)}, u32[]{:S(2)}, u32[]{:S(2)}) collective-permute-start(bf16[8,8,2176]{2,1,0:T(8,128)(2,1)S(1)} %all_to_all.21.own_ref), channel_id=1, source_target_pairs={{0,4},{4,0},{8,12},{12,8},{1,5},{5,1},{9,13},{13,9},{2,6},{6,2},{1... | collective-permute-start | bytes 835592 | tf_op jit(solution)/shard_map/ppermute | solution.py:288
  43.7 1.6 %collective-permute-start.1 = (bf16[64,2048]{1,0:T(8,128)(2,1)S(1)}, bf16[64,2048]{1,0:T(8,128)(2,1)S(1)}, u32[]{:S(2)}, u32[]{:S(2)}) collective-permute-start(bf16[64,2048]{1,0:T(8,128)(2,1)S(1)} %get-tuple-element.18), channel_id=1, source_target_pairs={{0,4},{4,0},{8,12},{12,8},{1,5},{5,1},{9,13},{13,9},{2,6},{6,2},{1... | collective-permute-start | bytes 786440 | tf_op jit(solution)/shard_map/ppermute | solution.py:305

commit v3 on v2

--- a/solution.py
+++ b/solution.py
@@ -20,6 +20,10 @@
 
 def in_hbm(x):
     return pltpu.with_memory_space_constraint(x, pltpu.HBM)
+
+
+def in_vmem(x):
+    return pltpu.with_memory_space_constraint(x, pltpu.VMEM)
 
 
 def attend_kernel(
@@ -137,14 +141,14 @@
     out_ref[...] = y.reshape(pieces, streams, y.shape[1]).astype(BF16)
 
 
-def norm_kernel(part_ref, res_ref, gain_ref, table_ref, hidden_ref, out_ref):
+def norm_kernel(part_ref, res_ref, gain_ref, table_ref, _up, _down, hidden_ref, out_ref):
     hidden = res_ref[...].astype(F32)
     for i in range(part_ref.shape[0]):
         hidden = hidden + part_ref[i].astype(F32)
     hidden_ref[...] = hidden
     width = hidden.shape[1]
     normed = hidden * lax.rsqrt(jnp.mean(hidden * hidden, axis=1, keepdims=True) + 1e-06)
-    normed = (normed * gain_ref[...].astype(F32)).astype(BF16)
+    normed = (normed * gain_ref[...].astype(F32).reshape(1, width)).astype(BF16)
     table = table_ref[...]
     for i in range(out_ref.shape[0]):
         out_ref[i, :, :width] = normed
@@ -153,22 +157,14 @@
 
 def expert_kernel(
     experts,
-    me_ref,
     own_ref,
     other_ref,
     gate_ref,
-    up_hbm,
-    down_hbm,
+    up_ref,
+    down_ref,
     keep_ref,
     send_ref,
-    up_ref,
-    down_ref,
-    sems,
 ):
-    up_copy = pltpu.make_async_copy(up_hbm, up_ref, sems.at[0])
-    down_copy = pltpu.make_async_copy(down_hbm, down_ref, sems.at[1])
-    up_copy.start()
-    down_copy.start()
     chips, streams, _ = own_ref.shape
     width = down_ref.shape[1]
     half = chips * streams
@@ -180,15 +176,13 @@
     rows = full[:, :width].astype(BF16)
     table = full[:, width:]
     lane = lax.broadcasted_iota(jnp.int32, table.shape, 1)
-    mine = me_ref[0]
+    mine = lax.axis_index("expert") * lax.axis_size("sub") + lax.axis_index("sub")
     chosen = (lane == mine) | (lane == mine + experts)
     weight = jnp.sum(jnp.where(chosen, table, 0.0), axis=1, keepdims=True)
     gate = jnp.dot(rows, gate_ref[...], preferred_element_type=F32)
     act = gate / (1.0 + jnp.exp(-gate))
-    up_copy.wait()
     up = jnp.dot(rows, up_ref[...], preferred_element_type=F32)
     act = (act * up).astype(BF16)
-    down_copy.wait()
     y = jnp.dot(act, down_ref[...], preferred_element_type=F32) * weight
     keep_ref[...] = y[:half]
     send_ref[...] = y[half:].astype(BF16)
@@ -277,31 +271,25 @@
     hidden, rows = pl.pallas_call(
         norm_kernel,
         out_shape=(shape((streams, width), F32), shape((chips, streams, width + table_width), BF16)),
-        in_specs=[VMEM] * 4,
+        in_specs=[VMEM] * 4 + [HBM] * 2,
         out_specs=(VMEM, VMEM),
         compiler_params=params(8),
         name="norm",
-    )(partial, resident, norm_gain.reshape(1, width), table)
+    )(partial, resident, norm_gain, table, in_hbm(expert_up[0]), in_hbm(expert_down[0]))
     own = lax.all_to_all(
         rows, both, split_axis=0, concat_axis=0, tiled=True, axis_index_groups=same_core
     )
     other = lax.ppermute(own, "expert", twins)
 
-    me = (lax.axis_index("expert") * n_sub + lax.axis_index("sub")).reshape(1)
     half = chips * streams
     keep, send = pl.pallas_call(
         functools.partial(expert_kernel, experts),
         out_shape=(shape((half, width), F32), shape((half, width), BF16)),
-        in_specs=[SMEM, VMEM, VMEM, VMEM, HBM, HBM],
+        in_specs=[VMEM] * 5,
         out_specs=(VMEM, VMEM),
-        scratch_shapes=[
-            pltpu.VMEM(expert_up.shape[1:], BF16),
-            pltpu.VMEM(expert_down.shape[1:], BF16),
-            pltpu.SemaphoreType.DMA((2,)),
-        ],
         compiler_params=params(18 + half // 16),
         name="expert",
-    )(me, own, other, gate, in_hbm(expert_up[0]), in_hbm(expert_down[0]))
+    )(own, other, in_vmem(gate), in_vmem(expert_up[0]), in_vmem(expert_down[0]))
     got = lax.ppermute(send, "expert", twins)
     summed = (keep + got.astype(F32)).astype(BF16).reshape(chips, streams, width)
     back = lax.all_to_all(

time: 59.2 us -> 54.3 us (0.917)
  blocking collectives: 36.7 us -> 45.4 us
  waiting for transfers between devices: 8.96 us -> 2.95 us
  Pallas kernels: 8.87 us -> 4.72 us
  starting transfers between devices: 3.52 us -> 0.2 us
    all_to_all x0 -> x1, blocking collectives: none -> 8.45 us  [body(): lax.all_to_all(partial, 'sub', split_axis=0, concat_axis=0, tiled=True)]
    all_to_all x1 -> x0, waiting for transfers between devices: 5.86 us -> none  [body(): lax.all_to_all(partial, 'sub', split_axis=0, concat_axis=0, tiled=True)]
    pallas_call x1, Pallas kernels: 4.96 us -> 1.48 us  [body(): pl.pallas_call(functools.partial(expert_kernel, experts), out_shape=(shap...]
    all_to_all x1 -> x0, starting transfers between devices: 3.32 us -> none  [body(): lax.all_to_all(partial, 'sub', split_axis=0, concat_axis=0, tiled=True)]
    pallas_call x1, Pallas kernels: 1.13 us -> 0.46 us  [body(): pl.pallas_call(project_kernel, out_shape=shape((n_sub, streams, width), B...]
  transfers between devices with their start and end apart: 3 -> 2, of which waited for: 3 -> 2; matrix products, arithmetic and copies ran while one was open for 0% -> 0% of each run, Pallas kernels for 0% -> 0%
where the time goes in v3:
time: 54.3 us; the launch traced here: 54 us
  blocking collectives  45.4 us (84%)
  Pallas kernels  4.72 us (9%)
  waiting for transfers between devices  2.95 us (5%)
  other arithmetic  0.71 us (1%)
    all_to_all x1, blocking collectives, body(): lax.all_to_all(summed, both, split_axis=0, concat_axis=0, tiled=True, axi...  12.8 us
    all_to_all x1, blocking collectives, body(): lax.all_to_all(rows, both, split_axis=0, concat_axis=0, tiled=True, axis_...  12.4 us
    all_to_all x1, blocking collectives, body(): lax.all_to_all(context, 'sub', split_axis=0, concat_axis=0, tiled=True)  11.8 us
    all_to_all x1, blocking collectives, body(): lax.all_to_all(partial, 'sub', split_axis=0, concat_axis=0, tiled=True)  8.45 us
    pallas_call x1, Pallas kernels, body(): pl.pallas_call(functools.partial(attend_kernel, experts), out_shape=(shap...  2.64 us
    ppermute x1, waiting for transfers between devices, body(): other = lax.ppermute(own, 'expert', twins)  1.56 us
    pallas_call x1, Pallas kernels, body(): pl.pallas_call(functools.partial(expert_kernel, experts), out_shape=(shap...  1.48 us
    ppermute x1, waiting for transfers between devices, body(): got = lax.ppermute(send, 'expert', twins)  1.4 us
  transfers between devices with their start and end apart: 2, of which 2 were waited for; matrix products, arithmetic and copies ran while one was open for 0% of the time, Pallas kernels for 0%

profile of v3, /device:TPU:0, one launch (start us, length us, event | category | flops | bytes accessed | tf_op | source)
XLA Modules:
  0.0 54.0 jit_solution(11169444572959203714)
XLA Ops:
  0.0 0.0 copy-start.3
  0.0 0.0 copy-start.4
  0.0 2.6 %attend.1 = (bf16[4,8,512]{2,1,0:T(8,128)(2,1)S(1)}, bf16[8,2048]{1,0:T(8,128)(2,1)S(1)}, bf16[8,128]{1,0:T(8,128)(2,1)S(1)}) custom-call(s32[8]{0:T(128)} %len_hbm.1, bf16[8,2048]{1,0:T(8,128)(2,1)} %q_hbm.1, bf16[8,512]{1,0:T(8,128)(2,1)} %nk_hbm.1, bf16[8,512]{1,0:T(8,128)(2,1)} %nv_hbm.1, bf16[8,128,512]{2,1,0:T(8,128)(2,1)} %k_hbm.1, ...), custom_call_target="tpu_custom_call" | custom-call | tf_op jit(solution)/shard_map/attend/pallas_call | solution.py:220
  2.7 11.8 %all_to_all.20.x_ref = bf16[4,8,512]{2,1,0:T(8,128)(2,1)S(1)} all-to-all(bf16[4,8,512]{2,1,0:T(8,128)(2,1)S(1)} %get-tuple-element.12), channel_id=1, replica_groups=mesh['groups'=2,'expert'=4,'sub'=4] {'sub'}, dimensions={0} | all-to-all | bytes 65536 | tf_op jit(solution)/shard_map/all_to_all | solution.py:259
  14.4 0.0 copy-done.3
  14.4 0.0 copy-start.2
  14.4 0.5 project.1
  14.9 8.4 %all_to_all.21.part_ref = bf16[4,8,2048]{2,1,0:T(8,128)(2,1)S(1)} all-to-all(bf16[4,8,2048]{2,1,0:T(8,128)(2,1)S(1)} %project.1), channel_id=1, replica_groups=mesh['groups'=2,'expert'=4,'sub'=4] {'sub'}, dimensions={0} | all-to-all | bytes 262144 | tf_op jit(solution)/shard_map/all_to_all | solution.py:269
  23.3 0.0 copy-done.4
  23.3 0.0 copy-start
  23.3 0.0 copy-start.1
  23.3 0.1 norm.1
  23.5 12.4 %all_to_all.22.own_ref = bf16[8,8,2176]{2,1,0:T(8,128)(2,1)S(1)} all-to-all(bf16[8,8,2176]{2,1,0:T(8,128)(2,1)S(1)} %get-tuple-element.16), channel_id=1, replica_groups={{0,1,2,3,8,9,10,11},{4,5,6,7,12,13,14,15},{16,17,18,19,24,25,26,27},{20..., dimensions={0} | all-to-all | bytes 557056 | tf_op jit(solution)/shard_map/all_to_all | solution.py:279
  35.9 0.0 collective-permute-start
  35.9 1.6 %collective-permute-done.other_ref = bf16[8,8,2176]{2,1,0:T(8,128)(2,1)S(1)} collective-permute-done((bf16[8,8,2176]{2,1,0:T(8,128)(2,1)S(1)}, bf16[8,8,2176]{2,1,0:T(8,128)(2,1)S(1)}, u32[]{:S(2)}, u32[]{:S(2)}) %collective-permute-start) | collective-permute-done | bytes 278560 | tf_op jit(solution)/shard_map/ppermute | solution.py:282
  37.5 0.0 copy-done.2
  37.5 0.0 copy-done
  37.5 0.0 copy-done.1
  37.5 1.5 %expert.1 = (f32[64,2048]{1,0:T(8,128)S(1)}, bf16[64,2048]{1,0:T(8,128)(2,1)S(1)}) custom-call(bf16[8,8,2176]{2,1,0:T(8,128)(2,1)S(1)} %all_to_all.22.own_ref, bf16[8,8,2176]{2,1,0:T(8,128)(2,1)S(1)} %collective-permute-done.other_ref, bf16[2048,768]{1,0:T(8,128)(2,1)S(1)} %bitcast.9, bf16[2048,768]{1,0:T(8,128)(2,1)S(1)} %bitcast.6, ...), custom_call_target="tpu_custom_call" | custom-call | tf_op jit(solution)/shard_map/expert/pallas_call | solution.py:285
  39.0 0.2 collective-permute-start.1
  39.2 1.4 %collective-permute-done.1 = bf16[64,2048]{1,0:T(8,128)(2,1)S(1)} collective-permute-done((bf16[64,2048]{1,0:T(8,128)(2,1)S(1)}, bf16[64,2048]{1,0:T(8,128)(2,1)S(1)}, u32[]{:S(2)}, u32[]{:S(2)}) %collective-permute-start.1) | collective-permute-done | bytes 262176 | tf_op jit(solution)/shard_map/ppermute | solution.py:293
  40.6 12.8 %all_to_all.23 = bf16[8,8,2048]{2,1,0:T(8,128)(2,1)S(1)} all-to-all(bf16[8,8,2048]{2,1,0:T(8,128)(2,1)S(1)} %fusion), channel_id=1, replica_groups={{0,1,2,3,8,9,10,11},{4,5,6,7,12,13,14,15},{16,17,18,19,24,25,26,27},{20..., dimensions={0} | all-to-all | bytes 524288 | tf_op jit(solution)/shard_map/all_to_all | solution.py:295
  53.4 0.6 %add_convert_fusion.1 = bf16[8,2048]{1,0:T(8,128)(2,1)} fusion(f32[8,2048]{1,0:T(8,128)S(1)} %get-tuple-element.15, f32[8,2048]{1,0:T(8,128)S(1)} %convert_reduce_fusion), kind=kLoop, calls=%fused_computation.3 | loop fusion | flops 32768 | bytes 163840 | tf_op jit(solution)/shard_map/convert_element_type | solution.py:298
  (2 shorter events, 0.1 us)
Async XLA Ops:
  0.0 14.4 %copy-start.3 = (bf16[512,2048]{1,0:T(8,128)(2,1)S(1)}, bf16[512,2048]{1,0:T(8,128)(2,1)}, u32[]{:S(2)}) copy-start(bf16[512,2048]{1,0:T(8,128)(2,1)} %w_ref.1) | copy-start | bytes 6291460
  0.0 23.3 %copy-start.4 = (bf16[2048]{0:T(1024)(128)(2,1)S(1)}, bf16[2048]{0:T(1024)(128)(2,1)}, u32[]{:S(2)}) copy-start(bf16[2048]{0:T(1024)(128)(2,1)} %gain_ref.1) | copy-start | bytes 12292
  14.4 23.0 %copy-start.2 = (bf16[1,2048,768]{2,1,0:T(8,128)(2,1)S(1)}, bf16[1,2048,768]{2,1,0:T(8,128)(2,1)}, u32[]{:S(2)}) copy-start(bf16[1,2048,768]{2,1,0:T(8,128)(2,1)} %param.25) | copy-start | bytes 9437188
  23.3 14.1 %copy-start = (bf16[1,2048,768]{2,1,0:T(8,128)(2,1)S(1)}, bf16[1,2048,768]{2,1,0:T(8,128)(2,1)}, u32[]{:S(2)}) copy-start(bf16[1,2048,768]{2,1,0:T(8,128)(2,1)} %param.26) | copy-start | bytes 9437188
  23.3 14.1 %copy-start.1 = (bf16[1,768,2048]{2,1,0:T(8,128)(2,1)S(1)}, bf16[1,768,2048]{2,1,0:T(8,128)(2,1)}, u32[]{:S(2)}) copy-start(bf16[1,768,2048]{2,1,0:T(8,128)(2,1)} %param.27) | copy-start | bytes 9437188
  35.9 1.6 %collective-permute-start = (bf16[8,8,2176]{2,1,0:T(8,128)(2,1)S(1)}, bf16[8,8,2176]{2,1,0:T(8,128)(2,1)S(1)}, u32[]{:S(2)}, u32[]{:S(2)}) collective-permute-start(bf16[8,8,2176]{2,1,0:T(8,128)(2,1)S(1)} %all_to_all.22.own_ref), channel_id=1, source_target_pairs={{0,4},{4,0},{8,12},{12,8},{1,5},{5,1},{9,13},{13,9},{2,6},{6,2},{1... | collective-permute-start | bytes 835592 | tf_op jit(solution)/shard_map/ppermute | solution.py:282
  39.0 1.6 %collective-permute-start.1 = (bf16[64,2048]{1,0:T(8,128)(2,1)S(1)}, bf16[64,2048]{1,0:T(8,128)(2,1)S(1)}, u32[]{:S(2)}, u32[]{:S(2)}) collective-permute-start(bf16[64,2048]{1,0:T(8,128)(2,1)S(1)} %get-tuple-element.18), channel_id=1, source_target_pairs={{0,4},{4,0},{8,12},{12,8},{1,5},{5,1},{9,13},{13,9},{2,6},{6,2},{1... | collective-permute-start | bytes 786440 | tf_op jit(solution)/shard_map/ppermute | solution.py:293

commit v4 on v3

--- a/solution.py
+++ b/solution.py
@@ -28,6 +28,7 @@
 
 def attend_kernel(
     experts,
+    steps,
     len_hbm,
     q_hbm,
     nk_hbm,
@@ -37,9 +38,17 @@
     res_hbm,
     ids_hbm,
     gates_hbm,
-    out_ref,
+    weight_hbm,
+    gain_hbm,
+    *refs,
+):
+    out_refs = refs[: len(steps)]
+    (
     res_ref,
     table_ref,
+    weight_ref,
+    gain_ref,
+    ctx_ref,
     len_ref,
     q_ref,
     nk_ref,
@@ -49,7 +58,7 @@
     ids_ref,
     gates_ref,
     sems,
-):
+    ) = refs[len(steps) :]
     pairs = (
         (k_hbm, k_buf),
         (q_hbm, q_ref),
@@ -60,6 +69,8 @@
         (ids_hbm, ids_ref),
         (gates_hbm, gates_ref),
         (res_hbm, res_ref),
+        (weight_hbm, weight_ref),
+        (gain_hbm, gain_ref),
     )
     copies = [pltpu.make_async_copy(a, b, sems.at[i]) for i, (a, b) in enumerate(pairs)]
     for copy in copies:
@@ -113,13 +124,16 @@
         probs, v_buf[...].reshape(streams * frames, kv_width), preferred_element_type=F32
     )
     new_value = nv_ref[...].astype(F32)
-    width = out_ref.shape[2]
+    width = ctx_ref.shape[2]
     for h in range(heads):
         c = (h // group) * HEAD_DIM
         part = context[h * streams : (h + 1) * streams, c : c + HEAD_DIM]
         part = part + new_probs[h] * new_value[:, c : c + HEAD_DIM]
         at = h * HEAD_DIM
-        out_ref[at // width, :, at % width : at % width + HEAD_DIM] = part.astype(BF16)
+        ctx_ref[at // width, :, at % width : at % width + HEAD_DIM] = part
+    me = lax.axis_index("sub")
+    for step, out_ref in zip(steps, out_refs):
+        out_ref[...] = ctx_ref[jnp.bitwise_xor(me, step)].astype(BF16)
     for copy in copies[6:]:
         copy.wait()
     gates = gates_ref[...]
@@ -134,58 +148,68 @@
     table_ref[...] = jnp.where(lane < experts, high, table - high).astype(BF16)
 
 
-def project_kernel(x_ref, w_ref, out_ref):
-    pieces, streams, depth = x_ref.shape
-    x = x_ref[...].astype(F32).reshape(pieces * streams, depth).astype(BF16)
-    y = jnp.dot(x, w_ref[...], preferred_element_type=F32)
-    out_ref[...] = y.reshape(pieces, streams, y.shape[1]).astype(BF16)
-
-
-def norm_kernel(part_ref, res_ref, gain_ref, table_ref, _up, _down, hidden_ref, out_ref):
+def project_kernel(count, *refs):
+    x = jnp.concatenate([ref[...].astype(F32) for ref in refs[:count]], axis=0).astype(BF16)
+    y = jnp.dot(x, refs[count][...], preferred_element_type=F32)
+    streams = refs[0].shape[0]
+    for i, ref in enumerate(refs[-count:]):
+        ref[...] = y[i * streams : (i + 1) * streams].astype(ref.dtype)
+
+
+def norm_kernel(count, *refs):
+    res_ref, gain_ref, table_ref, _, _, hidden_ref, out_ref = refs[count:]
     hidden = res_ref[...].astype(F32)
-    for i in range(part_ref.shape[0]):
-        hidden = hidden + part_ref[i].astype(F32)
+    for ref in refs[:count]:
+        hidden = hidden + ref[...].astype(F32)
     hidden_ref[...] = hidden
     width = hidden.shape[1]
     normed = hidden * lax.rsqrt(jnp.mean(hidden * hidden, axis=1, keepdims=True) + 1e-06)
     normed = (normed * gain_ref[...].astype(F32).reshape(1, width)).astype(BF16)
-    table = table_ref[...]
-    for i in range(out_ref.shape[0]):
-        out_ref[i, :, :width] = normed
-        out_ref[i, :, width:] = table
-
-
-def expert_kernel(
-    experts,
-    own_ref,
-    other_ref,
-    gate_ref,
-    up_ref,
-    down_ref,
-    keep_ref,
-    send_ref,
-):
-    chips, streams, _ = own_ref.shape
-    width = down_ref.shape[1]
-    half = chips * streams
-
-    def load(ref):
-        return ref[...].astype(F32).reshape(half, ref.shape[2])
-
-    full = jnp.concatenate([load(own_ref), load(other_ref)], axis=0)
+    out_ref[:, :width] = normed
+    out_ref[:, width:] = table_ref[...]
+
+
+def join_kernel(*refs):
+    refs[-1][...] = jnp.concatenate([ref[...].astype(F32) for ref in refs[:-1]], axis=0).astype(BF16)
+
+
+def expert_kernel(experts, count, *refs):
+    full = jnp.concatenate([ref[...].astype(F32) for ref in refs[:count]], axis=0)
+    weight_refs, out_refs = refs[count : count + 6], refs[count + 6 :]
+    step, width = out_refs[0].shape
     rows = full[:, :width].astype(BF16)
     table = full[:, width:]
     lane = lax.broadcasted_iota(jnp.int32, table.shape, 1)
-    mine = lax.axis_index("expert") * lax.axis_size("sub") + lax.axis_index("sub")
-    chosen = (lane == mine) | (lane == mine + experts)
-    weight = jnp.sum(jnp.where(chosen, table, 0.0), axis=1, keepdims=True)
-    gate = jnp.dot(rows, gate_ref[...], preferred_element_type=F32)
-    act = gate / (1.0 + jnp.exp(-gate))
-    up = jnp.dot(rows, up_ref[...], preferred_element_type=F32)
-    act = (act * up).astype(BF16)
-    y = jnp.dot(act, down_ref[...], preferred_element_type=F32) * weight
-    keep_ref[...] = y[:half]
-    send_ref[...] = y[half:].astype(BF16)
+    major, minor, n_sub = lax.axis_index("expert"), lax.axis_index("sub"), lax.axis_size("sub")
+    total = None
+    for i, place in enumerate((major, jnp.bitwise_xor(major, 1))):
+        gate_ref, up_ref, down_ref = weight_refs[3 * i : 3 * i + 3]
+        expert = place * n_sub + minor
+        chosen = (lane == expert) | (lane == expert + experts)
+        weight = jnp.sum(jnp.where(chosen, table, 0.0), axis=1, keepdims=True)
+        gate = jnp.dot(rows, gate_ref[...], preferred_element_type=F32)
+        up = jnp.dot(rows, up_ref[...], preferred_element_type=F32)
+        act = (gate / (1.0 + jnp.exp(-gate)) * up).astype(BF16)
+        y = jnp.dot(act, down_ref[...], preferred_element_type=F32) * weight
+        total = y if total is None else total + y
+    for i, ref in enumerate(out_refs):
+        ref[...] = total[i * step : (i + 1) * step].astype(ref.dtype)
+
+
+def fold_kernel(count, *refs):
+    total = refs[0][...]
+    for ref in refs[1:count]:
+        total = total + ref[...].astype(F32)
+    step = refs[count].shape[0]
+    for i, ref in enumerate(refs[count:]):
+        ref[...] = total[i * step : (i + 1) * step].astype(ref.dtype)
+
+
+def finish_kernel(*refs):
+    total = refs[0][...]
+    for ref in refs[1:-1]:
+        total = total + ref[...].astype(F32)
+    refs[-1][...] = total.astype(BF16)
 
 
 def body(
@@ -207,26 +231,44 @@
     streams, width = residual.shape
     n_expert, n_sub = lax.axis_size("expert"), lax.axis_size("sub")
     experts = n_expert * n_sub
-    chips = experts // 2
-    both = ("expert", "sub")
-    same_core = [
-        [(2 * i + core) * n_sub + s for i in range(n_expert // 2) for s in range(n_sub)]
-        for core in range(2)
-    ]
     twins = [(i, i ^ 1) for i in range(n_expert)]
     shape = jax.ShapeDtypeStruct
 
     table_width = -(-2 * experts // LANES) * LANES
-    context, resident, table = pl.pallas_call(
-        functools.partial(attend_kernel, experts),
+    mine = (expert_gate, expert_up, expert_down)
+    twin = [lax.ppermute(w, "expert", twins) for w in mine[:2]]
+
+    steps = (0, *range(n_sub - 1, 0, -1))
+    chip_steps = (0, *range(n_expert - 2, 0, -2))
+
+    def exchange(blocks, axis="sub"):
+        size, order = (n_sub, steps) if axis == "sub" else (n_expert, chip_steps)
+        sent = [
+            lax.ppermute(block, axis, [(i, i ^ step) for i in range(size)])
+            for step, block in zip(order[1:], blocks[1:])
+        ]
+        return [blocks[0], *sent]
+
+    def gather(block):
+        sent = [
+            lax.ppermute(block, "sub", [(i, i ^ step) for i in range(n_sub)])
+            for step in reversed(steps[1:])
+        ]
+        return [block, *reversed(sent)]
+
+    *context, resident, table, out_weight, norm_gain = pl.pallas_call(
+        functools.partial(attend_kernel, experts, steps),
         out_shape=(
-            shape((n_sub, streams, width // n_sub), BF16),
+            *(shape((streams, width // n_sub), BF16) for _ in steps),
             shape(residual.shape, BF16),
             shape((streams, table_width), BF16),
+            pltpu.VMEM(out_weight.shape, BF16),
+            pltpu.VMEM(norm_gain.shape, BF16),
         ),
-        in_specs=[HBM] * 9,
-        out_specs=(VMEM, VMEM, VMEM),
+        in_specs=[HBM] * 11,
+        out_specs=(VMEM,) * (n_sub + 4),
         scratch_shapes=[
+            pltpu.VMEM((n_sub, streams, width // n_sub), F32),
             pltpu.SMEM(cache_len.shape, jnp.int32),
             pltpu.VMEM(query.shape, BF16),
             pltpu.VMEM(new_key.shape, BF16),
@@ -235,7 +277,7 @@
             pltpu.VMEM(value_cache.shape, BF16),
             pltpu.VMEM(expert_ids.shape, jnp.int32),
             pltpu.VMEM(gate_scores.shape, F32),
-            pltpu.SemaphoreType.DMA((9,)),
+            pltpu.SemaphoreType.DMA((11,)),
         ],
         compiler_params=params(12),
         name="attend",
@@ -252,50 +294,73 @@
                 residual,
                 expert_ids,
                 gate_scores,
+                out_weight,
+                norm_gain,
             )
         )
     )
-    gate = expert_gate[0]
-    context = lax.all_to_all(context, "sub", split_axis=0, concat_axis=0, tiled=True)
-
+    context, last, twin[0] = lax.optimization_barrier((exchange(context), expert_down, twin[0]))
+    twin.append(lax.ppermute(last, "expert", twins))
     partial = pl.pallas_call(
-        project_kernel,
-        out_shape=shape((n_sub, streams, width), BF16),
-        in_specs=[VMEM, VMEM],
-        out_specs=VMEM,
+        functools.partial(project_kernel, n_sub),
+        out_shape=tuple(shape((streams, width), BF16 if step else F32) for step in steps),
+        in_specs=[VMEM] * (n_sub + 1) + [HBM],
+        out_specs=(VMEM,) * n_sub,
         compiler_params=params(8),
         name="project",
-    )(context, out_weight)
-    partial = lax.all_to_all(partial, "sub", split_axis=0, concat_axis=0, tiled=True)
+    )(*context, out_weight, in_hbm(expert_gate[0]))
 
     hidden, rows = pl.pallas_call(
-        norm_kernel,
-        out_shape=(shape((streams, width), F32), shape((chips, streams, width + table_width), BF16)),
-        in_specs=[VMEM] * 4 + [HBM] * 2,
+        functools.partial(norm_kernel, n_sub),
+        out_shape=(
+            shape((streams, width), F32),
+            shape((streams, width + table_width), BF16),
+        ),
+        in_specs=[VMEM] * (n_sub + 3) + [HBM] * 2,
         out_specs=(VMEM, VMEM),
         compiler_params=params(8),
         name="norm",
-    )(partial, resident, norm_gain, table, in_hbm(expert_up[0]), in_hbm(expert_down[0]))
-    own = lax.all_to_all(
-        rows, both, split_axis=0, concat_axis=0, tiled=True, axis_index_groups=same_core
-    )
-    other = lax.ppermute(own, "expert", twins)
-
-    half = chips * streams
-    keep, send = pl.pallas_call(
-        functools.partial(expert_kernel, experts),
-        out_shape=(shape((half, width), F32), shape((half, width), BF16)),
-        in_specs=[VMEM] * 5,
-        out_specs=(VMEM, VMEM),
-        compiler_params=params(18 + half // 16),
+    )(
+        *exchange(partial),
+        resident,
+        norm_gain,
+        table,
+        in_hbm(expert_up[0]),
+        in_hbm(expert_down[0]),
+    )
+    chips = len(chip_steps)
+    rows = pl.pallas_call(
+        join_kernel,
+        out_shape=shape((chips * streams, width + table_width), BF16),
+        in_specs=[VMEM] * chips,
+        out_specs=VMEM,
+        compiler_params=params(4),
+        name="join",
+    )(*exchange([rows] * chips, "expert"))
+    summed = pl.pallas_call(
+        functools.partial(expert_kernel, experts, n_sub),
+        out_shape=tuple(shape((chips * streams, width), BF16 if step else F32) for step in steps),
+        in_specs=[VMEM] * (n_sub + 6),
+        out_specs=(VMEM,) * n_sub,
+        compiler_params=params(8 + experts * streams // 64),
         name="expert",
-    )(own, other, in_vmem(gate), in_vmem(expert_up[0]), in_vmem(expert_down[0]))
-    got = lax.ppermute(send, "expert", twins)
-    summed = (keep + got.astype(F32)).astype(BF16).reshape(chips, streams, width)
-    back = lax.all_to_all(
-        summed, both, split_axis=0, concat_axis=0, tiled=True, axis_index_groups=same_core
-    )
-    return (hidden + jnp.sum(back.astype(F32), axis=0)).astype(BF16)
+    )(*gather(rows), *(in_vmem(w[0]) for w in (*mine, *twin)))
+    summed = pl.pallas_call(
+        functools.partial(fold_kernel, n_sub),
+        out_shape=tuple(shape((streams, width), BF16 if step else F32) for step in chip_steps),
+        in_specs=[VMEM] * n_sub,
+        out_specs=(VMEM,) * chips,
+        compiler_params=params(8),
+        name="fold",
+    )(*exchange(summed))
+    return pl.pallas_call(
+        finish_kernel,
+        out_shape=shape((streams, width), BF16),
+        in_specs=[VMEM] * (chips + 1),
+        out_specs=VMEM,
+        compiler_params=params(4),
+        name="finish",
+    )(hidden, *exchange(summed, "expert"))
 
 
 def solution(mesh):

time: 54.3 us -> 48.7 us (0.90)
  blocking collectives: 45.4 us -> 0 us
  starting transfers between devices: 0.2 us -> 22.2 us
  waiting for transfers between devices: 2.95 us -> 18.8 us
  Pallas kernels: 4.72 us -> 7.56 us
  other arithmetic: 0.71 us -> 0 us
    all_to_all x4 -> x0, blocking collectives: 45.4 us -> none  [the longest x1 12.8 us: body(): lax.all_to_all(summed, both, split_axis=0, concat_axis=0, tiled=True, axi...]
    ppermute x2 -> x17, starting transfers between devices: 0.2 us -> 22.2 us  [the longest x11 17.3 us: exchange(): lax.ppermute(block, axis, [(i, i ^ step) for i in range(size)])]
    ppermute x2 -> x17, waiting for transfers between devices: 2.95 us -> 18.8 us  [the longest x11 14.3 us: exchange(): lax.ppermute(block, axis, [(i, i ^ step) for i in range(size)])]
    pallas_call x4 -> x7, Pallas kernels: 4.72 us -> 7.56 us  [the longest x1 3.5 us: body(): pl.pallas_call(functools.partial(expert_kernel, experts, n_sub), out_shap...]
    convert_element_type x1 -> x0, other arithmetic: 0.63 us -> none  [body(): return (hidden + jnp.sum(back.astype(F32), axis=0)).astype(BF16)]
  transfers between devices with their start and end apart: 2 -> 17, of which waited for: 2 -> 11; matrix products, arithmetic and copies ran while one was open for 0% -> 0% of each run, Pallas kernels for 0% -> 7%
where the time goes in v4:
time: 48.7 us; the launch traced here: 48.6 us
  starting transfers between devices  22.2 us (46%)
  waiting for transfers between devices  18.8 us (39%)
  Pallas kernels  7.56 us (16%)
    ppermute x11, starting transfers between devices, exchange(): lax.ppermute(block, axis, [(i, i ^ step) for i in range(size)])  17.3 us
    ppermute x11, waiting for transfers between devices, exchange(): lax.ppermute(block, axis, [(i, i ^ step) for i in range(size)])  14.3 us
    ppermute x3, waiting for transfers between devices, gather(): lax.ppermute(block, 'sub', [(i, i ^ step) for i in range(n_sub)])  4.46 us
    ppermute x3, starting transfers between devices, gather(): lax.ppermute(block, 'sub', [(i, i ^ step) for i in range(n_sub)])  4.39 us
    pallas_call x1, Pallas kernels, body(): pl.pallas_call(functools.partial(expert_kernel, experts, n_sub), out_shap...  3.5 us
    pallas_call x1, Pallas kernels, body(): pl.pallas_call(functools.partial(attend_kernel, experts, steps), out_shap...  2.82 us
  transfers between devices with their start and end apart: 17, of which 11 were waited for; matrix products, arithmetic and copies ran while one was open for 0% of the time, Pallas kernels for 7%

profile of v4, /device:TPU:0, one launch (start us, length us, event | category | flops | bytes accessed | tf_op | source)
XLA Modules:
  0.0 48.6 jit_solution(4209567519090530421)
XLA Ops:
  0.0 0.5 collective-permute-start.3
  0.5 2.8 %attend.1 = (bf16[8,512]{1,0:T(8,128)(2,1)S(1)}, bf16[8,512]{1,0:T(8,128)(2,1)S(1)}, bf16[8,512]{1,0:T(8,128)(2,1)S(1)}, bf16[8,512]{1,0:T(8,128)(2,1)S(1)}, bf1...) custom-call(s32[8]{0:T(128)} %len_hbm.1, ...), custom_call_target="tpu_custom_call" | custom-call | tf_op jit(solution)/shard_map/attend/pallas_call | solution.py:259
  3.3 4.6 %collective-permute-start = (bf16[8,512]{1,0:T(8,128)(2,1)S(1)}, bf16[8,512]{1,0:T(8,128)(2,1)S(1)}, u32[]{:S(2)}, u32[]{:S(2)}) collective-permute-start(bf16[8,512]{1,0:T(8,128)(2,1)S(1)} %get-tuple-element.32), channel_id=1, source_target_pairs={{0,3},{1,2},{2,1},{3,0},{4,7},{5,6},{6,5},{7,4},{8,11},{9,10},{10,... | collective-permute-start | bytes 24584 | tf_op jit(solution)/shard_map/ppermute | solution.py:247
  7.9 0.0 collective-permute-start.1
  7.9 0.6 %collective-permute-start.2 = (bf16[8,512]{1,0:T(8,128)(2,1)S(1)}, bf16[8,512]{1,0:T(8,128)(2,1)S(1)}, u32[]{:S(2)}, u32[]{:S(2)}) collective-permute-start(bf16[8,512]{1,0:T(8,128)(2,1)S(1)} %get-tuple-element.34), channel_id=1, source_target_pairs={{0,1},{1,0},{2,3},{3,2},{4,5},{5,4},{6,7},{7,6},{8,9},{9,8},{10,11... | collective-permute-start | bytes 24584 | tf_op jit(solution)/shard_map/ppermute | solution.py:247
  8.5 0.1 collective-permute-start.11
  8.6 0.9 %collective-permute-done.refs_1_ = bf16[8,512]{1,0:T(8,128)(2,1)S(1)} collective-permute-done((bf16[8,512]{1,0:T(8,128)(2,1)S(1)}, bf16[8,512]{1,0:T(8,128)(2,1)S(1)}, u32[]{:S(2)}, u32[]{:S(2)}) %collective-permute-start) | collective-permute-done | bytes 8224 | tf_op jit(solution)/shard_map/ppermute | solution.py:247
  9.5 2.9 %collective-permute-done.1.refs_2_ = bf16[8,512]{1,0:T(8,128)(2,1)S(1)} collective-permute-done((bf16[8,512]{1,0:T(8,128)(2,1)S(1)}, bf16[8,512]{1,0:T(8,128)(2,1)S(1)}, u32[]{:S(2)}, u32[]{:S(2)}) %collective-permute-start.1) | collective-permute-done | bytes 8224 | tf_op jit(solution)/shard_map/ppermute | solution.py:247
  12.4 0.0 collective-permute-start.12
  12.5 0.5 project.1
  12.9 1.5 %collective-permute-start.4 = (bf16[8,2048]{1,0:T(8,128)(2,1)S(1)}, bf16[8,2048]{1,0:T(8,128)(2,1)S(1)}, u32[]{:S(2)}, u32[]{:S(2)}) collective-permute-start(bf16[8,2048]{1,0:T(8,128)(2,1)S(1)} %get-tuple-element.41), channel_id=1, source_target_pairs={{0,3},{1,2},{2,1},{3,0},{4,7},{5,6},{6,5},{7,4},{8,11},{9,10},{10,... | collective-permute-start | bytes 98312 | tf_op jit(solution)/shard_map/ppermute | solution.py:247
  14.4 0.6 %collective-permute-start.5 = (bf16[8,2048]{1,0:T(8,128)(2,1)S(1)}, bf16[8,2048]{1,0:T(8,128)(2,1)S(1)}, u32[]{:S(2)}, u32[]{:S(2)}) collective-permute-start(bf16[8,2048]{1,0:T(8,128)(2,1)S(1)} %get-tuple-element.42), channel_id=1, source_target_pairs={{0,2},{1,3},{2,0},{3,1},{4,6},{5,7},{6,4},{7,5},{8,10},{9,11},{10,... | collective-permute-start | bytes 98312 | tf_op jit(solution)/shard_map/ppermute | solution.py:247
  15.0 2.3 %collective-permute-start.6 = (bf16[8,2048]{1,0:T(8,128)(2,1)S(1)}, bf16[8,2048]{1,0:T(8,128)(2,1)S(1)}, u32[]{:S(2)}, u32[]{:S(2)}) collective-permute-start(bf16[8,2048]{1,0:T(8,128)(2,1)S(1)} %get-tuple-element.43), channel_id=1, source_target_pairs={{0,1},{1,0},{2,3},{3,2},{4,5},{5,4},{6,7},{7,6},{8,9},{9,8},{10,11... | collective-permute-start | bytes 98312 | tf_op jit(solution)/shard_map/ppermute | solution.py:247
  17.3 1.4 %collective-permute-done.4.refs_1_ = bf16[8,2048]{1,0:T(8,128)(2,1)S(1)} collective-permute-done((bf16[8,2048]{1,0:T(8,128)(2,1)S(1)}, bf16[8,2048]{1,0:T(8,128)(2,1)S(1)}, u32[]{:S(2)}, u32[]{:S(2)}) %collective-permute-start.4) | collective-permute-done | bytes 32800 | tf_op jit(solution)/shard_map/ppermute | solution.py:247
  18.7 1.0 %collective-permute-done.5.refs_2_ = bf16[8,2048]{1,0:T(8,128)(2,1)S(1)} collective-permute-done((bf16[8,2048]{1,0:T(8,128)(2,1)S(1)}, bf16[8,2048]{1,0:T(8,128)(2,1)S(1)}, u32[]{:S(2)}, u32[]{:S(2)}) %collective-permute-start.5) | collective-permute-done | bytes 32800 | tf_op jit(solution)/shard_map/ppermute | solution.py:247
  19.7 0.2 collective-permute-done.6.refs_3_
  19.9 0.1 norm.1
  20.0 1.6 %collective-permute-start.7 = (bf16[8,2176]{1,0:T(8,128)(2,1)S(1)}, bf16[8,2176]{1,0:T(8,128)(2,1)S(1)}, u32[]{:S(2)}, u32[]{:S(2)}) collective-permute-start(bf16[8,2176]{1,0:T(8,128)(2,1)S(1)} %get-tuple-element.48.refs_0_), channel_id=1, source_target_pairs={{0,8},{4,12},{8,0},{12,4},{1,9},{5,13},{9,1},{13,5},{2,10},{6,14},... | collective-permute-start | bytes 104456 | tf_op jit(solution)/shard_map/ppermute | solution.py:247
  21.6 2.4 %collective-permute-done.7.refs_1_ = bf16[8,2176]{1,0:T(8,128)(2,1)S(1)} collective-permute-done((bf16[8,2176]{1,0:T(8,128)(2,1)S(1)}, bf16[8,2176]{1,0:T(8,128)(2,1)S(1)}, u32[]{:S(2)}, u32[]{:S(2)}) %collective-permute-start.7) | collective-permute-done | bytes 34848 | tf_op jit(solution)/shard_map/ppermute | solution.py:247
  24.1 1.3 %collective-permute-start.10 = (bf16[16,2176]{1,0:T(8,128)(2,1)S(1)}, bf16[16,2176]{1,0:T(8,128)(2,1)S(1)}, u32[]{:S(2)}, u32[]{:S(2)}) collective-permute-start(bf16[16,2176]{1,0:T(8,128)(2,1)S(1)} %join.1.refs_0_), channel_id=1, source_target_pairs={{0,1},{1,0},{2,3},{3,2},{4,5},{5,4},{6,7},{7,6},{8,9},{9,8},{10,11... | collective-permute-start | bytes 208904 | tf_op jit(solution)/shard_map/ppermute | solution.py:254
  25.4 1.4 %collective-permute-start.9 = (bf16[16,2176]{1,0:T(8,128)(2,1)S(1)}, bf16[16,2176]{1,0:T(8,128)(2,1)S(1)}, u32[]{:S(2)}, u32[]{:S(2)}) collective-permute-start(bf16[16,2176]{1,0:T(8,128)(2,1)S(1)} %join.1.refs_0_), channel_id=1, source_target_pairs={{0,2},{1,3},{2,0},{3,1},{4,6},{5,7},{6,4},{7,5},{8,10},{9,11},{10,... | collective-permute-start | bytes 208904 | tf_op jit(solution)/shard_map/ppermute | solution.py:254
  26.8 1.6 %collective-permute-start.8 = (bf16[16,2176]{1,0:T(8,128)(2,1)S(1)}, bf16[16,2176]{1,0:T(8,128)(2,1)S(1)}, u32[]{:S(2)}, u32[]{:S(2)}) collective-permute-start(bf16[16,2176]{1,0:T(8,128)(2,1)S(1)} %join.1.refs_0_), channel_id=1, source_target_pairs={{0,3},{1,2},{2,1},{3,0},{4,7},{5,6},{6,5},{7,4},{8,11},{9,10},{10,... | collective-permute-start | bytes 208904 | tf_op jit(solution)/shard_map/ppermute | solution.py:254
  28.4 2.9 %collective-permute-done.9.refs_2_ = bf16[16,2176]{1,0:T(8,128)(2,1)S(1)} collective-permute-done((bf16[16,2176]{1,0:T(8,128)(2,1)S(1)}, bf16[16,2176]{1,0:T(8,128)(2,1)S(1)}, u32[]{:S(2)}, u32[]{:S(2)}) %collective-permute-start.9) | collective-permute-done | bytes 69664 | tf_op jit(solution)/shard_map/ppermute | solution.py:254
  31.3 1.6 %collective-permute-done.8.refs_1_ = bf16[16,2176]{1,0:T(8,128)(2,1)S(1)} collective-permute-done((bf16[16,2176]{1,0:T(8,128)(2,1)S(1)}, bf16[16,2176]{1,0:T(8,128)(2,1)S(1)}, u32[]{:S(2)}, u32[]{:S(2)}) %collective-permute-start.8) | collective-permute-done | bytes 69664 | tf_op jit(solution)/shard_map/ppermute | solution.py:254
  32.9 3.5 %expert.1 = (f32[16,2048]{1,0:T(8,128)S(1)}, bf16[16,2048]{1,0:T(8,128)(2,1)S(1)}, bf16[16,2048]{1,0:T(8,128)(2,1)S(1)}, bf16[16,2048]{1,0:T(8,128)(2,1)S(1)}) custom-call(bf16[16,2176]{1,0:T(8,128)(2,1)S(1)} %join.1.refs_0_, bf16[16,2176]{1,0:T(8,128)(2,1)S(1)} %collective-permute-done.8.refs_1_, bf16[16,2176]{1,0:T(8,128)(2,1)S(1)} %collective-permute-done.9.refs_2_, ...), custom_call_target="tpu_custom_call" | custom-call | tf_op jit(solution)/shard_map/expert/pallas_call | solution.py:340
  36.4 1.8 %collective-permute-start.13 = (bf16[16,2048]{1,0:T(8,128)(2,1)S(1)}, bf16[16,2048]{1,0:T(8,128)(2,1)S(1)}, u32[]{:S(2)}, u32[]{:S(2)}) collective-permute-start(bf16[16,2048]{1,0:T(8,128)(2,1)S(1)} %get-tuple-element.52), channel_id=1, source_target_pairs={{0,3},{1,2},{2,1},{3,0},{4,7},{5,6},{6,5},{7,4},{8,11},{9,10},{10,... | collective-permute-start | bytes 196616 | tf_op jit(solution)/shard_map/ppermute | solution.py:247
  38.2 2.6 %collective-permute-start.15 = (bf16[16,2048]{1,0:T(8,128)(2,1)S(1)}, bf16[16,2048]{1,0:T(8,128)(2,1)S(1)}, u32[]{:S(2)}, u32[]{:S(2)}) collective-permute-start(bf16[16,2048]{1,0:T(8,128)(2,1)S(1)} %get-tuple-element.54), channel_id=1, source_target_pairs={{0,1},{1,0},{2,3},{3,2},{4,5},{5,4},{6,7},{7,6},{8,9},{9,8},{10,11... | collective-permute-start | bytes 196616 | tf_op jit(solution)/shard_map/ppermute | solution.py:247
  40.9 1.7 %collective-permute-done.13.refs_1_ = bf16[16,2048]{1,0:T(8,128)(2,1)S(1)} collective-permute-done((bf16[16,2048]{1,0:T(8,128)(2,1)S(1)}, bf16[16,2048]{1,0:T(8,128)(2,1)S(1)}, u32[]{:S(2)}, u32[]{:S(2)}) %collective-permute-start.13) | collective-permute-done | bytes 65568 | tf_op jit(solution)/shard_map/ppermute | solution.py:247
  42.6 1.4 %collective-permute-done.14.refs_2_ = bf16[16,2048]{1,0:T(8,128)(2,1)S(1)} collective-permute-done((bf16[16,2048]{1,0:T(8,128)(2,1)S(1)}, bf16[16,2048]{1,0:T(8,128)(2,1)S(1)}, u32[]{:S(2)}, u32[]{:S(2)}) %collective-permute-start.14) | collective-permute-done | bytes 65568 | tf_op jit(solution)/shard_map/ppermute | solution.py:247
  44.0 1.6 %collective-permute-start.16 = (bf16[8,2048]{1,0:T(8,128)(2,1)S(1)}, bf16[8,2048]{1,0:T(8,128)(2,1)S(1)}, u32[]{:S(2)}, u32[]{:S(2)}) collective-permute-start(bf16[8,2048]{1,0:T(8,128)(2,1)S(1)} %get-tuple-element.56), channel_id=1, source_target_pairs={{0,8},{4,12},{8,0},{12,4},{1,9},{5,13},{9,1},{13,5},{2,10},{6,14},... | collective-permute-start | bytes 98312 | tf_op jit(solution)/shard_map/ppermute | solution.py:247
  45.6 2.4 %collective-permute-done.16.refs_2_ = bf16[8,2048]{1,0:T(8,128)(2,1)S(1)} collective-permute-done((bf16[8,2048]{1,0:T(8,128)(2,1)S(1)}, bf16[8,2048]{1,0:T(8,128)(2,1)S(1)}, u32[]{:S(2)}, u32[]{:S(2)}) %collective-permute-start.16) | collective-permute-done | bytes 32800 | tf_op jit(solution)/shard_map/ppermute | solution.py:247
  48.0 0.6 %finish.1 = bf16[8,2048]{1,0:T(8,128)(2,1)} custom-call(f32[8,2048]{1,0:T(8,128)S(1)} %get-tuple-element.47.refs_0_, f32[8,2048]{1,0:T(8,128)S(1)} %get-tuple-element.55.refs_1_, bf16[8,2048]{1,0:T(8,128)(2,1)S(1)} %collective-permute-done.16.refs_2_), custom_call_target="tpu_custom_call" | custom-call | tf_op jit(solution)/shard_map/finish/pallas_call | solution.py:356
  (17 shorter events, 0.1 us)
Async XLA Ops:
  0.0 8.5 %copy-start.1 = (bf16[1,2048,768]{2,1,0:T(8,128)(2,1)S(1)}, bf16[1,2048,768]{2,1,0:T(8,128)(2,1)}, u32[]{:S(2)}) copy-start(bf16[1,2048,768]{2,1,0:T(8,128)(2,1)} %param.26) | copy-start | bytes 9437188
  0.0 12.4 %collective-permute-start.3 = (bf16[1,2048,768]{2,1,0:T(8,128)(2,1)}, bf16[1,2048,768]{2,1,0:T(8,128)(2,1)S(1)}, u32[]{:S(2)}, u32[]{:S(2)}) collective-permute-start(bf16[1,2048,768]{2,1,0:T(8,128)(2,1)} %param.25), channel_id=1, source_target_pairs={{0,4},{4,0},{8,12},{12,8},{1,5},{5,1},{9,13},{13,9},{2,6},{6,2},{1... | collective-permute-start | bytes 9437192 | tf_op jit(solution)/shard_map/ppermute | solution.py:239
  3.3 6.2 %collective-permute-start = (bf16[8,512]{1,0:T(8,128)(2,1)S(1)}, bf16[8,512]{1,0:T(8,128)(2,1)S(1)}, u32[]{:S(2)}, u32[]{:S(2)}) collective-permute-start(bf16[8,512]{1,0:T(8,128)(2,1)S(1)} %get-tuple-element.32), channel_id=1, source_target_pairs={{0,3},{1,2},{2,1},{3,0},{4,7},{5,6},{6,5},{7,4},{8,11},{9,10},{10,... | collective-permute-start | bytes 24584 | tf_op jit(solution)/shard_map/ppermute | solution.py:247
  7.9 4.5 %collective-permute-start.1 = (bf16[8,512]{1,0:T(8,128)(2,1)S(1)}, bf16[8,512]{1,0:T(8,128)(2,1)S(1)}, u32[]{:S(2)}, u32[]{:S(2)}) collective-permute-start(bf16[8,512]{1,0:T(8,128)(2,1)S(1)} %get-tuple-element.33), channel_id=1, source_target_pairs={{0,2},{1,3},{2,0},{3,1},{4,6},{5,7},{6,4},{7,5},{8,10},{9,11},{10,... | collective-permute-start | bytes 24584 | tf_op jit(solution)/shard_map/ppermute | solution.py:247
  7.9 4.5 %collective-permute-start.2 = (bf16[8,512]{1,0:T(8,128)(2,1)S(1)}, bf16[8,512]{1,0:T(8,128)(2,1)S(1)}, u32[]{:S(2)}, u32[]{:S(2)}) collective-permute-start(bf16[8,512]{1,0:T(8,128)(2,1)S(1)} %get-tuple-element.34), channel_id=1, source_target_pairs={{0,1},{1,0},{2,3},{3,2},{4,5},{5,4},{6,7},{7,6},{8,9},{9,8},{10,11... | collective-permute-start | bytes 24584 | tf_op jit(solution)/shard_map/ppermute | solution.py:247
  8.5 19.9 %collective-permute-start.11 = (bf16[1,2048,768]{2,1,0:T(8,128)(2,1)S(1)}, bf16[1,2048,768]{2,1,0:T(8,128)(2,1)S(1)}, u32[]{:S(2)}, u32[]{:S(2)}) collective-permute-start(bf16[1,2048,768]{2,1,0:T(8,128)(2,1)S(1)} %copy-done.1), channel_id=1, source_target_pairs={{0,4},{4,0},{8,12},{12,8},{1,5},{5,1},{9,13},{13,9},{2,6},{6,2},{1... | collective-permute-start | bytes 9437192 | tf_op jit(solution)/shard_map/ppermute | solution.py:239
  12.4 20.5 %collective-permute-start.12 = (bf16[1,768,2048]{2,1,0:T(8,128)(2,1)}, bf16[1,768,2048]{2,1,0:T(8,128)(2,1)S(1)}, u32[]{:S(2)}, u32[]{:S(2)}) collective-permute-start(bf16[1,768,2048]{2,1,0:T(8,128)(2,1)} %param.27), channel_id=1, source_target_pairs={{0,4},{4,0},{8,12},{12,8},{1,5},{5,1},{9,13},{13,9},{2,6},{6,2},{1... | collective-permute-start | bytes 9437192 | tf_op jit(solution)/shard_map/ppermute | solution.py:303
  12.4 20.5 %copy-start.3 = (bf16[1,768,2048]{2,1,0:T(8,128)(2,1)S(1)}, bf16[1,768,2048]{2,1,0:T(8,128)(2,1)}, u32[]{:S(2)}) copy-start(bf16[1,768,2048]{2,1,0:T(8,128)(2,1)} %param.27) | copy-start | bytes 9437188
  12.9 5.8 %collective-permute-start.4 = (bf16[8,2048]{1,0:T(8,128)(2,1)S(1)}, bf16[8,2048]{1,0:T(8,128)(2,1)S(1)}, u32[]{:S(2)}, u32[]{:S(2)}) collective-permute-start(bf16[8,2048]{1,0:T(8,128)(2,1)S(1)} %get-tuple-element.41), channel_id=1, source_target_pairs={{0,3},{1,2},{2,1},{3,0},{4,7},{5,6},{6,5},{7,4},{8,11},{9,10},{10,... | collective-permute-start | bytes 98312 | tf_op jit(solution)/shard_map/ppermute | solution.py:247
  14.4 5.4 %collective-permute-start.5 = (bf16[8,2048]{1,0:T(8,128)(2,1)S(1)}, bf16[8,2048]{1,0:T(8,128)(2,1)S(1)}, u32[]{:S(2)}, u32[]{:S(2)}) collective-permute-start(bf16[8,2048]{1,0:T(8,128)(2,1)S(1)} %get-tuple-element.42), channel_id=1, source_target_pairs={{0,2},{1,3},{2,0},{3,1},{4,6},{5,7},{6,4},{7,5},{8,10},{9,11},{10,... | collective-permute-start | bytes 98312 | tf_op jit(solution)/shard_map/ppermute | solution.py:247
  15.0 4.9 %collective-permute-start.6 = (bf16[8,2048]{1,0:T(8,128)(2,1)S(1)}, bf16[8,2048]{1,0:T(8,128)(2,1)S(1)}, u32[]{:S(2)}, u32[]{:S(2)}) collective-permute-start(bf16[8,2048]{1,0:T(8,128)(2,1)S(1)} %get-tuple-element.43), channel_id=1, source_target_pairs={{0,1},{1,0},{2,3},{3,2},{4,5},{5,4},{6,7},{7,6},{8,9},{9,8},{10,11... | collective-permute-start | bytes 98312 | tf_op jit(solution)/shard_map/ppermute | solution.py:247
  19.9 13.0 %copy-start = (bf16[1,2048,768]{2,1,0:T(8,128)(2,1)S(1)}, bf16[1,2048,768]{2,1,0:T(8,128)(2,1)}, u32[]{:S(2)}) copy-start(bf16[1,2048,768]{2,1,0:T(8,128)(2,1)} %param.25) | copy-start | bytes 9437188
  19.9 13.0 %copy-start.2 = (bf16[1,2048,768]{2,1,0:T(8,128)(2,1)S(1)}, bf16[1,2048,768]{2,1,0:T(8,128)(2,1)}, u32[]{:S(2)}) copy-start(bf16[1,2048,768]{2,1,0:T(8,128)(2,1)} %param.26) | copy-start | bytes 9437188
  20.0 4.0 %collective-permute-start.7 = (bf16[8,2176]{1,0:T(8,128)(2,1)S(1)}, bf16[8,2176]{1,0:T(8,128)(2,1)S(1)}, u32[]{:S(2)}, u32[]{:S(2)}) collective-permute-start(bf16[8,2176]{1,0:T(8,128)(2,1)S(1)} %get-tuple-element.48.refs_0_), channel_id=1, source_target_pairs={{0,8},{4,12},{8,0},{12,4},{1,9},{5,13},{9,1},{13,5},{2,10},{6,14},... | collective-permute-start | bytes 104456 | tf_op jit(solution)/shard_map/ppermute | solution.py:247
  24.1 4.4 %collective-permute-start.10 = (bf16[16,2176]{1,0:T(8,128)(2,1)S(1)}, bf16[16,2176]{1,0:T(8,128)(2,1)S(1)}, u32[]{:S(2)}, u32[]{:S(2)}) collective-permute-start(bf16[16,2176]{1,0:T(8,128)(2,1)S(1)} %join.1.refs_0_), channel_id=1, source_target_pairs={{0,1},{1,0},{2,3},{3,2},{4,5},{5,4},{6,7},{7,6},{8,9},{9,8},{10,11... | collective-permute-start | bytes 208904 | tf_op jit(solution)/shard_map/ppermute | solution.py:254
  25.4 6.0 %collective-permute-start.9 = (bf16[16,2176]{1,0:T(8,128)(2,1)S(1)}, bf16[16,2176]{1,0:T(8,128)(2,1)S(1)}, u32[]{:S(2)}, u32[]{:S(2)}) collective-permute-start(bf16[16,2176]{1,0:T(8,128)(2,1)S(1)} %join.1.refs_0_), channel_id=1, source_target_pairs={{0,2},{1,3},{2,0},{3,1},{4,6},{5,7},{6,4},{7,5},{8,10},{9,11},{10,... | collective-permute-start | bytes 208904 | tf_op jit(solution)/shard_map/ppermute | solution.py:254
  26.8 6.1 %collective-permute-start.8 = (bf16[16,2176]{1,0:T(8,128)(2,1)S(1)}, bf16[16,2176]{1,0:T(8,128)(2,1)S(1)}, u32[]{:S(2)}, u32[]{:S(2)}) collective-permute-start(bf16[16,2176]{1,0:T(8,128)(2,1)S(1)} %join.1.refs_0_), channel_id=1, source_target_pairs={{0,3},{1,2},{2,1},{3,0},{4,7},{5,6},{6,5},{7,4},{8,11},{9,10},{10,... | collective-permute-start | bytes 208904 | tf_op jit(solution)/shard_map/ppermute | solution.py:254
  36.4 6.1 %collective-permute-start.13 = (bf16[16,2048]{1,0:T(8,128)(2,1)S(1)}, bf16[16,2048]{1,0:T(8,128)(2,1)S(1)}, u32[]{:S(2)}, u32[]{:S(2)}) collective-permute-start(bf16[16,2048]{1,0:T(8,128)(2,1)S(1)} %get-tuple-element.52), channel_id=1, source_target_pairs={{0,3},{1,2},{2,1},{3,0},{4,7},{5,6},{6,5},{7,4},{8,11},{9,10},{10,... | collective-permute-start | bytes 196616 | tf_op jit(solution)/shard_map/ppermute | solution.py:247
  38.2 5.7 %collective-permute-start.14 = (bf16[16,2048]{1,0:T(8,128)(2,1)S(1)}, bf16[16,2048]{1,0:T(8,128)(2,1)S(1)}, u32[]{:S(2)}, u32[]{:S(2)}) collective-permute-start(bf16[16,2048]{1,0:T(8,128)(2,1)S(1)} %get-tuple-element.53), channel_id=1, source_target_pairs={{0,2},{1,3},{2,0},{3,1},{4,6},{5,7},{6,4},{7,5},{8,10},{9,11},{10,... | collective-permute-start | bytes 196616 | tf_op jit(solution)/shard_map/ppermute | solution.py:247
  38.2 5.7 %collective-permute-start.15 = (bf16[16,2048]{1,0:T(8,128)(2,1)S(1)}, bf16[16,2048]{1,0:T(8,128)(2,1)S(1)}, u32[]{:S(2)}, u32[]{:S(2)}) collective-permute-start(bf16[16,2048]{1,0:T(8,128)(2,1)S(1)} %get-tuple-element.54), channel_id=1, source_target_pairs={{0,1},{1,0},{2,3},{3,2},{4,5},{5,4},{6,7},{7,6},{8,9},{9,8},{10,11... | collective-permute-start | bytes 196616 | tf_op jit(solution)/shard_map/ppermute | solution.py:247
  44.0 4.0 %collective-permute-start.16 = (bf16[8,2048]{1,0:T(8,128)(2,1)S(1)}, bf16[8,2048]{1,0:T(8,128)(2,1)S(1)}, u32[]{:S(2)}, u32[]{:S(2)}) collective-permute-start(bf16[8,2048]{1,0:T(8,128)(2,1)S(1)} %get-tuple-element.56), channel_id=1, source_target_pairs={{0,8},{4,12},{8,0},{12,4},{1,9},{5,13},{9,1},{13,5},{2,10},{6,14},... | collective-permute-start | bytes 98312 | tf_op jit(solution)/shard_map/ppermute | solution.py:247

commit v5 on v4

--- a/solution.py
+++ b/solution.py
@@ -28,7 +28,6 @@
 
 def attend_kernel(
     experts,
-    steps,
     len_hbm,
     q_hbm,
     nk_hbm,
@@ -38,27 +37,24 @@
     res_hbm,
     ids_hbm,
     gates_hbm,
-    weight_hbm,
     gain_hbm,
     *refs,
 ):
-    out_refs = refs[: len(steps)]
     (
-    res_ref,
-    table_ref,
-    weight_ref,
-    gain_ref,
-    ctx_ref,
-    len_ref,
-    q_ref,
-    nk_ref,
-    nv_ref,
-    k_buf,
-    v_buf,
-    ids_ref,
-    gates_ref,
-    sems,
-    ) = refs[len(steps) :]
+        ctx_ref,
+        res_ref,
+        table_ref,
+        gain_ref,
+        len_ref,
+        q_ref,
+        nk_ref,
+        nv_ref,
+        k_buf,
+        v_buf,
+        ids_ref,
+        gates_ref,
+        sems,
+    ) = refs
     pairs = (
         (k_hbm, k_buf),
         (q_hbm, q_ref),
@@ -69,7 +65,6 @@
         (ids_hbm, ids_ref),
         (gates_hbm, gates_ref),
         (res_hbm, res_ref),
-        (weight_hbm, weight_ref),
         (gain_hbm, gain_ref),
     )
     copies = [pltpu.make_async_copy(a, b, sems.at[i]) for i, (a, b) in enumerate(pairs)]
@@ -94,12 +89,11 @@
         k = new_key[:, g * HEAD_DIM : (g + 1) * HEAD_DIM]
         new_scores.append(jnp.sum(q * k, axis=1, keepdims=True) * scale)
     spread = jnp.concatenate(rows, axis=0).astype(BF16)
-    row = lax.broadcasted_iota(jnp.int32, (streams, streams * frames), 0)
-    col = lax.broadcasted_iota(jnp.int32, (streams, streams * frames), 1)
-    end = jnp.zeros_like(row)
+    row = lax.broadcasted_iota(jnp.int32, (streams, frames), 0)
+    col = lax.broadcasted_iota(jnp.int32, (streams, frames), 1)
+    held = jnp.zeros_like(row)
     for s in range(streams):
-        end = jnp.where(row == s, len_ref[s] + s * frames, end)
-    valid = (col >= row * frames) & (col < end)
+        held = jnp.where(row == s, len_ref[s], held)
     copies[0].wait()
     scores = lax.dot_general(
         spread,
@@ -109,13 +103,20 @@
     )
     probs, new_probs = [], []
     for h in range(heads):
-        old = jnp.where(valid, scores[h * streams : (h + 1) * streams] * scale, -1e30)
+        block = scores[h * streams : (h + 1) * streams]
+        old = block[:, :frames]
+        for s in range(1, streams):
+            old = jnp.where(row == s, block[:, s * frames : (s + 1) * frames], old)
+        old = jnp.where(col < held, old * scale, -1e30)
         new = new_scores[h]
         top = jnp.maximum(jnp.max(old, axis=1, keepdims=True), new)
         old = jnp.exp(old - top)
         new = jnp.exp(new - top)
         total = jnp.sum(old, axis=1, keepdims=True) + new
-        probs.append(old / total)
+        old = old / total
+        probs.append(
+            jnp.concatenate([jnp.where(row == s, old, 0.0) for s in range(streams)], axis=1)
+        )
         new_probs.append((new / total).astype(BF16).astype(F32))
     probs = jnp.concatenate(probs, axis=0).astype(BF16)
     copies[4].wait()
@@ -131,9 +132,6 @@
         part = part + new_probs[h] * new_value[:, c : c + HEAD_DIM]
         at = h * HEAD_DIM
         ctx_ref[at // width, :, at % width : at % width + HEAD_DIM] = part
-    me = lax.axis_index("sub")
-    for step, out_ref in zip(steps, out_refs):
-        out_ref[...] = ctx_ref[jnp.bitwise_xor(me, step)].astype(BF16)
     for copy in copies[6:]:
         copy.wait()
     gates = gates_ref[...]
@@ -148,6 +146,12 @@
     table_ref[...] = jnp.where(lane < experts, high, table - high).astype(BF16)
 
 
+def route_kernel(steps, ctx_ref, _, *refs):
+    me = lax.axis_index("sub")
+    for step, ref in zip(steps, refs):
+        ref[...] = ctx_ref[jnp.bitwise_xor(me, step)].astype(BF16)
+
+
 def project_kernel(count, *refs):
     x = jnp.concatenate([ref[...].astype(F32) for ref in refs[:count]], axis=0).astype(BF16)
     y = jnp.dot(x, refs[count][...], preferred_element_type=F32)
@@ -177,6 +181,9 @@
     full = jnp.concatenate([ref[...].astype(F32) for ref in refs[:count]], axis=0)
     weight_refs, out_refs = refs[count : count + 6], refs[count + 6 :]
     step, width = out_refs[0].shape
+    spare = 128 - full.shape[0]
+    if spare > 0:
+        full = jnp.concatenate([full, jnp.zeros((spare, full.shape[1]), F32)], axis=0)
     rows = full[:, :width].astype(BF16)
     table = full[:, width:]
     lane = lax.broadcasted_iota(jnp.int32, table.shape, 1)
@@ -256,19 +263,17 @@
         ]
         return [block, *reversed(sent)]
 
-    *context, resident, table, out_weight, norm_gain = pl.pallas_call(
-        functools.partial(attend_kernel, experts, steps),
+    context, resident, table, norm_gain = pl.pallas_call(
+        functools.partial(attend_kernel, experts),
         out_shape=(
-            *(shape((streams, width // n_sub), BF16) for _ in steps),
+            shape((n_sub, streams, width // n_sub), F32),
             shape(residual.shape, BF16),
             shape((streams, table_width), BF16),
-            pltpu.VMEM(out_weight.shape, BF16),
             pltpu.VMEM(norm_gain.shape, BF16),
         ),
-        in_specs=[HBM] * 11,
-        out_specs=(VMEM,) * (n_sub + 4),
+        in_specs=[HBM] * 10,
+        out_specs=(VMEM,) * 4,
         scratch_shapes=[
-            pltpu.VMEM((n_sub, streams, width // n_sub), F32),
             pltpu.SMEM(cache_len.shape, jnp.int32),
             pltpu.VMEM(query.shape, BF16),
             pltpu.VMEM(new_key.shape, BF16),
@@ -277,7 +282,7 @@
             pltpu.VMEM(value_cache.shape, BF16),
             pltpu.VMEM(expert_ids.shape, jnp.int32),
             pltpu.VMEM(gate_scores.shape, F32),
-            pltpu.SemaphoreType.DMA((11,)),
+            pltpu.SemaphoreType.DMA((10,)),
         ],
         compiler_params=params(12),
         name="attend",
@@ -294,11 +299,18 @@
                 residual,
                 expert_ids,
                 gate_scores,
-                out_weight,
                 norm_gain,
             )
         )
     )
+    context = pl.pallas_call(
+        functools.partial(route_kernel, steps),
+        out_shape=(shape((streams, width // n_sub), BF16),) * n_sub,
+        in_specs=[VMEM, HBM],
+        out_specs=(VMEM,) * n_sub,
+        compiler_params=params(4),
+        name="route",
+    )(context, in_hbm(expert_gate[0]))
     context, last, twin[0] = lax.optimization_barrier((exchange(context), expert_down, twin[0]))
     twin.append(lax.ppermute(last, "expert", twins))
     partial = pl.pallas_call(
@@ -308,7 +320,7 @@
         out_specs=(VMEM,) * n_sub,
         compiler_params=params(8),
         name="project",
-    )(*context, out_weight, in_hbm(expert_gate[0]))
+    )(*context, in_vmem(out_weight), in_hbm(expert_gate[0]))
 
     hidden, rows = pl.pallas_call(
         functools.partial(norm_kernel, n_sub),

time: 48.7 us -> 48 us (0.986)
  Pallas kernels: 7.56 us -> 6.74 us
    pallas_call x1, Pallas kernels: 3.5 us -> 2.8 us  [body(): pl.pallas_call(functools.partial(expert_kernel, experts, n_sub), out_shap...]
    pallas_call x1 -> x2, Pallas kernels: 2.82 us -> 2.69 us  [the longest x1 2.68 us: body(): pl.pallas_call(functools.partial(attend_kernel, experts), out_shape=(shap...]
where the time goes in v5:
time: 48 us; the launch traced here: 47.8 us
  starting transfers between devices  22.3 us (46%)
  waiting for transfers between devices  18.6 us (39%)
  Pallas kernels  6.74 us (14%)
    ppermute x11, starting transfers between devices, exchange(): lax.ppermute(block, axis, [(i, i ^ step) for i in range(size)])  17.3 us
    ppermute x11, waiting for transfers between devices, exchange(): lax.ppermute(block, axis, [(i, i ^ step) for i in range(size)])  14.2 us
    ppermute x3, waiting for transfers between devices, gather(): lax.ppermute(block, 'sub', [(i, i ^ step) for i in range(n_sub)])  4.46 us
    ppermute x3, starting transfers between devices, gather(): lax.ppermute(block, 'sub', [(i, i ^ step) for i in range(n_sub)])  4.39 us
    pallas_call x1, Pallas kernels, body(): pl.pallas_call(functools.partial(expert_kernel, experts, n_sub), out_shap...  2.8 us
    pallas_call x1, Pallas kernels, body(): pl.pallas_call(functools.partial(attend_kernel, experts), out_shape=(shap...  2.68 us
  transfers between devices with their start and end apart: 17, of which 11 were waited for; matrix products, arithmetic and copies ran while one was open for 0% of the time, Pallas kernels for 7%

profile of v5, /device:TPU:0, one launch (start us, length us, event | category | flops | bytes accessed | tf_op | source)
XLA Modules:
  0.0 47.8 jit_solution(17621946131600534322)
XLA Ops:
  0.0 0.5 collective-permute-start.3
  0.5 2.7 %attend.1 = (f32[4,8,512]{2,1,0:T(8,128)S(1)}, bf16[8,2048]{1,0:T(8,128)(2,1)S(1)}, bf16[8,128]{1,0:T(8,128)(2,1)S(1)}, bf16[2048]{0:T(1024)(128)(2,1)S(1)}) custom-call(s32[8]{0:T(128)} %len_hbm.1, bf16[8,2048]{1,0:T(8,128)(2,1)} %q_hbm.1, bf16[8,512]{1,0:T(8,128)(2,1)} %nk_hbm.1, bf16[8,512]{1,0:T(8,128)(2,1)} %nv_hbm.1, bf16[8,128,512]{2,1,0:T(8,128)(2,1)} %k_hbm.1, ...), custom_call_target="tpu_custom_call" | custom-call | tf_op jit(solution)/shard_map/attend/pallas_call | solution.py:266
  3.2 4.6 %collective-permute-start = (bf16[8,512]{1,0:T(8,128)(2,1)S(1)}, bf16[8,512]{1,0:T(8,128)(2,1)S(1)}, u32[]{:S(2)}, u32[]{:S(2)}) collective-permute-start(bf16[8,512]{1,0:T(8,128)(2,1)S(1)} %get-tuple-element.33), channel_id=1, source_target_pairs={{0,3},{1,2},{2,1},{3,0},{4,7},{5,6},{6,5},{7,4},{8,11},{9,10},{10,... | collective-permute-start | bytes 24584 | tf_op jit(solution)/shard_map/ppermute | solution.py:254
  7.8 0.6 %collective-permute-start.2 = (bf16[8,512]{1,0:T(8,128)(2,1)S(1)}, bf16[8,512]{1,0:T(8,128)(2,1)S(1)}, u32[]{:S(2)}, u32[]{:S(2)}) collective-permute-start(bf16[8,512]{1,0:T(8,128)(2,1)S(1)} %get-tuple-element.35), channel_id=1, source_target_pairs={{0,1},{1,0},{2,3},{3,2},{4,5},{5,4},{6,7},{7,6},{8,9},{9,8},{10,11... | collective-permute-start | bytes 24584 | tf_op jit(solution)/shard_map/ppermute | solution.py:254
  8.4 0.1 collective-permute-start.11
  8.6 0.9 %collective-permute-done.refs_1_ = bf16[8,512]{1,0:T(8,128)(2,1)S(1)} collective-permute-done((bf16[8,512]{1,0:T(8,128)(2,1)S(1)}, bf16[8,512]{1,0:T(8,128)(2,1)S(1)}, u32[]{:S(2)}, u32[]{:S(2)}) %collective-permute-start) | collective-permute-done | bytes 8224 | tf_op jit(solution)/shard_map/ppermute | solution.py:254
  9.5 2.8 %collective-permute-done.1.refs_2_ = bf16[8,512]{1,0:T(8,128)(2,1)S(1)} collective-permute-done((bf16[8,512]{1,0:T(8,128)(2,1)S(1)}, bf16[8,512]{1,0:T(8,128)(2,1)S(1)}, u32[]{:S(2)}, u32[]{:S(2)}) %collective-permute-start.1) | collective-permute-done | bytes 8224 | tf_op jit(solution)/shard_map/ppermute | solution.py:254
  12.3 0.0 collective-permute-done.2.refs_3_
  12.3 0.0 collective-permute-start.12
  12.4 0.5 project.1
  12.8 1.5 %collective-permute-start.4 = (bf16[8,2048]{1,0:T(8,128)(2,1)S(1)}, bf16[8,2048]{1,0:T(8,128)(2,1)S(1)}, u32[]{:S(2)}, u32[]{:S(2)}) collective-permute-start(bf16[8,2048]{1,0:T(8,128)(2,1)S(1)} %get-tuple-element.41), channel_id=1, source_target_pairs={{0,3},{1,2},{2,1},{3,0},{4,7},{5,6},{6,5},{7,4},{8,11},{9,10},{10,... | collective-permute-start | bytes 98312 | tf_op jit(solution)/shard_map/ppermute | solution.py:254
  14.3 0.6 %collective-permute-start.5 = (bf16[8,2048]{1,0:T(8,128)(2,1)S(1)}, bf16[8,2048]{1,0:T(8,128)(2,1)S(1)}, u32[]{:S(2)}, u32[]{:S(2)}) collective-permute-start(bf16[8,2048]{1,0:T(8,128)(2,1)S(1)} %get-tuple-element.42), channel_id=1, source_target_pairs={{0,2},{1,3},{2,0},{3,1},{4,6},{5,7},{6,4},{7,5},{8,10},{9,11},{10,... | collective-permute-start | bytes 98312 | tf_op jit(solution)/shard_map/ppermute | solution.py:254
  14.9 2.3 %collective-permute-start.6 = (bf16[8,2048]{1,0:T(8,128)(2,1)S(1)}, bf16[8,2048]{1,0:T(8,128)(2,1)S(1)}, u32[]{:S(2)}, u32[]{:S(2)}) collective-permute-start(bf16[8,2048]{1,0:T(8,128)(2,1)S(1)} %get-tuple-element.43), channel_id=1, source_target_pairs={{0,1},{1,0},{2,3},{3,2},{4,5},{5,4},{6,7},{7,6},{8,9},{9,8},{10,11... | collective-permute-start | bytes 98312 | tf_op jit(solution)/shard_map/ppermute | solution.py:254
  17.2 1.4 %collective-permute-done.4.refs_1_ = bf16[8,2048]{1,0:T(8,128)(2,1)S(1)} collective-permute-done((bf16[8,2048]{1,0:T(8,128)(2,1)S(1)}, bf16[8,2048]{1,0:T(8,128)(2,1)S(1)}, u32[]{:S(2)}, u32[]{:S(2)}) %collective-permute-start.4) | collective-permute-done | bytes 32800 | tf_op jit(solution)/shard_map/ppermute | solution.py:254
  18.6 1.0 %collective-permute-done.5.refs_2_ = bf16[8,2048]{1,0:T(8,128)(2,1)S(1)} collective-permute-done((bf16[8,2048]{1,0:T(8,128)(2,1)S(1)}, bf16[8,2048]{1,0:T(8,128)(2,1)S(1)}, u32[]{:S(2)}, u32[]{:S(2)}) %collective-permute-start.5) | collective-permute-done | bytes 32800 | tf_op jit(solution)/shard_map/ppermute | solution.py:254
  19.6 0.2 collective-permute-done.6.refs_3_
  19.8 0.1 norm.1
  19.9 1.6 %collective-permute-start.7 = (bf16[8,2176]{1,0:T(8,128)(2,1)S(1)}, bf16[8,2176]{1,0:T(8,128)(2,1)S(1)}, u32[]{:S(2)}, u32[]{:S(2)}) collective-permute-start(bf16[8,2176]{1,0:T(8,128)(2,1)S(1)} %get-tuple-element.48.refs_0_), channel_id=1, source_target_pairs={{0,8},{4,12},{8,0},{12,4},{1,9},{5,13},{9,1},{13,5},{2,10},{6,14},... | collective-permute-start | bytes 104456 | tf_op jit(solution)/shard_map/ppermute | solution.py:254
  21.6 2.4 %collective-permute-done.7.refs_1_ = bf16[8,2176]{1,0:T(8,128)(2,1)S(1)} collective-permute-done((bf16[8,2176]{1,0:T(8,128)(2,1)S(1)}, bf16[8,2176]{1,0:T(8,128)(2,1)S(1)}, u32[]{:S(2)}, u32[]{:S(2)}) %collective-permute-start.7) | collective-permute-done | bytes 34848 | tf_op jit(solution)/shard_map/ppermute | solution.py:254
  23.9 1.3 %collective-permute-start.10 = (bf16[16,2176]{1,0:T(8,128)(2,1)S(1)}, bf16[16,2176]{1,0:T(8,128)(2,1)S(1)}, u32[]{:S(2)}, u32[]{:S(2)}) collective-permute-start(bf16[16,2176]{1,0:T(8,128)(2,1)S(1)} %join.1.refs_0_), channel_id=1, source_target_pairs={{0,1},{1,0},{2,3},{3,2},{4,5},{5,4},{6,7},{7,6},{8,9},{9,8},{10,11... | collective-permute-start | bytes 208904 | tf_op jit(solution)/shard_map/ppermute | solution.py:261
  25.3 1.4 %collective-permute-start.9 = (bf16[16,2176]{1,0:T(8,128)(2,1)S(1)}, bf16[16,2176]{1,0:T(8,128)(2,1)S(1)}, u32[]{:S(2)}, u32[]{:S(2)}) collective-permute-start(bf16[16,2176]{1,0:T(8,128)(2,1)S(1)} %join.1.refs_0_), channel_id=1, source_target_pairs={{0,2},{1,3},{2,0},{3,1},{4,6},{5,7},{6,4},{7,5},{8,10},{9,11},{10,... | collective-permute-start | bytes 208904 | tf_op jit(solution)/shard_map/ppermute | solution.py:261
  26.7 1.6 %collective-permute-start.8 = (bf16[16,2176]{1,0:T(8,128)(2,1)S(1)}, bf16[16,2176]{1,0:T(8,128)(2,1)S(1)}, u32[]{:S(2)}, u32[]{:S(2)}) collective-permute-start(bf16[16,2176]{1,0:T(8,128)(2,1)S(1)} %join.1.refs_0_), channel_id=1, source_target_pairs={{0,3},{1,2},{2,1},{3,0},{4,7},{5,6},{6,5},{7,4},{8,11},{9,10},{10,... | collective-permute-start | bytes 208904 | tf_op jit(solution)/shard_map/ppermute | solution.py:261
  28.3 2.9 %collective-permute-done.9.refs_2_ = bf16[16,2176]{1,0:T(8,128)(2,1)S(1)} collective-permute-done((bf16[16,2176]{1,0:T(8,128)(2,1)S(1)}, bf16[16,2176]{1,0:T(8,128)(2,1)S(1)}, u32[]{:S(2)}, u32[]{:S(2)}) %collective-permute-start.9) | collective-permute-done | bytes 69664 | tf_op jit(solution)/shard_map/ppermute | solution.py:261
  31.2 1.6 %collective-permute-done.8.refs_1_ = bf16[16,2176]{1,0:T(8,128)(2,1)S(1)} collective-permute-done((bf16[16,2176]{1,0:T(8,128)(2,1)S(1)}, bf16[16,2176]{1,0:T(8,128)(2,1)S(1)}, u32[]{:S(2)}, u32[]{:S(2)}) %collective-permute-start.8) | collective-permute-done | bytes 69664 | tf_op jit(solution)/shard_map/ppermute | solution.py:261
  32.8 2.8 %expert.1 = (f32[16,2048]{1,0:T(8,128)S(1)}, bf16[16,2048]{1,0:T(8,128)(2,1)S(1)}, bf16[16,2048]{1,0:T(8,128)(2,1)S(1)}, bf16[16,2048]{1,0:T(8,128)(2,1)S(1)}) custom-call(bf16[16,2176]{1,0:T(8,128)(2,1)S(1)} %join.1.refs_0_, bf16[16,2176]{1,0:T(8,128)(2,1)S(1)} %collective-permute-done.8.refs_1_, bf16[16,2176]{1,0:T(8,128)(2,1)S(1)} %collective-permute-done.9.refs_2_, ...), custom_call_target="tpu_custom_call" | custom-call | tf_op jit(solution)/shard_map/expert/pallas_call | solution.py:352
  35.6 1.8 %collective-permute-start.13 = (bf16[16,2048]{1,0:T(8,128)(2,1)S(1)}, bf16[16,2048]{1,0:T(8,128)(2,1)S(1)}, u32[]{:S(2)}, u32[]{:S(2)}) collective-permute-start(bf16[16,2048]{1,0:T(8,128)(2,1)S(1)} %get-tuple-element.52), channel_id=1, source_target_pairs={{0,3},{1,2},{2,1},{3,0},{4,7},{5,6},{6,5},{7,4},{8,11},{9,10},{10,... | collective-permute-start | bytes 196616 | tf_op jit(solution)/shard_map/ppermute | solution.py:254
  37.5 2.6 %collective-permute-start.15 = (bf16[16,2048]{1,0:T(8,128)(2,1)S(1)}, bf16[16,2048]{1,0:T(8,128)(2,1)S(1)}, u32[]{:S(2)}, u32[]{:S(2)}) collective-permute-start(bf16[16,2048]{1,0:T(8,128)(2,1)S(1)} %get-tuple-element.54), channel_id=1, source_target_pairs={{0,1},{1,0},{2,3},{3,2},{4,5},{5,4},{6,7},{7,6},{8,9},{9,8},{10,11... | collective-permute-start | bytes 196616 | tf_op jit(solution)/shard_map/ppermute | solution.py:254
  40.1 1.7 %collective-permute-done.13.refs_1_ = bf16[16,2048]{1,0:T(8,128)(2,1)S(1)} collective-permute-done((bf16[16,2048]{1,0:T(8,128)(2,1)S(1)}, bf16[16,2048]{1,0:T(8,128)(2,1)S(1)}, u32[]{:S(2)}, u32[]{:S(2)}) %collective-permute-start.13) | collective-permute-done | bytes 65568 | tf_op jit(solution)/shard_map/ppermute | solution.py:254
  41.8 1.4 %collective-permute-done.14.refs_2_ = bf16[16,2048]{1,0:T(8,128)(2,1)S(1)} collective-permute-done((bf16[16,2048]{1,0:T(8,128)(2,1)S(1)}, bf16[16,2048]{1,0:T(8,128)(2,1)S(1)}, u32[]{:S(2)}, u32[]{:S(2)}) %collective-permute-start.14) | collective-permute-done | bytes 65568 | tf_op jit(solution)/shard_map/ppermute | solution.py:254
  43.2 1.6 %collective-permute-start.16 = (bf16[8,2048]{1,0:T(8,128)(2,1)S(1)}, bf16[8,2048]{1,0:T(8,128)(2,1)S(1)}, u32[]{:S(2)}, u32[]{:S(2)}) collective-permute-start(bf16[8,2048]{1,0:T(8,128)(2,1)S(1)} %get-tuple-element.56), channel_id=1, source_target_pairs={{0,8},{4,12},{8,0},{12,4},{1,9},{5,13},{9,1},{13,5},{2,10},{6,14},... | collective-permute-start | bytes 98312 | tf_op jit(solution)/shard_map/ppermute | solution.py:254
  44.8 2.4 %collective-permute-done.16.refs_2_ = bf16[8,2048]{1,0:T(8,128)(2,1)S(1)} collective-permute-done((bf16[8,2048]{1,0:T(8,128)(2,1)S(1)}, bf16[8,2048]{1,0:T(8,128)(2,1)S(1)}, u32[]{:S(2)}, u32[]{:S(2)}) %collective-permute-start.16) | collective-permute-done | bytes 32800 | tf_op jit(solution)/shard_map/ppermute | solution.py:254
  47.2 0.6 %finish.1 = bf16[8,2048]{1,0:T(8,128)(2,1)} custom-call(f32[8,2048]{1,0:T(8,128)S(1)} %get-tuple-element.47.refs_0_, f32[8,2048]{1,0:T(8,128)S(1)} %get-tuple-element.55.refs_1_, bf16[8,2048]{1,0:T(8,128)(2,1)S(1)} %collective-permute-done.16.refs_2_), custom_call_target="tpu_custom_call" | custom-call | tf_op jit(solution)/shard_map/finish/pallas_call | solution.py:368
  (20 shorter events, 0.1 us)
Async XLA Ops:
  0.0 8.4 %copy-start.1 = (bf16[1,2048,768]{2,1,0:T(8,128)(2,1)S(1)}, bf16[1,2048,768]{2,1,0:T(8,128)(2,1)}, u32[]{:S(2)}) copy-start(bf16[1,2048,768]{2,1,0:T(8,128)(2,1)} %param.26) | copy-start | bytes 9437188
  0.0 12.3 %copy-start.4 = (bf16[512,2048]{1,0:T(8,128)(2,1)S(1)}, bf16[512,2048]{1,0:T(8,128)(2,1)}, u32[]{:S(2)}) copy-start(bf16[512,2048]{1,0:T(8,128)(2,1)} %refs_4_.1) | copy-start | bytes 6291460
  0.0 12.3 %collective-permute-start.3 = (bf16[1,2048,768]{2,1,0:T(8,128)(2,1)}, bf16[1,2048,768]{2,1,0:T(8,128)(2,1)S(1)}, u32[]{:S(2)}, u32[]{:S(2)}) collective-permute-start(bf16[1,2048,768]{2,1,0:T(8,128)(2,1)} %param.25), channel_id=1, source_target_pairs={{0,4},{4,0},{8,12},{12,8},{1,5},{5,1},{9,13},{13,9},{2,6},{6,2},{1... | collective-permute-start | bytes 9437192 | tf_op jit(solution)/shard_map/ppermute | solution.py:246
  3.2 6.3 %collective-permute-start = (bf16[8,512]{1,0:T(8,128)(2,1)S(1)}, bf16[8,512]{1,0:T(8,128)(2,1)S(1)}, u32[]{:S(2)}, u32[]{:S(2)}) collective-permute-start(bf16[8,512]{1,0:T(8,128)(2,1)S(1)} %get-tuple-element.33), channel_id=1, source_target_pairs={{0,3},{1,2},{2,1},{3,0},{4,7},{5,6},{6,5},{7,4},{8,11},{9,10},{10,... | collective-permute-start | bytes 24584 | tf_op jit(solution)/shard_map/ppermute | solution.py:254
  7.8 4.5 %collective-permute-start.1 = (bf16[8,512]{1,0:T(8,128)(2,1)S(1)}, bf16[8,512]{1,0:T(8,128)(2,1)S(1)}, u32[]{:S(2)}, u32[]{:S(2)}) collective-permute-start(bf16[8,512]{1,0:T(8,128)(2,1)S(1)} %get-tuple-element.34), channel_id=1, source_target_pairs={{0,2},{1,3},{2,0},{3,1},{4,6},{5,7},{6,4},{7,5},{8,10},{9,11},{10,... | collective-permute-start | bytes 24584 | tf_op jit(solution)/shard_map/ppermute | solution.py:254
  7.8 4.5 %collective-permute-start.2 = (bf16[8,512]{1,0:T(8,128)(2,1)S(1)}, bf16[8,512]{1,0:T(8,128)(2,1)S(1)}, u32[]{:S(2)}, u32[]{:S(2)}) collective-permute-start(bf16[8,512]{1,0:T(8,128)(2,1)S(1)} %get-tuple-element.35), channel_id=1, source_target_pairs={{0,1},{1,0},{2,3},{3,2},{4,5},{5,4},{6,7},{7,6},{8,9},{9,8},{10,11... | collective-permute-start | bytes 24584 | tf_op jit(solution)/shard_map/ppermute | solution.py:254
  8.4 19.9 %collective-permute-start.11 = (bf16[1,2048,768]{2,1,0:T(8,128)(2,1)S(1)}, bf16[1,2048,768]{2,1,0:T(8,128)(2,1)S(1)}, u32[]{:S(2)}, u32[]{:S(2)}) collective-permute-start(bf16[1,2048,768]{2,1,0:T(8,128)(2,1)S(1)} %copy-done.1), channel_id=1, source_target_pairs={{0,4},{4,0},{8,12},{12,8},{1,5},{5,1},{9,13},{13,9},{2,6},{6,2},{1... | collective-permute-start | bytes 9437192 | tf_op jit(solution)/shard_map/ppermute | solution.py:246
  12.3 20.5 %collective-permute-start.12 = (bf16[1,768,2048]{2,1,0:T(8,128)(2,1)}, bf16[1,768,2048]{2,1,0:T(8,128)(2,1)S(1)}, u32[]{:S(2)}, u32[]{:S(2)}) collective-permute-start(bf16[1,768,2048]{2,1,0:T(8,128)(2,1)} %param.27), channel_id=1, source_target_pairs={{0,4},{4,0},{8,12},{12,8},{1,5},{5,1},{9,13},{13,9},{2,6},{6,2},{1... | collective-permute-start | bytes 9437192 | tf_op jit(solution)/shard_map/ppermute | solution.py:315
  12.3 20.5 %copy-start.3 = (bf16[1,768,2048]{2,1,0:T(8,128)(2,1)S(1)}, bf16[1,768,2048]{2,1,0:T(8,128)(2,1)}, u32[]{:S(2)}) copy-start(bf16[1,768,2048]{2,1,0:T(8,128)(2,1)} %param.27) | copy-start | bytes 9437188
  12.8 5.8 %collective-permute-start.4 = (bf16[8,2048]{1,0:T(8,128)(2,1)S(1)}, bf16[8,2048]{1,0:T(8,128)(2,1)S(1)}, u32[]{:S(2)}, u32[]{:S(2)}) collective-permute-start(bf16[8,2048]{1,0:T(8,128)(2,1)S(1)} %get-tuple-element.41), channel_id=1, source_target_pairs={{0,3},{1,2},{2,1},{3,0},{4,7},{5,6},{6,5},{7,4},{8,11},{9,10},{10,... | collective-permute-start | bytes 98312 | tf_op jit(solution)/shard_map/ppermute | solution.py:254
  14.3 5.3 %collective-permute-start.5 = (bf16[8,2048]{1,0:T(8,128)(2,1)S(1)}, bf16[8,2048]{1,0:T(8,128)(2,1)S(1)}, u32[]{:S(2)}, u32[]{:S(2)}) collective-permute-start(bf16[8,2048]{1,0:T(8,128)(2,1)S(1)} %get-tuple-element.42), channel_id=1, source_target_pairs={{0,2},{1,3},{2,0},{3,1},{4,6},{5,7},{6,4},{7,5},{8,10},{9,11},{10,... | collective-permute-start | bytes 98312 | tf_op jit(solution)/shard_map/ppermute | solution.py:254
  14.9 4.9 %collective-permute-start.6 = (bf16[8,2048]{1,0:T(8,128)(2,1)S(1)}, bf16[8,2048]{1,0:T(8,128)(2,1)S(1)}, u32[]{:S(2)}, u32[]{:S(2)}) collective-permute-start(bf16[8,2048]{1,0:T(8,128)(2,1)S(1)} %get-tuple-element.43), channel_id=1, source_target_pairs={{0,1},{1,0},{2,3},{3,2},{4,5},{5,4},{6,7},{7,6},{8,9},{9,8},{10,11... | collective-permute-start | bytes 98312 | tf_op jit(solution)/shard_map/ppermute | solution.py:254
  19.8 13.0 %copy-start = (bf16[1,2048,768]{2,1,0:T(8,128)(2,1)S(1)}, bf16[1,2048,768]{2,1,0:T(8,128)(2,1)}, u32[]{:S(2)}) copy-start(bf16[1,2048,768]{2,1,0:T(8,128)(2,1)} %param.25) | copy-start | bytes 9437188
  19.8 13.0 %copy-start.2 = (bf16[1,2048,768]{2,1,0:T(8,128)(2,1)S(1)}, bf16[1,2048,768]{2,1,0:T(8,128)(2,1)}, u32[]{:S(2)}) copy-start(bf16[1,2048,768]{2,1,0:T(8,128)(2,1)} %param.26) | copy-start | bytes 9437188
  19.9 4.0 %collective-permute-start.7 = (bf16[8,2176]{1,0:T(8,128)(2,1)S(1)}, bf16[8,2176]{1,0:T(8,128)(2,1)S(1)}, u32[]{:S(2)}, u32[]{:S(2)}) collective-permute-start(bf16[8,2176]{1,0:T(8,128)(2,1)S(1)} %get-tuple-element.48.refs_0_), channel_id=1, source_target_pairs={{0,8},{4,12},{8,0},{12,4},{1,9},{5,13},{9,1},{13,5},{2,10},{6,14},... | collective-permute-start | bytes 104456 | tf_op jit(solution)/shard_map/ppermute | solution.py:254
  23.9 4.4 %collective-permute-start.10 = (bf16[16,2176]{1,0:T(8,128)(2,1)S(1)}, bf16[16,2176]{1,0:T(8,128)(2,1)S(1)}, u32[]{:S(2)}, u32[]{:S(2)}) collective-permute-start(bf16[16,2176]{1,0:T(8,128)(2,1)S(1)} %join.1.refs_0_), channel_id=1, source_target_pairs={{0,1},{1,0},{2,3},{3,2},{4,5},{5,4},{6,7},{7,6},{8,9},{9,8},{10,11... | collective-permute-start | bytes 208904 | tf_op jit(solution)/shard_map/ppermute | solution.py:261
  25.3 6.0 %collective-permute-start.9 = (bf16[16,2176]{1,0:T(8,128)(2,1)S(1)}, bf16[16,2176]{1,0:T(8,128)(2,1)S(1)}, u32[]{:S(2)}, u32[]{:S(2)}) collective-permute-start(bf16[16,2176]{1,0:T(8,128)(2,1)S(1)} %join.1.refs_0_), channel_id=1, source_target_pairs={{0,2},{1,3},{2,0},{3,1},{4,6},{5,7},{6,4},{7,5},{8,10},{9,11},{10,... | collective-permute-start | bytes 208904 | tf_op jit(solution)/shard_map/ppermute | solution.py:261
  26.7 6.1 %collective-permute-start.8 = (bf16[16,2176]{1,0:T(8,128)(2,1)S(1)}, bf16[16,2176]{1,0:T(8,128)(2,1)S(1)}, u32[]{:S(2)}, u32[]{:S(2)}) collective-permute-start(bf16[16,2176]{1,0:T(8,128)(2,1)S(1)} %join.1.refs_0_), channel_id=1, source_target_pairs={{0,3},{1,2},{2,1},{3,0},{4,7},{5,6},{6,5},{7,4},{8,11},{9,10},{10,... | collective-permute-start | bytes 208904 | tf_op jit(solution)/shard_map/ppermute | solution.py:261
  35.6 6.1 %collective-permute-start.13 = (bf16[16,2048]{1,0:T(8,128)(2,1)S(1)}, bf16[16,2048]{1,0:T(8,128)(2,1)S(1)}, u32[]{:S(2)}, u32[]{:S(2)}) collective-permute-start(bf16[16,2048]{1,0:T(8,128)(2,1)S(1)} %get-tuple-element.52), channel_id=1, source_target_pairs={{0,3},{1,2},{2,1},{3,0},{4,7},{5,6},{6,5},{7,4},{8,11},{9,10},{10,... | collective-permute-start | bytes 196616 | tf_op jit(solution)/shard_map/ppermute | solution.py:254
  37.5 5.7 %collective-permute-start.14 = (bf16[16,2048]{1,0:T(8,128)(2,1)S(1)}, bf16[16,2048]{1,0:T(8,128)(2,1)S(1)}, u32[]{:S(2)}, u32[]{:S(2)}) collective-permute-start(bf16[16,2048]{1,0:T(8,128)(2,1)S(1)} %get-tuple-element.53), channel_id=1, source_target_pairs={{0,2},{1,3},{2,0},{3,1},{4,6},{5,7},{6,4},{7,5},{8,10},{9,11},{10,... | collective-permute-start | bytes 196616 | tf_op jit(solution)/shard_map/ppermute | solution.py:254
  37.5 5.7 %collective-permute-start.15 = (bf16[16,2048]{1,0:T(8,128)(2,1)S(1)}, bf16[16,2048]{1,0:T(8,128)(2,1)S(1)}, u32[]{:S(2)}, u32[]{:S(2)}) collective-permute-start(bf16[16,2048]{1,0:T(8,128)(2,1)S(1)} %get-tuple-element.54), channel_id=1, source_target_pairs={{0,1},{1,0},{2,3},{3,2},{4,5},{5,4},{6,7},{7,6},{8,9},{9,8},{10,11... | collective-permute-start | bytes 196616 | tf_op jit(solution)/shard_map/ppermute | solution.py:254
  43.2 4.0 %collective-permute-start.16 = (bf16[8,2048]{1,0:T(8,128)(2,1)S(1)}, bf16[8,2048]{1,0:T(8,128)(2,1)S(1)}, u32[]{:S(2)}, u32[]{:S(2)}) collective-permute-start(bf16[8,2048]{1,0:T(8,128)(2,1)S(1)} %get-tuple-element.56), channel_id=1, source_target_pairs={{0,8},{4,12},{8,0},{12,4},{1,9},{5,13},{9,1},{13,5},{2,10},{6,14},... | collective-permute-start | bytes 98312 | tf_op jit(solution)/shard_map/ppermute | solution.py:254

commit v6 on v5

--- a/solution.py
+++ b/solution.py
@@ -188,17 +188,16 @@
     table = full[:, width:]
     lane = lax.broadcasted_iota(jnp.int32, table.shape, 1)
     major, minor, n_sub = lax.axis_index("expert"), lax.axis_index("sub"), lax.axis_size("sub")
-    total = None
+    acts, weights = [], []
     for i, place in enumerate((major, jnp.bitwise_xor(major, 1))):
-        gate_ref, up_ref, down_ref = weight_refs[3 * i : 3 * i + 3]
         expert = place * n_sub + minor
         chosen = (lane == expert) | (lane == expert + experts)
-        weight = jnp.sum(jnp.where(chosen, table, 0.0), axis=1, keepdims=True)
-        gate = jnp.dot(rows, gate_ref[...], preferred_element_type=F32)
-        up = jnp.dot(rows, up_ref[...], preferred_element_type=F32)
-        act = (gate / (1.0 + jnp.exp(-gate)) * up).astype(BF16)
-        y = jnp.dot(act, down_ref[...], preferred_element_type=F32) * weight
-        total = y if total is None else total + y
+        weights.append(jnp.sum(jnp.where(chosen, table, 0.0), axis=1, keepdims=True))
+        gate = jnp.dot(rows, weight_refs[3 * i][...], preferred_element_type=F32)
+        up = jnp.dot(rows, weight_refs[3 * i + 1][...], preferred_element_type=F32)
+        acts.append((gate / (1.0 + jnp.exp(-gate)) * up).astype(BF16))
+    total = weights[0] * jnp.dot(acts[0], weight_refs[2][...], preferred_element_type=F32)
+    total = total + weights[1] * jnp.dot(acts[1], weight_refs[5][...], preferred_element_type=F32)
     for i, ref in enumerate(out_refs):
         ref[...] = total[i * step : (i + 1) * step].astype(ref.dtype)
 

time: 48 us -> 47.8 us (level)
  no operation moved by 1% of the time
where the time goes in v6:
time: 47.8 us; the launch traced here: 47.7 us
  starting transfers between devices  22.3 us (47%)
  waiting for transfers between devices  18.6 us (39%)
  Pallas kernels  6.58 us (14%)
    ppermute x11, starting transfers between devices, exchange(): lax.ppermute(block, axis, [(i, i ^ step) for i in range(size)])  17.3 us
    ppermute x11, waiting for transfers between devices, exchange(): lax.ppermute(block, axis, [(i, i ^ step) for i in range(size)])  14.2 us
    ppermute x3, waiting for transfers between devices, gather(): lax.ppermute(block, 'sub', [(i, i ^ step) for i in range(n_sub)])  4.46 us
    ppermute x3, starting transfers between devices, gather(): lax.ppermute(block, 'sub', [(i, i ^ step) for i in range(n_sub)])  4.39 us
    pallas_call x1, Pallas kernels, body(): pl.pallas_call(functools.partial(attend_kernel, experts), out_shape=(shap...  2.68 us
    pallas_call x1, Pallas kernels, body(): pl.pallas_call(functools.partial(expert_kernel, experts, n_sub), out_shap...  2.65 us
  transfers between devices with their start and end apart: 17, of which 11 were waited for; matrix products, arithmetic and copies ran while one was open for 0% of the time, Pallas kernels for 7%

profile of v6, /device:TPU:0, one launch (start us, length us, event | category | flops | bytes accessed | tf_op | source)
XLA Modules:
  0.0 47.7 jit_solution(14263931572915816799)
XLA Ops:
  0.0 0.5 collective-permute-start.3
  0.5 2.7 %attend.1 = (f32[4,8,512]{2,1,0:T(8,128)S(1)}, bf16[8,2048]{1,0:T(8,128)(2,1)S(1)}, bf16[8,128]{1,0:T(8,128)(2,1)S(1)}, bf16[2048]{0:T(1024)(128)(2,1)S(1)}) custom-call(s32[8]{0:T(128)} %len_hbm.1, bf16[8,2048]{1,0:T(8,128)(2,1)} %q_hbm.1, bf16[8,512]{1,0:T(8,128)(2,1)} %nk_hbm.1, bf16[8,512]{1,0:T(8,128)(2,1)} %nv_hbm.1, bf16[8,128,512]{2,1,0:T(8,128)(2,1)} %k_hbm.1, ...), custom_call_target="tpu_custom_call" | custom-call | tf_op jit(solution)/shard_map/attend/pallas_call | solution.py:265
  3.2 4.6 %collective-permute-start = (bf16[8,512]{1,0:T(8,128)(2,1)S(1)}, bf16[8,512]{1,0:T(8,128)(2,1)S(1)}, u32[]{:S(2)}, u32[]{:S(2)}) collective-permute-start(bf16[8,512]{1,0:T(8,128)(2,1)S(1)} %get-tuple-element.33), channel_id=1, source_target_pairs={{0,3},{1,2},{2,1},{3,0},{4,7},{5,6},{6,5},{7,4},{8,11},{9,10},{10,... | collective-permute-start | bytes 24584 | tf_op jit(solution)/shard_map/ppermute | solution.py:253
  7.8 0.6 %collective-permute-start.2 = (bf16[8,512]{1,0:T(8,128)(2,1)S(1)}, bf16[8,512]{1,0:T(8,128)(2,1)S(1)}, u32[]{:S(2)}, u32[]{:S(2)}) collective-permute-start(bf16[8,512]{1,0:T(8,128)(2,1)S(1)} %get-tuple-element.35), channel_id=1, source_target_pairs={{0,1},{1,0},{2,3},{3,2},{4,5},{5,4},{6,7},{7,6},{8,9},{9,8},{10,11... | collective-permute-start | bytes 24584 | tf_op jit(solution)/shard_map/ppermute | solution.py:253
  8.4 0.1 collective-permute-start.11
  8.6 0.9 %collective-permute-done.refs_1_ = bf16[8,512]{1,0:T(8,128)(2,1)S(1)} collective-permute-done((bf16[8,512]{1,0:T(8,128)(2,1)S(1)}, bf16[8,512]{1,0:T(8,128)(2,1)S(1)}, u32[]{:S(2)}, u32[]{:S(2)}) %collective-permute-start) | collective-permute-done | bytes 8224 | tf_op jit(solution)/shard_map/ppermute | solution.py:253
  9.5 2.8 %collective-permute-done.1.refs_2_ = bf16[8,512]{1,0:T(8,128)(2,1)S(1)} collective-permute-done((bf16[8,512]{1,0:T(8,128)(2,1)S(1)}, bf16[8,512]{1,0:T(8,128)(2,1)S(1)}, u32[]{:S(2)}, u32[]{:S(2)}) %collective-permute-start.1) | collective-permute-done | bytes 8224 | tf_op jit(solution)/shard_map/ppermute | solution.py:253
  12.3 0.0 collective-permute-done.2.refs_3_
  12.3 0.0 collective-permute-start.12
  12.4 0.5 project.1
  12.8 1.5 %collective-permute-start.4 = (bf16[8,2048]{1,0:T(8,128)(2,1)S(1)}, bf16[8,2048]{1,0:T(8,128)(2,1)S(1)}, u32[]{:S(2)}, u32[]{:S(2)}) collective-permute-start(bf16[8,2048]{1,0:T(8,128)(2,1)S(1)} %get-tuple-element.41), channel_id=1, source_target_pairs={{0,3},{1,2},{2,1},{3,0},{4,7},{5,6},{6,5},{7,4},{8,11},{9,10},{10,... | collective-permute-start | bytes 98312 | tf_op jit(solution)/shard_map/ppermute | solution.py:253
  14.3 0.6 %collective-permute-start.5 = (bf16[8,2048]{1,0:T(8,128)(2,1)S(1)}, bf16[8,2048]{1,0:T(8,128)(2,1)S(1)}, u32[]{:S(2)}, u32[]{:S(2)}) collective-permute-start(bf16[8,2048]{1,0:T(8,128)(2,1)S(1)} %get-tuple-element.42), channel_id=1, source_target_pairs={{0,2},{1,3},{2,0},{3,1},{4,6},{5,7},{6,4},{7,5},{8,10},{9,11},{10,... | collective-permute-start | bytes 98312 | tf_op jit(solution)/shard_map/ppermute | solution.py:253
  14.9 2.3 %collective-permute-start.6 = (bf16[8,2048]{1,0:T(8,128)(2,1)S(1)}, bf16[8,2048]{1,0:T(8,128)(2,1)S(1)}, u32[]{:S(2)}, u32[]{:S(2)}) collective-permute-start(bf16[8,2048]{1,0:T(8,128)(2,1)S(1)} %get-tuple-element.43), channel_id=1, source_target_pairs={{0,1},{1,0},{2,3},{3,2},{4,5},{5,4},{6,7},{7,6},{8,9},{9,8},{10,11... | collective-permute-start | bytes 98312 | tf_op jit(solution)/shard_map/ppermute | solution.py:253
  17.2 1.4 %collective-permute-done.4.refs_1_ = bf16[8,2048]{1,0:T(8,128)(2,1)S(1)} collective-permute-done((bf16[8,2048]{1,0:T(8,128)(2,1)S(1)}, bf16[8,2048]{1,0:T(8,128)(2,1)S(1)}, u32[]{:S(2)}, u32[]{:S(2)}) %collective-permute-start.4) | collective-permute-done | bytes 32800 | tf_op jit(solution)/shard_map/ppermute | solution.py:253
  18.6 1.0 %collective-permute-done.5.refs_2_ = bf16[8,2048]{1,0:T(8,128)(2,1)S(1)} collective-permute-done((bf16[8,2048]{1,0:T(8,128)(2,1)S(1)}, bf16[8,2048]{1,0:T(8,128)(2,1)S(1)}, u32[]{:S(2)}, u32[]{:S(2)}) %collective-permute-start.5) | collective-permute-done | bytes 32800 | tf_op jit(solution)/shard_map/ppermute | solution.py:253
  19.6 0.2 collective-permute-done.6.refs_3_
  19.8 0.1 norm.1
  19.9 1.6 %collective-permute-start.7 = (bf16[8,2176]{1,0:T(8,128)(2,1)S(1)}, bf16[8,2176]{1,0:T(8,128)(2,1)S(1)}, u32[]{:S(2)}, u32[]{:S(2)}) collective-permute-start(bf16[8,2176]{1,0:T(8,128)(2,1)S(1)} %get-tuple-element.48.refs_0_), channel_id=1, source_target_pairs={{0,8},{4,12},{8,0},{12,4},{1,9},{5,13},{9,1},{13,5},{2,10},{6,14},... | collective-permute-start | bytes 104456 | tf_op jit(solution)/shard_map/ppermute | solution.py:253
  21.6 2.4 %collective-permute-done.7.refs_1_ = bf16[8,2176]{1,0:T(8,128)(2,1)S(1)} collective-permute-done((bf16[8,2176]{1,0:T(8,128)(2,1)S(1)}, bf16[8,2176]{1,0:T(8,128)(2,1)S(1)}, u32[]{:S(2)}, u32[]{:S(2)}) %collective-permute-start.7) | collective-permute-done | bytes 34848 | tf_op jit(solution)/shard_map/ppermute | solution.py:253
  23.9 1.3 %collective-permute-start.10 = (bf16[16,2176]{1,0:T(8,128)(2,1)S(1)}, bf16[16,2176]{1,0:T(8,128)(2,1)S(1)}, u32[]{:S(2)}, u32[]{:S(2)}) collective-permute-start(bf16[16,2176]{1,0:T(8,128)(2,1)S(1)} %join.1.refs_0_), channel_id=1, source_target_pairs={{0,1},{1,0},{2,3},{3,2},{4,5},{5,4},{6,7},{7,6},{8,9},{9,8},{10,11... | collective-permute-start | bytes 208904 | tf_op jit(solution)/shard_map/ppermute | solution.py:260
  25.3 1.4 %collective-permute-start.9 = (bf16[16,2176]{1,0:T(8,128)(2,1)S(1)}, bf16[16,2176]{1,0:T(8,128)(2,1)S(1)}, u32[]{:S(2)}, u32[]{:S(2)}) collective-permute-start(bf16[16,2176]{1,0:T(8,128)(2,1)S(1)} %join.1.refs_0_), channel_id=1, source_target_pairs={{0,2},{1,3},{2,0},{3,1},{4,6},{5,7},{6,4},{7,5},{8,10},{9,11},{10,... | collective-permute-start | bytes 208904 | tf_op jit(solution)/shard_map/ppermute | solution.py:260
  26.7 1.6 %collective-permute-start.8 = (bf16[16,2176]{1,0:T(8,128)(2,1)S(1)}, bf16[16,2176]{1,0:T(8,128)(2,1)S(1)}, u32[]{:S(2)}, u32[]{:S(2)}) collective-permute-start(bf16[16,2176]{1,0:T(8,128)(2,1)S(1)} %join.1.refs_0_), channel_id=1, source_target_pairs={{0,3},{1,2},{2,1},{3,0},{4,7},{5,6},{6,5},{7,4},{8,11},{9,10},{10,... | collective-permute-start | bytes 208904 | tf_op jit(solution)/shard_map/ppermute | solution.py:260
  28.3 2.9 %collective-permute-done.9.refs_2_ = bf16[16,2176]{1,0:T(8,128)(2,1)S(1)} collective-permute-done((bf16[16,2176]{1,0:T(8,128)(2,1)S(1)}, bf16[16,2176]{1,0:T(8,128)(2,1)S(1)}, u32[]{:S(2)}, u32[]{:S(2)}) %collective-permute-start.9) | collective-permute-done | bytes 69664 | tf_op jit(solution)/shard_map/ppermute | solution.py:260
  31.2 1.6 %collective-permute-done.8.refs_1_ = bf16[16,2176]{1,0:T(8,128)(2,1)S(1)} collective-permute-done((bf16[16,2176]{1,0:T(8,128)(2,1)S(1)}, bf16[16,2176]{1,0:T(8,128)(2,1)S(1)}, u32[]{:S(2)}, u32[]{:S(2)}) %collective-permute-start.8) | collective-permute-done | bytes 69664 | tf_op jit(solution)/shard_map/ppermute | solution.py:260
  32.8 2.6 %expert.1 = (f32[16,2048]{1,0:T(8,128)S(1)}, bf16[16,2048]{1,0:T(8,128)(2,1)S(1)}, bf16[16,2048]{1,0:T(8,128)(2,1)S(1)}, bf16[16,2048]{1,0:T(8,128)(2,1)S(1)}) custom-call(bf16[16,2176]{1,0:T(8,128)(2,1)S(1)} %join.1.refs_0_, bf16[16,2176]{1,0:T(8,128)(2,1)S(1)} %collective-permute-done.8.refs_1_, bf16[16,2176]{1,0:T(8,128)(2,1)S(1)} %collective-permute-done.9.refs_2_, ...), custom_call_target="tpu_custom_call" | custom-call | tf_op jit(solution)/shard_map/expert/pallas_call | solution.py:351
  35.5 1.8 %collective-permute-start.13 = (bf16[16,2048]{1,0:T(8,128)(2,1)S(1)}, bf16[16,2048]{1,0:T(8,128)(2,1)S(1)}, u32[]{:S(2)}, u32[]{:S(2)}) collective-permute-start(bf16[16,2048]{1,0:T(8,128)(2,1)S(1)} %get-tuple-element.52), channel_id=1, source_target_pairs={{0,3},{1,2},{2,1},{3,0},{4,7},{5,6},{6,5},{7,4},{8,11},{9,10},{10,... | collective-permute-start | bytes 196616 | tf_op jit(solution)/shard_map/ppermute | solution.py:253
  37.3 2.6 %collective-permute-start.15 = (bf16[16,2048]{1,0:T(8,128)(2,1)S(1)}, bf16[16,2048]{1,0:T(8,128)(2,1)S(1)}, u32[]{:S(2)}, u32[]{:S(2)}) collective-permute-start(bf16[16,2048]{1,0:T(8,128)(2,1)S(1)} %get-tuple-element.54), channel_id=1, source_target_pairs={{0,1},{1,0},{2,3},{3,2},{4,5},{5,4},{6,7},{7,6},{8,9},{9,8},{10,11... | collective-permute-start | bytes 196616 | tf_op jit(solution)/shard_map/ppermute | solution.py:253
  39.9 1.7 %collective-permute-done.13.refs_1_ = bf16[16,2048]{1,0:T(8,128)(2,1)S(1)} collective-permute-done((bf16[16,2048]{1,0:T(8,128)(2,1)S(1)}, bf16[16,2048]{1,0:T(8,128)(2,1)S(1)}, u32[]{:S(2)}, u32[]{:S(2)}) %collective-permute-start.13) | collective-permute-done | bytes 65568 | tf_op jit(solution)/shard_map/ppermute | solution.py:253
  41.6 1.4 %collective-permute-done.14.refs_2_ = bf16[16,2048]{1,0:T(8,128)(2,1)S(1)} collective-permute-done((bf16[16,2048]{1,0:T(8,128)(2,1)S(1)}, bf16[16,2048]{1,0:T(8,128)(2,1)S(1)}, u32[]{:S(2)}, u32[]{:S(2)}) %collective-permute-start.14) | collective-permute-done | bytes 65568 | tf_op jit(solution)/shard_map/ppermute | solution.py:253
  43.0 1.6 %collective-permute-start.16 = (bf16[8,2048]{1,0:T(8,128)(2,1)S(1)}, bf16[8,2048]{1,0:T(8,128)(2,1)S(1)}, u32[]{:S(2)}, u32[]{:S(2)}) collective-permute-start(bf16[8,2048]{1,0:T(8,128)(2,1)S(1)} %get-tuple-element.56), channel_id=1, source_target_pairs={{0,8},{4,12},{8,0},{12,4},{1,9},{5,13},{9,1},{13,5},{2,10},{6,14},... | collective-permute-start | bytes 98312 | tf_op jit(solution)/shard_map/ppermute | solution.py:253
  44.7 2.4 %collective-permute-done.16.refs_2_ = bf16[8,2048]{1,0:T(8,128)(2,1)S(1)} collective-permute-done((bf16[8,2048]{1,0:T(8,128)(2,1)S(1)}, bf16[8,2048]{1,0:T(8,128)(2,1)S(1)}, u32[]{:S(2)}, u32[]{:S(2)}) %collective-permute-start.16) | collective-permute-done | bytes 32800 | tf_op jit(solution)/shard_map/ppermute | solution.py:253
  47.0 0.6 %finish.1 = bf16[8,2048]{1,0:T(8,128)(2,1)} custom-call(f32[8,2048]{1,0:T(8,128)S(1)} %get-tuple-element.47.refs_0_, f32[8,2048]{1,0:T(8,128)S(1)} %get-tuple-element.55.refs_1_, bf16[8,2048]{1,0:T(8,128)(2,1)S(1)} %collective-permute-done.16.refs_2_), custom_call_target="tpu_custom_call" | custom-call | tf_op jit(solution)/shard_map/finish/pallas_call | solution.py:367
  (20 shorter events, 0.1 us)
Async XLA Ops:
  0.0 8.4 %copy-start.1 = (bf16[1,2048,768]{2,1,0:T(8,128)(2,1)S(1)}, bf16[1,2048,768]{2,1,0:T(8,128)(2,1)}, u32[]{:S(2)}) copy-start(bf16[1,2048,768]{2,1,0:T(8,128)(2,1)} %param.26) | copy-start | bytes 9437188
  0.0 12.3 %copy-start.4 = (bf16[512,2048]{1,0:T(8,128)(2,1)S(1)}, bf16[512,2048]{1,0:T(8,128)(2,1)}, u32[]{:S(2)}) copy-start(bf16[512,2048]{1,0:T(8,128)(2,1)} %refs_4_.1) | copy-start | bytes 6291460
  0.0 12.3 %collective-permute-start.3 = (bf16[1,2048,768]{2,1,0:T(8,128)(2,1)}, bf16[1,2048,768]{2,1,0:T(8,128)(2,1)S(1)}, u32[]{:S(2)}, u32[]{:S(2)}) collective-permute-start(bf16[1,2048,768]{2,1,0:T(8,128)(2,1)} %param.25), channel_id=1, source_target_pairs={{0,4},{4,0},{8,12},{12,8},{1,5},{5,1},{9,13},{13,9},{2,6},{6,2},{1... | collective-permute-start | bytes 9437192 | tf_op jit(solution)/shard_map/ppermute | solution.py:245
  3.2 6.3 %collective-permute-start = (bf16[8,512]{1,0:T(8,128)(2,1)S(1)}, bf16[8,512]{1,0:T(8,128)(2,1)S(1)}, u32[]{:S(2)}, u32[]{:S(2)}) collective-permute-start(bf16[8,512]{1,0:T(8,128)(2,1)S(1)} %get-tuple-element.33), channel_id=1, source_target_pairs={{0,3},{1,2},{2,1},{3,0},{4,7},{5,6},{6,5},{7,4},{8,11},{9,10},{10,... | collective-permute-start | bytes 24584 | tf_op jit(solution)/shard_map/ppermute | solution.py:253
  7.8 4.5 %collective-permute-start.1 = (bf16[8,512]{1,0:T(8,128)(2,1)S(1)}, bf16[8,512]{1,0:T(8,128)(2,1)S(1)}, u32[]{:S(2)}, u32[]{:S(2)}) collective-permute-start(bf16[8,512]{1,0:T(8,128)(2,1)S(1)} %get-tuple-element.34), channel_id=1, source_target_pairs={{0,2},{1,3},{2,0},{3,1},{4,6},{5,7},{6,4},{7,5},{8,10},{9,11},{10,... | collective-permute-start | bytes 24584 | tf_op jit(solution)/shard_map/ppermute | solution.py:253
  7.8 4.5 %collective-permute-start.2 = (bf16[8,512]{1,0:T(8,128)(2,1)S(1)}, bf16[8,512]{1,0:T(8,128)(2,1)S(1)}, u32[]{:S(2)}, u32[]{:S(2)}) collective-permute-start(bf16[8,512]{1,0:T(8,128)(2,1)S(1)} %get-tuple-element.35), channel_id=1, source_target_pairs={{0,1},{1,0},{2,3},{3,2},{4,5},{5,4},{6,7},{7,6},{8,9},{9,8},{10,11... | collective-permute-start | bytes 24584 | tf_op jit(solution)/shard_map/ppermute | solution.py:253
  8.4 19.9 %collective-permute-start.11 = (bf16[1,2048,768]{2,1,0:T(8,128)(2,1)S(1)}, bf16[1,2048,768]{2,1,0:T(8,128)(2,1)S(1)}, u32[]{:S(2)}, u32[]{:S(2)}) collective-permute-start(bf16[1,2048,768]{2,1,0:T(8,128)(2,1)S(1)} %copy-done.1), channel_id=1, source_target_pairs={{0,4},{4,0},{8,12},{12,8},{1,5},{5,1},{9,13},{13,9},{2,6},{6,2},{1... | collective-permute-start | bytes 9437192 | tf_op jit(solution)/shard_map/ppermute | solution.py:245
  12.3 20.5 %collective-permute-start.12 = (bf16[1,768,2048]{2,1,0:T(8,128)(2,1)}, bf16[1,768,2048]{2,1,0:T(8,128)(2,1)S(1)}, u32[]{:S(2)}, u32[]{:S(2)}) collective-permute-start(bf16[1,768,2048]{2,1,0:T(8,128)(2,1)} %param.27), channel_id=1, source_target_pairs={{0,4},{4,0},{8,12},{12,8},{1,5},{5,1},{9,13},{13,9},{2,6},{6,2},{1... | collective-permute-start | bytes 9437192 | tf_op jit(solution)/shard_map/ppermute | solution.py:314
  12.3 20.5 %copy-start.3 = (bf16[1,768,2048]{2,1,0:T(8,128)(2,1)S(1)}, bf16[1,768,2048]{2,1,0:T(8,128)(2,1)}, u32[]{:S(2)}) copy-start(bf16[1,768,2048]{2,1,0:T(8,128)(2,1)} %param.27) | copy-start | bytes 9437188
  12.8 5.8 %collective-permute-start.4 = (bf16[8,2048]{1,0:T(8,128)(2,1)S(1)}, bf16[8,2048]{1,0:T(8,128)(2,1)S(1)}, u32[]{:S(2)}, u32[]{:S(2)}) collective-permute-start(bf16[8,2048]{1,0:T(8,128)(2,1)S(1)} %get-tuple-element.41), channel_id=1, source_target_pairs={{0,3},{1,2},{2,1},{3,0},{4,7},{5,6},{6,5},{7,4},{8,11},{9,10},{10,... | collective-permute-start | bytes 98312 | tf_op jit(solution)/shard_map/ppermute | solution.py:253
  14.3 5.3 %collective-permute-start.5 = (bf16[8,2048]{1,0:T(8,128)(2,1)S(1)}, bf16[8,2048]{1,0:T(8,128)(2,1)S(1)}, u32[]{:S(2)}, u32[]{:S(2)}) collective-permute-start(bf16[8,2048]{1,0:T(8,128)(2,1)S(1)} %get-tuple-element.42), channel_id=1, source_target_pairs={{0,2},{1,3},{2,0},{3,1},{4,6},{5,7},{6,4},{7,5},{8,10},{9,11},{10,... | collective-permute-start | bytes 98312 | tf_op jit(solution)/shard_map/ppermute | solution.py:253
  14.9 4.9 %collective-permute-start.6 = (bf16[8,2048]{1,0:T(8,128)(2,1)S(1)}, bf16[8,2048]{1,0:T(8,128)(2,1)S(1)}, u32[]{:S(2)}, u32[]{:S(2)}) collective-permute-start(bf16[8,2048]{1,0:T(8,128)(2,1)S(1)} %get-tuple-element.43), channel_id=1, source_target_pairs={{0,1},{1,0},{2,3},{3,2},{4,5},{5,4},{6,7},{7,6},{8,9},{9,8},{10,11... | collective-permute-start | bytes 98312 | tf_op jit(solution)/shard_map/ppermute | solution.py:253
  19.8 13.0 %copy-start = (bf16[1,2048,768]{2,1,0:T(8,128)(2,1)S(1)}, bf16[1,2048,768]{2,1,0:T(8,128)(2,1)}, u32[]{:S(2)}) copy-start(bf16[1,2048,768]{2,1,0:T(8,128)(2,1)} %param.25) | copy-start | bytes 9437188
  19.8 13.0 %copy-start.2 = (bf16[1,2048,768]{2,1,0:T(8,128)(2,1)S(1)}, bf16[1,2048,768]{2,1,0:T(8,128)(2,1)}, u32[]{:S(2)}) copy-start(bf16[1,2048,768]{2,1,0:T(8,128)(2,1)} %param.26) | copy-start | bytes 9437188
  19.9 4.0 %collective-permute-start.7 = (bf16[8,2176]{1,0:T(8,128)(2,1)S(1)}, bf16[8,2176]{1,0:T(8,128)(2,1)S(1)}, u32[]{:S(2)}, u32[]{:S(2)}) collective-permute-start(bf16[8,2176]{1,0:T(8,128)(2,1)S(1)} %get-tuple-element.48.refs_0_), channel_id=1, source_target_pairs={{0,8},{4,12},{8,0},{12,4},{1,9},{5,13},{9,1},{13,5},{2,10},{6,14},... | collective-permute-start | bytes 104456 | tf_op jit(solution)/shard_map/ppermute | solution.py:253
  23.9 4.4 %collective-permute-start.10 = (bf16[16,2176]{1,0:T(8,128)(2,1)S(1)}, bf16[16,2176]{1,0:T(8,128)(2,1)S(1)}, u32[]{:S(2)}, u32[]{:S(2)}) collective-permute-start(bf16[16,2176]{1,0:T(8,128)(2,1)S(1)} %join.1.refs_0_), channel_id=1, source_target_pairs={{0,1},{1,0},{2,3},{3,2},{4,5},{5,4},{6,7},{7,6},{8,9},{9,8},{10,11... | collective-permute-start | bytes 208904 | tf_op jit(solution)/shard_map/ppermute | solution.py:260
  25.3 6.0 %collective-permute-start.9 = (bf16[16,2176]{1,0:T(8,128)(2,1)S(1)}, bf16[16,2176]{1,0:T(8,128)(2,1)S(1)}, u32[]{:S(2)}, u32[]{:S(2)}) collective-permute-start(bf16[16,2176]{1,0:T(8,128)(2,1)S(1)} %join.1.refs_0_), channel_id=1, source_target_pairs={{0,2},{1,3},{2,0},{3,1},{4,6},{5,7},{6,4},{7,5},{8,10},{9,11},{10,... | collective-permute-start | bytes 208904 | tf_op jit(solution)/shard_map/ppermute | solution.py:260
  26.7 6.1 %collective-permute-start.8 = (bf16[16,2176]{1,0:T(8,128)(2,1)S(1)}, bf16[16,2176]{1,0:T(8,128)(2,1)S(1)}, u32[]{:S(2)}, u32[]{:S(2)}) collective-permute-start(bf16[16,2176]{1,0:T(8,128)(2,1)S(1)} %join.1.refs_0_), channel_id=1, source_target_pairs={{0,3},{1,2},{2,1},{3,0},{4,7},{5,6},{6,5},{7,4},{8,11},{9,10},{10,... | collective-permute-start | bytes 208904 | tf_op jit(solution)/shard_map/ppermute | solution.py:260
  35.5 6.1 %collective-permute-start.13 = (bf16[16,2048]{1,0:T(8,128)(2,1)S(1)}, bf16[16,2048]{1,0:T(8,128)(2,1)S(1)}, u32[]{:S(2)}, u32[]{:S(2)}) collective-permute-start(bf16[16,2048]{1,0:T(8,128)(2,1)S(1)} %get-tuple-element.52), channel_id=1, source_target_pairs={{0,3},{1,2},{2,1},{3,0},{4,7},{5,6},{6,5},{7,4},{8,11},{9,10},{10,... | collective-permute-start | bytes 196616 | tf_op jit(solution)/shard_map/ppermute | solution.py:253
  37.3 5.7 %collective-permute-start.14 = (bf16[16,2048]{1,0:T(8,128)(2,1)S(1)}, bf16[16,2048]{1,0:T(8,128)(2,1)S(1)}, u32[]{:S(2)}, u32[]{:S(2)}) collective-permute-start(bf16[16,2048]{1,0:T(8,128)(2,1)S(1)} %get-tuple-element.53), channel_id=1, source_target_pairs={{0,2},{1,3},{2,0},{3,1},{4,6},{5,7},{6,4},{7,5},{8,10},{9,11},{10,... | collective-permute-start | bytes 196616 | tf_op jit(solution)/shard_map/ppermute | solution.py:253
  37.3 5.7 %collective-permute-start.15 = (bf16[16,2048]{1,0:T(8,128)(2,1)S(1)}, bf16[16,2048]{1,0:T(8,128)(2,1)S(1)}, u32[]{:S(2)}, u32[]{:S(2)}) collective-permute-start(bf16[16,2048]{1,0:T(8,128)(2,1)S(1)} %get-tuple-element.54), channel_id=1, source_target_pairs={{0,1},{1,0},{2,3},{3,2},{4,5},{5,4},{6,7},{7,6},{8,9},{9,8},{10,11... | collective-permute-start | bytes 196616 | tf_op jit(solution)/shard_map/ppermute | solution.py:253
  43.0 4.0 %collective-permute-start.16 = (bf16[8,2048]{1,0:T(8,128)(2,1)S(1)}, bf16[8,2048]{1,0:T(8,128)(2,1)S(1)}, u32[]{:S(2)}, u32[]{:S(2)}) collective-permute-start(bf16[8,2048]{1,0:T(8,128)(2,1)S(1)} %get-tuple-element.56), channel_id=1, source_target_pairs={{0,8},{4,12},{8,0},{12,4},{1,9},{5,13},{9,1},{13,5},{2,10},{6,14},... | collective-permute-start | bytes 98312 | tf_op jit(solution)/shard_map/ppermute | solution.py:253
